TPU v7x, 32 devices: a whole 2x2x4 slice. The times are simulated.
32 devices in a mesh: groups: 2 (over y), wide: 4 (over x, core), rows: 4 (over z).
Axes of the slice: x: 2, y: 2, z: 4, core: 2. Of those that a mesh axis runs over, the one named last changes fastest.
Arguments:
- features: bfloat16 [256, 24576], P('wide', ('groups', 'rows')), parts along dimension 1, may hold values from -6 to 6
- tile_weights: bfloat16 [1920, 128, 128], P(('groups', 'rows')), parts along dimension 0, may hold values from -0.25 to 0.25
- tile_source: int32 [1920], P(('groups', 'rows')), parts along dimension 0, may hold values from 0 to 23
- tile_dest: int32 [1920], P(('groups', 'rows')), parts along dimension 0, may hold values from 0 to 95, as said below
- tile_count: int32 [8], P(('groups', 'rows')), parts along dimension 0, may hold values from 1 to 240, as said below
- weight: bfloat16 [256, 256], replicated, may hold values from -0.375 to 0.375
- bias: bfloat16 [256], replicated, may hold values from -3 to 3
- cotangent: bfloat16 [24576, 256], P(('groups', 'rows', 'wide')), parts along dimension 0, may hold values from -6 to 6
Outputs:
- activation: bfloat16 [24576, 256], P(('groups', 'rows', 'wide')), parts along dimension 0
- grad_features: bfloat16 [256, 24576], P('wide', ('groups', 'rows')), parts along dimension 1
- grad_weight: float32 [512, 256], P('groups'), parts along dimension 0
- grad_bias: float32 [512], P('groups'), parts along dimension 0
There are 2 independent parts, one for each index of `groups`. A program takes and returns all parts, laid end to end along the dimension named above; an argument that names none is the same for every part. Nothing has to cross between parts.
Inputs may be any that keep to these rules, and one draw needn't show every extreme that they name: `tile_dest`: destination row block of each tile; a block may receive tiles from slots of several indices of rows. `tile_count`: live tile slots of one index of rows; in every draw some index has all 240 slots live.
All inputs are finite; a program needn't handle non-finite values.
Results may differ from a plain program's by a relative error of at most 0.0062.
Values may be sent and summed in bfloat16 or wider, within the bound.
No kernel may reach another device: no remote copies, remote signals or barrier semaphores. Data moves between devices by JAX's collectives and lax.ppermute only.
A program may use at most 128 MiB of HBM per device.

v0:
```python
import jax
import jax.numpy as jnp
from jax import lax
from jax.sharding import PartitionSpec as P

BLK = 128


def smooth_gate(value):
    return jax.nn.gelu(value, approximate=True)


def regroup(owned):
    return lax.all_to_all(owned, "wide", split_axis=0, concat_axis=1, tiled=True)


def per_device(features, tile_weights, tile_source, tile_dest, tile_count, weight, bias, cotangent):
    columns = features.shape[0]
    per_dev = features.shape[1] // BLK
    tile_total = tile_weights.shape[0]
    own_blocks = jnp.transpose(features.reshape(columns, per_dev, BLK), (1, 0, 2))
    live_count = tile_count[0]
    trips = (live_count + per_dev - 1) // per_dev
    offsets = jnp.arange(per_dev, dtype=jnp.int32)

    def block_of(turn):
        first = turn * per_dev
        weights_now = lax.dynamic_slice_in_dim(tile_weights, first, per_dev, 0)
        sources = lax.dynamic_slice_in_dim(tile_source, first, per_dev, 0)
        targets = lax.dynamic_slice_in_dim(tile_dest, first, per_dev, 0)
        active = first + offsets < live_count
        return (weights_now, sources, targets, active)

    def tile_products(turn):
        weights_now, sources, targets, active = block_of(turn)
        picked = jnp.take(own_blocks, sources, axis=0)
        product = jnp.einsum(
            "tcj,tij->tci", picked, weights_now, preferred_element_type=jnp.float32
        )
        return (jnp.where(active[:, None, None], product, jnp.float32(0.0)), targets)

    def store_turn(turn, stored):
        product, targets = tile_products(turn)
        return lax.dynamic_update_slice_in_dim(stored, product, turn * per_dev, 0)

    stored = lax.fori_loop(0, trips, store_turn, jnp.zeros((tile_total, columns, BLK), jnp.float32))
    local = tile_dest
    inside = (local >= 0) & (local < lax.axis_size("rows") * per_dev)
    local = jnp.where(inside, local, lax.axis_size("rows") * per_dev)
    owned = lax.psum_scatter(
        jnp.zeros((lax.axis_size("rows") * per_dev, columns, BLK), jnp.float32)
        .at[local]
        .add(stored, mode="drop"),
        "rows",
        scatter_dimension=0,
        tiled=True,
    ).astype(jnp.bfloat16)
    agg_rows = regroup(owned)
    row_blocks = agg_rows.shape[0]
    hidden = agg_rows.shape[1]
    pre = jnp.einsum("bfn,fo->bno", agg_rows, weight, preferred_element_type=jnp.float32)
    pre = pre.reshape(row_blocks * BLK, hidden) + bias.astype(jnp.float32)
    activated, pullback = jax.vjp(smooth_gate, pre)
    activation = activated.astype(jnp.bfloat16)
    delta = pullback(cotangent.astype(jnp.float32))[0].astype(jnp.bfloat16)
    delta_blocks = delta.reshape(row_blocks, BLK, hidden)
    local_weight = jnp.einsum(
        "bfn,bno->fo", agg_rows, delta_blocks, preferred_element_type=jnp.float32
    )
    local_bias = jnp.sum(delta.astype(jnp.float32), axis=0)
    grad_weight, grad_bias = lax.psum((local_weight, local_bias), ("wide", "rows"))
    propagated = jnp.einsum(
        "bno,fo->bfn", delta_blocks, weight, preferred_element_type=jnp.float32
    ).astype(jnp.bfloat16)
    column_view = lax.all_to_all(propagated, "wide", split_axis=1, concat_axis=0, tiled=True)
    every_block = lax.all_gather(column_view, "rows", axis=0, tiled=True)

    def backward_turn(turn, total):
        weights_now, sources, targets, active = block_of(turn)
        picked = jnp.take(every_block, targets, axis=0)
        product = jnp.einsum(
            "tci,tij->tcj", picked, weights_now, preferred_element_type=jnp.float32
        )
        product = jnp.where(active[:, None, None], product, jnp.float32(0.0))
        return total.at[sources].add(product)

    collected = lax.fori_loop(
        0, trips, backward_turn, jnp.zeros((per_dev, columns, BLK), jnp.float32)
    )
    grad_features = (
        jnp.transpose(collected, (1, 0, 2)).reshape(columns, per_dev * BLK).astype(jnp.bfloat16)
    )
    return (activation, grad_features, grad_weight, grad_bias)


def solution(mesh):
    in_specs = (
        P("wide", ("groups", "rows")),
        P(("groups", "rows"), None, None),
        P(("groups", "rows")),
        P(("groups", "rows")),
        P(("groups", "rows")),
        P(),
        P(),
        P(("groups", "rows", "wide"), None),
    )
    out_specs = (
        P(("groups", "rows", "wide"), None),
        P("wide", ("groups", "rows")),
        P("groups", None),
        P("groups"),
    )
    return jax.shard_map(
        per_device, mesh=mesh, in_specs=in_specs, out_specs=out_specs, check_vma=False
    )
```

profile of v0, /device:TPU:0, one launch (start us, length us, event | category | flops | bytes accessed | tf_op | source)
XLA Modules:
  0.0 307.5 jit_solution(9593090737811565037)
XLA Ops:
  7.2 0.0 copy-start
  7.2 0.0 copy-start.3
  7.2 0.0 reduce-scatter.2.cloned.1.call-start
  7.9 1.1 copy.34
  9.0 0.1 copy.25
  9.1 4.1 %broadcast_in_dim.66 = f32[240,64,128]{2,1,0:T(8,128)} broadcast(f32[]{:T(128)} %constant.47.clone.1), dimensions={} | broadcast | bytes 7864324 | tf_op jit(solution)/shard_map/broadcast_in_dim | solution.py:46
  13.2 0.0 copy-done.3
  13.2 0.0 copy-start.2
  13.2 4.1 %while.22 = (s32[]{:T(128)}, f32[240,64,128]{2,1,0:T(8,128)}, s32[]{:T(128)}, s32[]{:T(128)}, s32[240]{0:T(256)S(1)}, /*index=5*/bf16[24,64,128]{2,1,0:T(8,128)(...) while((s32[]{:T(128)}, f32[240,64,128]{2,1,0:T(8,128)}, ...), condition=%wide.region_1.2_spmd.clone, body=%wide.region_0.1_spmd.clone.sunk | while | flops 50726084 | bytes 2758279 | solution.py:46
  13.2 0.7 compare_and_fusion.4
  13.9 0.6 gather_fusion
  14.5 2.7 fusion.44
  17.2 0.0 copy-done.2
  17.3 0.4 broadcast_in_dim.64
  17.6 0.0 copy-start.4
  17.7 24.8 %scatter_fusion.1 = f32[96,64,128]{2,1,0:T(8,128)S(1)} fusion(f32[96,64,128]{2,1,0:T(8,128)S(1)} %broadcast_in_dim.64, s32[240]{0:T(256)S(1)} %compare_select_fusion.3, f32[240,64,128]{2,1,0:T(8,128)} %get-tuple-element.95), kind=kCustom, calls=%fused_computation.3 | custom fusion | flops 1966080 | bytes 23593920 | tf_op jit(solution)/shard_map/scatter-add | solution.py:53
  42.5 0.0 copy-start.1
  42.5 1.6 copy-done.1
  44.1 0.0 reduce-scatter.2.cloned.1.call-update
  44.1 97.7 %reduce-scatter.2.cloned.1.call-done = f32[24,64,128]{2,1,0:T(8,128)} async-done(((f32[96,64,128]{2,1,0:T(8,128)}), f32[24,64,128]{2,1,0:T(8,128)}) %reduce-scatter.2.cloned.1.call-update) | async-done | bytes 786448 | tf_op jit(solution)/shard_map/reduce_scatter | solution.py:50
  141.8 1.9 convert_element_type.33
  143.8 3.5 %all-to-all-start = ((bf16[24,64,128]{2,1,0:T(8,128)(2,1)}), bf16[24,64,128]{2,1,0:T(8,128)(2,1)S(1)}, u32[]{:S(2)}, u32[]{:S(2)}) async-start(bf16[24,64,128]{2,1,0:T(8,128)(2,1)} %convert_element_type.33), calls=%async_computation.1 | async-start | bytes 786432 | tf_op jit(solution)/shard_map/all_to_all | solution.py:14
  147.2 0.0 all-gather.2.cloned.1.call-start
  147.3 0.0 copy-done.4
  147.3 7.3 %all-to-all-done = bf16[24,64,128]{2,1,0:T(8,128)(2,1)S(1)} async-done(((bf16[24,64,128]{2,1,0:T(8,128)(2,1)}), bf16[24,64,128]{2,1,0:T(8,128)(2,1)S(1)}, u32[]{:S(2)}, u32[]{:S(2)}) %all-to-all-start) | async-done | bytes 393248 | tf_op jit(solution)/shard_map/all_to_all | solution.py:14
  154.7 0.2 copy.27
  154.9 0.0 copy-done
  154.9 2.6 convert_reduce_fusion
  157.5 0.3 fusion.19
  157.8 0.3 copy.28
  158.1 11.2 %all_to_all.36 = bf16[6,256,128]{2,0,1:T(8,128)(2,1)S(1)} all-to-all(bf16[6,256,128]{2,0,1:T(8,128)(2,1)S(1)} %copy.28), channel_id=1, replica_groups=mesh['groups'=2,'wide'=4,'rows'=4] {'wide'}, dimensions={1} | all-to-all | bytes 786432 | tf_op jit(solution)/shard_map/all_to_all | solution.py:75
  169.3 0.8 copy.30
  170.2 0.0 all-gather.2.cloned.1.call-update
  170.2 0.0 all-reduce.2.cloned.1.call-start
  170.2 32.7 %psum.15 = f32[256]{0:T(256)} all-reduce(f32[256]{0:T(256)S(1)} %get-tuple-element.188), channel_id=1, replica_groups=mesh['groups'=2,'wide'=4,'rows'=4] {'wide','rows'}, use_global_device_ids=true, to_apply=%region_9.10 | all-reduce | flops 256 | bytes 2048 | tf_op jit(solution)/shard_map/psum | solution.py:71
  202.9 1.0 convolution_bitcast_fusion
  203.9 0.0 all-reduce.2.cloned.1.call-update
  203.9 3.6 %all-gather.2.cloned.1.call-done = bf16[96,64,128]{2,1,0:T(8,128)(2,1)} async-done(((bf16[24,64,128]{2,1,0:T(8,128)(2,1)}), bf16[96,64,128]{2,1,0:T(8,128)(2,1)}) %all-gather.2.cloned.1.call-update) | async-done | bytes 1572880 | tf_op jit(solution)/shard_map/all_gather | solution.py:76
  207.5 0.1 broadcast_in_dim.67
  207.6 6.5 %while.23 = (s32[]{:T(128)}, f32[24,64,128]{2,1,0:T(8,128)S(1)}, s32[]{:T(128)}, s32[240]{0:T(256)S(1)}, s32[]{:T(128)}, /*index=5*/s32[240]{0:T(256)S(1)}, bf16...) while((s32[]{:T(128)}, f32[24,64,128]{2,1,0:T(8,128)S(1)}, ...), condition=%wide.region_6.7_spmd.clone, body=%wide.region_4.6_spmd.clone.sunk | while | flops 50922764 | bytes 5116855 | solution.py:87
  207.6 0.7 compare_and_fusion.5
  208.4 2.0 gather_fusion.1
  210.4 1.5 convolution_select_fusion.3
  211.9 0.1 compare_select_fusion.7
  212.0 2.1 scatter_fusion
  214.1 0.8 copy_bitcast_fusion
  214.9 84.3 %all-reduce.2.cloned.1.call-done = f32[256,256]{1,0:T(8,128)} async-done(((f32[256,256]{1,0:T(8,128)}), f32[256,256]{1,0:T(8,128)}) %all-reduce.2.cloned.1.call-update) | async-done | bytes 262160 | tf_op jit(solution)/shard_map/psum | solution.py:71
  299.3 1.7 copy.53
  (5 shorter events, 0.0 us)
Async XLA Ops:
  7.2 147.7 %copy-start = (bf16[256,256]{1,0:T(8,128)(2,1)S(1)}, bf16[256,256]{1,0:T(8,128)(2,1)}, u32[]{:S(2)}) copy-start(bf16[256,256]{1,0:T(8,128)(2,1)} %param.17) | copy-start | bytes 393220
  7.2 6.0 %copy-start.3 = (s32[240]{0:T(256)S(1)}, s32[240]{0:T(256)}, u32[]{:S(2)}) copy-start(s32[240]{0:T(256)} %param.14) | copy-start | bytes 2884
  7.2 134.6 %reduce-scatter.2.cloned.1.call-start = ((), (), s32[]{:S(2)}) async-start(), calls=%async_computation.3 | async-start | bytes 3932160 | tf_op jit(solution)/shard_map/reduce_scatter | solution.py:50
  13.2 4.1 %copy-start.2 = (s32[240]{0:T(256)S(1)}, s32[240]{0:T(256)}, u32[]{:S(2)}) copy-start(s32[240]{0:T(256)} %param.15) | copy-start | bytes 2884
  17.6 129.7 %copy-start.4 = (bf16[256]{0:T(256)(128)(2,1)S(1)}, bf16[256]{0:T(256)(128)(2,1)}, u32[]{:S(2)}) copy-start(bf16[256]{0:T(256)(128)(2,1)} %param.18) | copy-start | bytes 1540
  42.5 1.6 copy-start.1
  143.8 10.9 %all-to-all-start = ((bf16[24,64,128]{2,1,0:T(8,128)(2,1)}), bf16[24,64,128]{2,1,0:T(8,128)(2,1)S(1)}, u32[]{:S(2)}, u32[]{:S(2)}) async-start(bf16[24,64,128]{2,1,0:T(8,128)(2,1)} %convert_element_type.33), calls=%async_computation.1 | async-start | bytes 786432 | tf_op jit(solution)/shard_map/all_to_all | solution.py:14
  147.2 60.3 %all-gather.2.cloned.1.call-start = ((), (), s32[]{:S(2)}) async-start(), calls=%async_computation.4 | async-start | bytes 1966080 | tf_op jit(solution)/shard_map/all_gather | solution.py:76
  170.2 129.1 %all-reduce.2.cloned.1.call-start = ((), (), s32[]{:S(2)}) async-start(), calls=%async_computation.5 | async-start | bytes 524288 | tf_op jit(solution)/shard_map/psum | solution.py:71
Sparse Core Ops, SparseCore 0:
  44.2 97.5 reduce-scatter.1
  170.3 37.1 all-gather.1
  211.5 87.7 all-reduce.1
where the time goes:
time: 310 us; the launch traced here: 307 us
  waiting for transfers between devices  193 us (62%)
  blocking collectives  43.9 us (14%)
  other arithmetic  31.2 us (10%)
  between operations  14.6 us (5%)
  local copies, waits for them, and re-layouts  13 us (4%)
  matrix products  8.06 us (3%)
  starting transfers between devices  3.58 us (1%)
    reduce_scatter x1, waiting for transfers between devices, per_device(): lax.psum_scatter(jnp.zeros((lax.axis_size('rows') * per_dev, columns, BLK...  97.7 us
    psum x1, waiting for transfers between devices, per_device(): lax.psum((local_weight, local_bias), ('wide', 'rows'))  84.3 us
    psum x1, blocking collectives, per_device(): lax.psum((local_weight, local_bias), ('wide', 'rows'))  32.7 us
    scatter-add x1, other arithmetic, per_device(): owned = lax.psum_scatter(jnp.zeros((lax.axis_size('rows') * per_dev, colu...  24.8 us
    all_to_all x1, blocking collectives, per_device(): lax.all_to_all(propagated, 'wide', split_axis=1, concat_axis=0, tiled=True)  11.2 us
    all_to_all x1, waiting for transfers between devices, regroup(): lax.all_to_all(owned, 'wide', split_axis=0, concat_axis=1, tiled=True)  7.34 us
  transfers between devices with their start and end apart: 4, of which 4 were waited for; matrix products, arithmetic and copies ran while one was open for 3% of the time, Pallas kernels for 0%

commit v1 on v0

v1 whole, which is shorter than its diff:
```python
import functools
import math

import jax
import jax.numpy as jnp
from jax import lax
from jax.experimental import pallas as pl
from jax.experimental.pallas import tpu as pltpu
from jax.sharding import PartitionSpec as P

BLK = 128
GROUP = 8
RING = 8
VMEM_BYTES = 48 * 1024 * 1024
ROOT = math.sqrt(2.0 / math.pi)
CUBIC = 0.044715
BF16 = jnp.bfloat16
F32 = jnp.float32

SMEM_SPEC = pl.BlockSpec(memory_space=pltpu.SMEM)
VMEM_SPEC = pl.BlockSpec(memory_space=pltpu.VMEM)
ANY_SPEC = pl.BlockSpec(memory_space=pl.ANY)


def bits_of(size):
    return max(1, int(size).bit_length())


def call(body, name, out_shape, in_specs, scratch, flops, nbytes):
    return pl.pallas_call(
        body,
        name=name,
        out_shape=out_shape,
        in_specs=in_specs,
        out_specs=jax.tree.map(lambda _: VMEM_SPEC, out_shape),
        scratch_shapes=scratch,
        compiler_params=pltpu.CompilerParams(vmem_limit_bytes=VMEM_BYTES),
        cost_estimate=pl.CostEstimate(flops=flops, bytes_accessed=nbytes, transcendentals=0),
    )


def each_tile(meta, tiles, picked, ring, sems, tile_bits, dead, multiply, add):
    total = meta.shape[0]
    tile_mask = (1 << tile_bits) - 1

    def scan(step, found):
        for u in range(GROUP):
            entry = meta[step * GROUP + u]
            picked[found] = entry
            found = found + jnp.where(entry >= 0, 1, 0)
        return found

    found = lax.fori_loop(0, total // GROUP, scan, jnp.int32(0))
    for u in range(GROUP):
        picked[found + u] = jnp.int32(dead)
    groups = lax.div(found + (GROUP - 1), GROUP)

    def copies(group):
        base = lax.rem(group, RING) * GROUP
        for u in range(GROUP):
            tile = picked[group * GROUP + u] & tile_mask
            yield pltpu.make_async_copy(tiles.at[tile], ring.at[base + u], sems.at[base + u])

    def start(group, carry):
        for copy in copies(group):
            copy.start()
        return carry

    lax.fori_loop(0, jnp.minimum(groups, RING), start, 0)

    def work(group, carry):
        for copy in copies(group):
            copy.wait()
        base = lax.rem(group, RING) * GROUP
        entries = [picked[group * GROUP + u] >> tile_bits for u in range(GROUP)]
        products = [multiply(entries[u], ring.at[base + u]) for u in range(GROUP)]
        for u in range(GROUP):
            add(entries[u], products[u])

        @pl.when(group + RING < groups)
        def _():
            start(group + RING, 0)

        return carry

    lax.fori_loop(0, groups, work, 0)


def ring_scratch(slots):
    return [
        pltpu.SMEM((slots + GROUP + 1,), jnp.int32),
        pltpu.VMEM((RING * GROUP, BLK, BLK), BF16),
        pltpu.SemaphoreType.DMA((RING * GROUP,)),
    ]


def aggregate(meta, place, tiles, parts, sources, dests, chunk, tile_bits, source_bits, kinds):
    slots = meta.shape[0]
    columns = sum(part.shape[0] for part in parts)
    dead = (dests << source_bits) << tile_bits

    def body(meta_ref, place_ref, tiles_ref, *refs):
        part_refs = refs[: len(parts)]
        outs = refs[len(parts) : len(parts) + len(kinds)]
        turned, total, picked, ring, sems = refs[len(parts) + len(kinds) :]
        for s in range(sources):
            block = jnp.concatenate([ref[:, s * BLK : (s + 1) * BLK] for ref in part_refs], axis=0)
            turned[s] = jnp.transpose(block)
        total[...] = jnp.zeros_like(total)

        def multiply(entry, tile):
            source = entry & ((1 << source_bits) - 1)
            return jnp.dot(tile[...], turned[source], preferred_element_type=F32)

        def add(entry, product):
            total[entry >> source_bits] += product

        each_tile(meta_ref, tiles_ref, picked, ring, sems, tile_bits, dead, multiply, add)
        for i, out in enumerate(outs):
            rows = out.shape[0] // BLK
            out[...] = total[pl.ds(place_ref[i] * chunk, rows)].reshape(out.shape).astype(out.dtype)

    return call(
        body,
        "aggregate",
        [jax.ShapeDtypeStruct((blocks * BLK, columns), kind) for blocks, kind in kinds],
        [SMEM_SPEC, SMEM_SPEC, ANY_SPEC] + [VMEM_SPEC] * len(parts),
        [pltpu.VMEM((sources, BLK, columns), BF16), pltpu.VMEM((dests + 1, BLK, columns), F32)]
        + ring_scratch(slots),
        slots * BLK * BLK * columns,
        slots * BLK * BLK,
    )(meta, place, tiles, *parts)


def spread_back(meta, place, tiles, parts, sources, dests, chunk, tile_bits, source_bits, cols):
    slots = meta.shape[0]
    columns = parts[0].shape[0]
    chips = columns // (2 * cols)
    dead = (dests << source_bits) << tile_bits

    def body(meta_ref, place_ref, tiles_ref, *refs):
        part_refs = refs[: len(parts)]
        keep, send = refs[len(parts) : len(parts) + 2]
        held, total, picked, ring, sems = refs[len(parts) + 2 :]
        held[dests] = jnp.zeros_like(held[dests])
        for i, ref in enumerate(part_refs):
            for q in range(ref.shape[1] // BLK):
                held[place_ref[i] * chunk + q] = ref[:, q * BLK : (q + 1) * BLK]
        total[...] = jnp.zeros_like(total)

        def multiply(entry, tile):
            return jnp.dot(held[entry >> source_bits], tile[...], preferred_element_type=F32)

        def add(entry, product):
            source = entry & ((1 << source_bits) - 1)
            total[source] += product

        each_tile(meta_ref, tiles_ref, picked, ring, sems, tile_bits, dead, multiply, add)
        for s in range(sources):
            for chip in range(chips):
                low = 2 * chip * cols
                spot = (slice(chip * cols, (chip + 1) * cols), slice(s * BLK, (s + 1) * BLK))
                keep[spot] = total[s, low : low + cols, :]
                send[spot] = total[s, low + cols : low + 2 * cols, :].astype(BF16)

    return call(
        body,
        "spread_back",
        [
            jax.ShapeDtypeStruct((chips * cols, sources * BLK), F32),
            jax.ShapeDtypeStruct((chips * cols, sources * BLK), BF16),
        ],
        [SMEM_SPEC, SMEM_SPEC, ANY_SPEC] + [VMEM_SPEC] * len(parts),
        [
            pltpu.VMEM((dests + 2 * chunk, columns, BLK), BF16),
            pltpu.VMEM((sources, columns, BLK), F32),
        ]
        + ring_scratch(slots),
        slots * BLK * BLK * columns,
        slots * BLK * BLK,
    )(meta, place, tiles, *parts)


def layer(spot, near, far, weight, bias, cotangent, cols, chips):
    rows, hidden = cotangent.shape
    near_cols = near[0].shape[1]
    step = 2 * BLK if rows % (2 * BLK) == 0 else BLK
    count = 2 * chips
    lines = cols + 8

    def body(spot_ref, *refs):
        near_refs = refs[: len(near)]
        far_refs = refs[len(near) : len(near) + len(far)]
        weight_ref, bias_ref, cot_ref = refs[len(near) + len(far) : len(near) + len(far) + 3]
        act_ref, near_out, far_out, grad_ref = refs[len(near) + len(far) + 3 :]
        grad_w = [jnp.zeros((near_cols, hidden), F32), jnp.zeros((hidden - near_cols, hidden), F32)]
        grad_b = jnp.zeros((1, hidden), F32)
        for low in range(0, rows, step):
            now = slice(low, low + step)
            mixed = []
            for group in (near_refs, far_refs):
                value = group[0][now, :].astype(F32)
                for ref in group[1:]:
                    value = value + ref[now, :].astype(F32)
                mixed.append(value.astype(BF16))
            pre = jnp.dot(mixed[0], weight_ref[:near_cols, :], preferred_element_type=F32)
            pre = pre + jnp.dot(mixed[1], weight_ref[near_cols:, :], preferred_element_type=F32)
            pre = pre + bias_ref[...].astype(F32)
            square = pre * pre
            bend = jnp.tanh(ROOT * pre * (1.0 + CUBIC * square))
            half = 0.5 * (1.0 + bend)
            act_ref[now, :] = (pre * half).astype(BF16)
            slope = half + 0.5 * ROOT * pre * (1.0 - bend * bend) * (1.0 + 3.0 * CUBIC * square)
            delta = (cot_ref[now, :].astype(F32) * slope).astype(BF16)
            turned = lax.dot_general(
                weight_ref[...], delta, (((1,), (1,)), ((), ())), preferred_element_type=F32
            ).astype(BF16)
            near_out[:, now] = turned[:near_cols, :]
            far_out[:, now] = turned[near_cols:, :]
            for i in range(2):
                grad_w[i] = grad_w[i] + jnp.dot(
                    jnp.transpose(mixed[i]), delta, preferred_element_type=F32
                )
            grad_b = grad_b + jnp.sum(delta.astype(F32), axis=0, keepdims=True)
        tail = jnp.broadcast_to(grad_b, (8, hidden))
        for part in range(count):
            source = grad_w[0] if part < 2 else grad_w[1]
            low = part * cols - (0 if part < 2 else near_cols)
            grad_ref[part % 2, part // 2, :cols, :] = source[low : low + cols, :]
            grad_ref[part % 2, part // 2, cols:, :] = tail

    return call(
        body,
        "layer",
        [
            jax.ShapeDtypeStruct((rows, hidden), BF16),
            jax.ShapeDtypeStruct((near_cols, rows), BF16),
            jax.ShapeDtypeStruct((hidden - near_cols, rows), BF16),
            jax.ShapeDtypeStruct((2, chips, lines, hidden), F32),
        ],
        [SMEM_SPEC] + [VMEM_SPEC] * (len(near) + len(far) + 3),
        [],
        6 * rows * hidden * hidden,
        10 * rows * hidden,
    )(spot, *near, *far, weight, bias, cotangent)


def assemble(spot, mine, other, cols, chips):
    hidden = mine[0].shape[1]

    def body(spot_ref, *refs):
        out, bias_out = refs[-2:]
        chip, core = spot_ref[0], spot_ref[1]
        for k, group in enumerate((refs[:chips], refs[chips : 2 * chips])):
            for s in range(chips):
                owner = lax.rem(chip + s, chips) * 2 + (core if k == 0 else 1 - core)
                low = pl.multiple_of(owner * cols, cols)
                out[pl.ds(low, cols), :] = group[s][:cols, :]
        bias_out[...] = refs[0][cols : cols + 1, :]

    return call(
        body,
        "assemble",
        [
            jax.ShapeDtypeStruct((2 * chips * cols, hidden), F32),
            jax.ShapeDtypeStruct((1, hidden), F32),
        ],
        [SMEM_SPEC] + [VMEM_SPEC] * (2 * chips),
        [],
        0,
        8 * chips * cols * hidden,
    )(spot, *mine, *other)


def per_device(features, tile_weights, tile_source, tile_dest, tile_count, weight, bias, cotangent):
    cols, width = features.shape
    sources = width // BLK
    slots = tile_weights.shape[0]
    hidden = weight.shape[0]
    wide = lax.axis_size("wide")
    chips = wide // 2
    n_rows = lax.axis_size("rows")
    chunk = sources // wide
    dests = n_rows * chunk
    relay = n_rows == 4
    tile_bits, source_bits = bits_of(slots), bits_of(sources)

    at = lax.axis_index("wide")
    chip, core = at // 2, at % 2
    row = lax.axis_index("rows")

    def swap_cores(value):
        return lax.ppermute(value, "wide", [(i, i ^ 1) for i in range(wide)])

    def from_chip(value, shift):
        pairs = [(2 * ((i + shift) % chips) + k, 2 * i + k) for i in range(chips) for k in range(2)]
        return lax.ppermute(value, "wide", pairs)

    def along(value, pairs):
        return lax.ppermute(value, "rows", pairs)

    up, down = [(0, 1), (1, 2), (2, 3)], [(1, 0), (2, 1), (3, 2)]
    skip = [(0, 2), (1, 3), (2, 0), (3, 1)]

    slot = jnp.arange(slots, dtype=jnp.int32)
    within = tile_dest % sources
    mine = (slot < tile_count[0]) & (within // chunk == at)
    index = (tile_dest // sources) * chunk + within % chunk
    meta = jnp.where(mine, (index << (source_bits + tile_bits)) | (tile_source << tile_bits) | slot, -1)

    distant = [from_chip(features, s) for s in range(1, chips)]
    near_parts = [features, swap_cores(features)]

    if relay:
        last = n_rows - 1
        out_place = jnp.stack(
            [row, jnp.minimum(row + 1, last), jnp.maximum(row - 1, 0), row ^ 2, last - row]
        ).astype(jnp.int32)
        kinds = [(chunk, F32)] + [(chunk, BF16)] * 4
    else:
        out_place = jnp.zeros((1,), jnp.int32)
        kinds = [(dests, BF16)]

    def summed(parts):
        outs = aggregate(
            meta, out_place, tile_weights, parts, sources, dests, chunk, tile_bits, source_bits, kinds
        )
        if not relay:
            return [lax.psum_scatter(outs[0], "rows", scatter_dimension=0, tiled=True)]
        own, to_up, to_down, to_skip, ends = outs
        passed = along(ends, [(0, 1), (3, 2)])
        got_up = along(to_up, up)
        got_down = along(to_down, down)
        got_skip = along((to_skip.astype(F32) + passed.astype(F32)).astype(BF16), skip)
        return [own, got_up, got_down, got_skip]

    near = summed(near_parts)
    far_parts = []
    for value in distant:
        far_parts += [value, swap_cores(value)]
    far = summed(far_parts)

    order = (2 * ((chip + jnp.arange(chips)) % chips))[:, None] + (core ^ jnp.arange(2))[None, :]
    ordered = jnp.take(weight.reshape(wide, cols, hidden), order.reshape(-1), axis=0)
    spot = jnp.stack([chip, core]).astype(jnp.int32)
    activation, near_prop, far_prop, grads = layer(
        spot, near, far, ordered.reshape(hidden, hidden), bias.reshape(1, hidden), cotangent, cols, chips
    )

    if relay:
        in_place = jnp.stack(
            [
                row,
                jnp.where(row > 0, row - 1, n_rows),
                jnp.where(row < last, row + 1, n_rows),
                row ^ 2,
                jnp.where(row == 0, last, jnp.where(row == last, 0, n_rows)),
            ]
        ).astype(jnp.int32)
    else:
        in_place = jnp.zeros((1,), jnp.int32)

    def gathered(value):
        if not relay:
            return [lax.all_gather(value, "rows", axis=1, tiled=True)]
        got_skip = along(value, skip)
        got_up = along(value, up)
        got_down = along(value, down)
        got_ends = along(got_skip, [(2, 3), (1, 0)])
        return [value, got_up, got_down, got_skip, got_ends]

    def back(value):
        return spread_back(
            meta, in_place, tile_weights, gathered(value), sources, dests, chunk, tile_bits, source_bits, cols
        )

    far_keep, far_send = back(far_prop)
    far_sum = (far_keep + swap_cores(far_send).astype(F32)).astype(BF16)
    arrived = [
        from_chip(far_sum[(chips - s - 1) * cols : (chips - s) * cols], s) for s in range(1, chips)
    ]

    part = grads[0] + swap_cores(grads[1])
    quarter = part[0]
    for s in range(1, chips):
        quarter = quarter + from_chip(part[chips - s], s)
    if relay:
        quarter = quarter + along(quarter, [(0, 1), (1, 0), (2, 3), (3, 2)])
        quarter = quarter + along(quarter, skip)
    else:
        quarter = lax.psum(quarter, "rows")
    half = [quarter] + [from_chip(quarter, s) for s in range(1, chips)]
    whole_half = jnp.stack(half)
    other_half = swap_cores(whole_half)
    grad_weight, grad_bias = assemble(
        spot, half, [other_half[s] for s in range(chips)], cols, chips
    )

    near_keep, near_send = back(near_prop)
    total = near_keep + swap_cores(near_send).astype(F32)
    for value in arrived:
        total = total + value.astype(F32)
    grad_features = total.astype(BF16)
    return (activation, grad_features, grad_weight, grad_bias.reshape(hidden))


def solution(mesh):
    in_specs = (
        P("wide", ("groups", "rows")),
        P(("groups", "rows"), None, None),
        P(("groups", "rows")),
        P(("groups", "rows")),
        P(("groups", "rows")),
        P(),
        P(),
        P(("groups", "rows", "wide"), None),
    )
    out_specs = (
        P(("groups", "rows", "wide"), None),
        P("wide", ("groups", "rows")),
        P("groups", None),
        P("groups"),
    )
    return jax.shard_map(
        per_device, mesh=mesh, in_specs=in_specs, out_specs=out_specs, check_vma=False
    )
```

time: 310 us -> 135 us (0.44)
  waiting for transfers between devices: 193 us -> 56.7 us
  blocking collectives: 43.9 us -> 0 us
  starting transfers between devices: 3.58 us -> 47.4 us
  other arithmetic: 31.2 us -> 2.18 us
  Pallas kernels: 0 us -> 24 us
  between operations: 14.6 us -> 1.67 us
  local copies, waits for them, and re-layouts: 13 us -> 2.09 us
  matrix products: 8.06 us -> 0 us
    reduce_scatter x1 -> x0, waiting for transfers between devices: 97.7 us -> none  [per_device(): lax.psum_scatter(jnp.zeros((lax.axis_size('rows') * per_dev, columns, BLK...]
    psum x1 -> x0, waiting for transfers between devices: 84.3 us -> none  [per_device(): lax.psum((local_weight, local_bias), ('wide', 'rows'))]
    ppermute x0 -> x28, waiting for transfers between devices: none -> 56.7 us  [the longest x18 39.8 us: along(): return lax.ppermute(value, 'rows', pairs)]
    ppermute x0 -> x28, starting transfers between devices: none -> 47.4 us  [the longest x18 40.2 us: along(): return lax.ppermute(value, 'rows', pairs)]
    psum x1 -> x0, blocking collectives: 32.7 us -> none  [per_device(): lax.psum((local_weight, local_bias), ('wide', 'rows'))]
    scatter-add x2 -> x0, other arithmetic: 26.9 us -> none  [the longest x1 24.8 us: per_device(): owned = lax.psum_scatter(jnp.zeros((lax.axis_size('rows') * per_dev, colu...]
    pallas_call x0 -> x6, Pallas kernels: none -> 24 us  [the longest x2 10.1 us: aggregate(): call(body, 'aggregate', [jax.ShapeDtypeStruct((blocks * BLK, columns), ki...]
    all_to_all x1 -> x0, blocking collectives: 11.2 us -> none  [per_device(): lax.all_to_all(propagated, 'wide', split_axis=1, concat_axis=0, tiled=True)]
  transfers between devices with their start and end apart: 4 -> 28, of which waited for: 4 -> 8; matrix products, arithmetic and copies ran while one was open for 3% -> 2% of each run, Pallas kernels for 0% -> 16%
where the time goes in v1:
time: 135 us; the launch traced here: 134 us
  waiting for transfers between devices  56.7 us (42%)
  starting transfers between devices  47.4 us (35%)
  Pallas kernels  24 us (18%)
  other arithmetic  2.18 us (2%)
  local copies, waits for them, and re-layouts  2.09 us (2%)
  between operations  1.67 us (1%)
    ppermute x18, starting transfers between devices, along(): return lax.ppermute(value, 'rows', pairs)  40.2 us
    ppermute x18, waiting for transfers between devices, along(): return lax.ppermute(value, 'rows', pairs)  39.8 us
    ppermute x4, waiting for transfers between devices, from_chip(): return lax.ppermute(value, 'wide', pairs)  15.7 us
    pallas_call x2, Pallas kernels, aggregate(): call(body, 'aggregate', [jax.ShapeDtypeStruct((blocks * BLK, columns), ki...  10.1 us
    pallas_call x2, Pallas kernels, spread_back(): call(body, 'spread_back', [jax.ShapeDtypeStruct((chips * cols, sources *...  9.98 us
    ppermute x4, starting transfers between devices, from_chip(): return lax.ppermute(value, 'wide', pairs)  6.24 us
  transfers between devices with their start and end apart: 28, of which 8 were waited for; matrix products, arithmetic and copies ran while one was open for 2% of the time, Pallas kernels for 16%

profile of v1, /device:TPU:0, one launch (start us, length us, event | category | flops | bytes accessed | tf_op | source)
XLA Modules:
  0.0 134.1 jit_solution(10829875893964005335)
XLA Ops:
  0.6 0.0 copy-start
  0.7 0.5 collective-permute-start
  1.2 2.6 %collective-permute-start.5 = (bf16[64,3072]{1,0:T(8,128)(2,1)}, bf16[64,3072]{1,0:T(8,128)(2,1)S(1)}, u32[]{:S(2)}, u32[]{:S(2)}) collective-permute-start(bf16[64,3072]{1,0:T(8,128)(2,1)} %refs_0_.1), channel_id=1, source_target_pairs={{8,0},{12,4},{0,8},{4,12},{9,1},{13,5},{1,9},{5,13},{10,2},{14,6},... | collective-permute-start | bytes 1179656 | tf_op jit(solution)/shard_map/ppermute | solution.py:297
  3.8 0.1 broadcast_add_fusion
  3.8 0.1 add.131
  3.9 0.1 add.129
  4.7 0.1 stack.58.place_ref
  4.7 0.7 and_select_fusion.3.meta_ref
  5.5 8.2 %collective-permute-done.5.refs_0_ = bf16[64,3072]{1,0:T(8,128)(2,1)S(1)} collective-permute-done((bf16[64,3072]{1,0:T(8,128)(2,1)}, bf16[64,3072]{1,0:T(8,128)(2,1)S(1)}, u32[]{:S(2)}, u32[]{:S(2)}) %collective-permute-start.5) | collective-permute-done | bytes 393248 | tf_op jit(solution)/shard_map/ppermute | solution.py:297
  13.7 0.0 collective-permute-start.6
  13.7 0.0 copy-start.1
  13.7 1.0 copy-done.1
  14.7 5.0 %aggregate.2 = (f32[768,128]{1,0:T(8,128)S(1)}, bf16[768,128]{1,0:T(8,128)(2,1)S(1)}, bf16[768,128]{1,0:T(8,128)(2,1)S(1)}, bf16[768,128]{1,0:T(8,128)(2,1)S(1)}, bf16[768,128]{1,0:T(8,128)(2,1)S(1)}) custom-call(s32[240]{0:T(256)S(1)} %and_select_fusion.3.meta_ref, s32[5]{0:T(128)S(1)} %stack.58.place_ref, bf16[240,128,128]{2,1,0:T(8,128)(2,1)} %tiles_ref.7, ...), custom_call_target="tpu_custom_call" | custom-call | flops 503316480 | bytes 3932160 | tf_op jit(solution)/shard_map/aggregate/pallas_call | solution.py:123
  19.7 3.3 %collective-permute-start.3 = (bf16[768,128]{1,0:T(8,128)(2,1)S(1)}, bf16[768,128]{1,0:T(8,128)(2,1)S(1)}, u32[]{:S(2)}, u32[]{:S(2)}) collective-permute-start(bf16[768,128]{1,0:T(8,128)(2,1)S(1)} %get-tuple-element.28), channel_id=1, source_target_pairs={{0,1},{3,2},{4,5},{7,6},{8,9},{11,10},{12,13},{15,14},{16,17},{19,... | collective-permute-start | bytes 589832 | tf_op jit(solution)/shard_map/ppermute | solution.py:300
  23.0 0.1 broadcast_in_dim.18
  23.1 0.1 broadcast_in_dim.19
  23.2 0.6 gather_fusion
  23.8 0.1 pad_add_fusion.spot_ref
  23.8 1.3 collective-permute-start.1
  25.1 1.3 collective-permute-start.2
  26.4 0.0 collective-permute-done.6.refs_1_
  26.4 5.0 %aggregate.3 = (f32[768,128]{1,0:T(8,128)S(1)}, bf16[768,128]{1,0:T(8,128)(2,1)S(1)}, bf16[768,128]{1,0:T(8,128)(2,1)S(1)}, bf16[768,128]{1,0:T(8,128)(2,1)S(1)}, bf16[768,128]{1,0:T(8,128)(2,1)S(1)}) custom-call(s32[240]{0:T(256)S(1)} %and_select_fusion.3.meta_ref, s32[5]{0:T(128)S(1)} %stack.58.place_ref, bf16[240,128,128]{2,1,0:T(8,128)(2,1)} %tiles_ref.7, ...), custom_call_target="tpu_custom_call" | custom-call | flops 503316480 | bytes 3932160 | tf_op jit(solution)/shard_map/aggregate/pallas_call | solution.py:123
  31.5 4.1 %collective-permute-start.9 = (bf16[768,128]{1,0:T(8,128)(2,1)S(1)}, bf16[768,128]{1,0:T(8,128)(2,1)S(1)}, u32[]{:S(2)}, u32[]{:S(2)}) collective-permute-start(bf16[768,128]{1,0:T(8,128)(2,1)S(1)} %get-tuple-element.33), channel_id=1, source_target_pairs={{0,1},{3,2},{4,5},{7,6},{8,9},{11,10},{12,13},{15,14},{16,17},{19,... | collective-permute-start | bytes 589832 | tf_op jit(solution)/shard_map/ppermute | solution.py:300
  35.6 0.0 collective-permute-done.3
  35.6 0.1 add_convert_fusion.3
  35.7 1.1 collective-permute-start.4
  36.7 4.6 %collective-permute-start.7 = (bf16[768,128]{1,0:T(8,128)(2,1)S(1)}, bf16[768,128]{1,0:T(8,128)(2,1)S(1)}, u32[]{:S(2)}, u32[]{:S(2)}) collective-permute-start(bf16[768,128]{1,0:T(8,128)(2,1)S(1)} %get-tuple-element.30), channel_id=1, source_target_pairs={{0,1},{1,2},{2,3},{4,5},{5,6},{6,7},{8,9},{9,10},{10,11},{12,13},{... | collective-permute-start | bytes 589832 | tf_op jit(solution)/shard_map/ppermute | solution.py:300
  41.3 0.0 collective-permute-done.9
  41.3 1.3 collective-permute-start.8
  42.6 0.1 add_convert_fusion.2
  42.6 0.0 collective-permute-done.1.refs_1_
  42.7 4.3 %collective-permute-start.10 = (bf16[768,128]{1,0:T(8,128)(2,1)S(1)}, bf16[768,128]{1,0:T(8,128)(2,1)S(1)}, u32[]{:S(2)}, u32[]{:S(2)}) collective-permute-start(bf16[768,128]{1,0:T(8,128)(2,1)S(1)} %add_convert_fusion.2), channel_id=1, source_target_pairs={{0,2},{1,3},{2,0},{3,1},{4,6},{5,7},{6,4},{7,5},{8,10},{9,11},{10,... | collective-permute-start | bytes 589832 | tf_op jit(solution)/shard_map/ppermute | solution.py:300
  47.0 0.1 bitcast_select_fusion.refs_8_
  47.1 2.2 %collective-permute-done.7.refs_5_ = bf16[768,128]{1,0:T(8,128)(2,1)S(1)} collective-permute-done((bf16[768,128]{1,0:T(8,128)(2,1)S(1)}, bf16[768,128]{1,0:T(8,128)(2,1)S(1)}, u32[]{:S(2)}, u32[]{:S(2)}) %collective-permute-start.7) | collective-permute-done | bytes 196640 | tf_op jit(solution)/shard_map/ppermute | solution.py:300
  49.3 10.9 %collective-permute-done.10.refs_7_ = bf16[768,128]{1,0:T(8,128)(2,1)S(1)} collective-permute-done((bf16[768,128]{1,0:T(8,128)(2,1)S(1)}, bf16[768,128]{1,0:T(8,128)(2,1)S(1)}, u32[]{:S(2)}, u32[]{:S(2)}) %collective-permute-start.10) | collective-permute-done | bytes 196640 | tf_op jit(solution)/shard_map/ppermute | solution.py:300
  60.2 2.7 %layer.1 = (bf16[768,256]{1,0:T(8,128)(2,1)}, bf16[128,768]{1,0:T(8,128)(2,1)S(1)}, bf16[128,768]{1,0:T(8,128)(2,1)S(1)}, f32[2,2,72,256]{3,2,1,0:T(8,128)S(1)}) custom-call(s32[2]{0:T(128)S(1)} %pad_add_fusion.spot_ref, f32[768,128]{1,0:T(8,128)S(1)} %get-tuple-element.24.refs_0_, bf16[768,128]{1,0:T(8,128)(2,1)S(1)} %collective-permute-done.1.refs_1_, ...), custom_call_target="tpu_custom_call" | custom-call | flops 301989888 | bytes 1966080 | tf_op jit(solution)/shard_map/layer/pallas_call | solution.py:232
  62.9 0.1 collective-permute-start.22
  63.0 1.8 %collective-permute-start.16 = (bf16[128,768]{1,0:T(8,128)(2,1)S(1)}, bf16[128,768]{1,0:T(8,128)(2,1)S(1)}, u32[]{:S(2)}, u32[]{:S(2)}) collective-permute-start(bf16[128,768]{1,0:T(8,128)(2,1)S(1)} %get-tuple-element.38.refs_0_), channel_id=1, source_target_pairs={{0,1},{1,2},{2,3},{4,5},{5,6},{6,7},{8,9},{9,10},{10,11},{12,13},{... | collective-permute-start | bytes 589832 | tf_op jit(solution)/shard_map/ppermute | solution.py:300
  64.8 1.3 collective-permute-start.17
  66.1 4.1 %collective-permute-start.18 = (bf16[128,768]{1,0:T(8,128)(2,1)S(1)}, bf16[128,768]{1,0:T(8,128)(2,1)S(1)}, u32[]{:S(2)}, u32[]{:S(2)}) collective-permute-start(bf16[128,768]{1,0:T(8,128)(2,1)S(1)} %get-tuple-element.38.refs_0_), channel_id=1, source_target_pairs={{0,2},{1,3},{2,0},{3,1},{4,6},{5,7},{6,4},{7,5},{8,10},{9,11},{10,... | collective-permute-start | bytes 589832 | tf_op jit(solution)/shard_map/ppermute | solution.py:300
  70.1 0.1 collective-permute-start.13
  70.2 18.1 %collective-permute-done.18.refs_3_ = bf16[128,768]{1,0:T(8,128)(2,1)S(1)} collective-permute-done((bf16[128,768]{1,0:T(8,128)(2,1)S(1)}, bf16[128,768]{1,0:T(8,128)(2,1)S(1)}, u32[]{:S(2)}, u32[]{:S(2)}) %collective-permute-start.18) | collective-permute-done | bytes 196640 | tf_op jit(solution)/shard_map/ppermute | solution.py:300
  88.4 1.3 collective-permute-start.19
  89.7 1.5 %collective-permute-start.23 = (f32[72,256]{1,0:T(8,128)S(1)}, f32[72,256]{1,0:T(8,128)S(1)}, u32[]{:S(2)}, u32[]{:S(2)}) collective-permute-start(f32[72,256]{1,0:T(8,128)S(1)} %slice_bitcast_fusion.3), channel_id=1, source_target_pairs={{8,0},{12,4},{0,8},{4,12},{9,1},{13,5},{1,9},{5,13},{10,2},{14,6},... | collective-permute-start | bytes 221192 | tf_op jit(solution)/shard_map/ppermute | solution.py:297
  91.2 0.1 stack.62.place_ref
  91.3 4.6 %collective-permute-start.11 = (bf16[128,768]{1,0:T(8,128)(2,1)S(1)}, bf16[128,768]{1,0:T(8,128)(2,1)S(1)}, u32[]{:S(2)}, u32[]{:S(2)}) collective-permute-start(bf16[128,768]{1,0:T(8,128)(2,1)S(1)} %get-tuple-element.35.refs_0_), channel_id=1, source_target_pairs={{0,1},{1,2},{2,3},{4,5},{5,6},{6,7},{8,9},{9,10},{10,11},{12,13},{... | collective-permute-start | bytes 589832 | tf_op jit(solution)/shard_map/ppermute | solution.py:300
  95.8 1.3 collective-permute-start.12
  97.2 1.3 collective-permute-start.14
  98.5 5.0 %spread_back.3 = (f32[64,3072]{1,0:T(8,128)S(1)}, bf16[64,3072]{1,0:T(8,128)(2,1)S(1)}) custom-call(s32[240]{0:T(256)S(1)} %and_select_fusion.3.meta_ref, s32[5]{0:T(128)S(1)} %stack.62.place_ref, bf16[240,128,128]{2,1,0:T(8,128)(2,1)} %tiles_ref.7, bf16[128,768]{1,0:T(8,128)(2,1)S(1)} %get-tuple-element.38.refs_0_, ...), custom_call_target="tpu_custom_call" | custom-call | flops 503316480 | bytes 3932160 | tf_op jit(solution)/shard_map/spread_back/pallas_call | solution.py:166
  103.5 0.1 collective-permute-start.20
  103.6 2.2 %collective-permute-start.24 = (f32[72,256]{1,0:T(8,128)S(1)}, f32[72,256]{1,0:T(8,128)S(1)}, u32[]{:S(2)}, u32[]{:S(2)}) collective-permute-start(f32[72,256]{1,0:T(8,128)S(1)} %fusion), channel_id=1, source_target_pairs={{0,1},{1,0},{2,3},{3,2},{4,5},{5,4},{6,7},{7,6},{8,9},{9,8},{10,11... | collective-permute-start | bytes 221192 | tf_op jit(solution)/shard_map/ppermute | solution.py:300
  105.8 3.0 %collective-permute-done.24 = f32[72,256]{1,0:T(8,128)S(1)} collective-permute-done((f32[72,256]{1,0:T(8,128)S(1)}, f32[72,256]{1,0:T(8,128)S(1)}, u32[]{:S(2)}, u32[]{:S(2)}) %collective-permute-start.24) | collective-permute-done | bytes 73760 | tf_op jit(solution)/shard_map/ppermute | solution.py:300
  108.8 1.2 collective-permute-start.25
  110.0 5.6 %collective-permute-done.25 = f32[72,256]{1,0:T(8,128)S(1)} collective-permute-done((f32[72,256]{1,0:T(8,128)S(1)}, f32[72,256]{1,0:T(8,128)S(1)}, u32[]{:S(2)}, u32[]{:S(2)}) %collective-permute-start.25) | collective-permute-done | bytes 73760 | tf_op jit(solution)/shard_map/ppermute | solution.py:300
  115.6 0.9 collective-permute-start.26
  116.5 5.0 %spread_back.2 = (f32[64,3072]{1,0:T(8,128)S(1)}, bf16[64,3072]{1,0:T(8,128)(2,1)S(1)}) custom-call(s32[240]{0:T(256)S(1)} %and_select_fusion.3.meta_ref, s32[5]{0:T(128)S(1)} %stack.62.place_ref, bf16[240,128,128]{2,1,0:T(8,128)(2,1)} %tiles_ref.7, bf16[128,768]{1,0:T(8,128)(2,1)S(1)} %get-tuple-element.35.refs_0_, ...), custom_call_target="tpu_custom_call" | custom-call | flops 503316480 | bytes 3932160 | tf_op jit(solution)/shard_map/spread_back/pallas_call | solution.py:166
  121.5 0.1 collective-permute-start.15
  121.5 0.1 add_convert_fusion.1
  121.6 1.3 collective-permute-start.21
  122.9 0.3 collective-permute-start.27
  123.2 1.2 collective-permute-done.27
  124.4 1.3 assemble.1
  125.7 7.6 %collective-permute-done.21 = bf16[64,3072]{1,0:T(8,128)(2,1)S(1)} collective-permute-done((bf16[64,3072]{1,0:T(8,128)(2,1)S(1)}, bf16[64,3072]{1,0:T(8,128)(2,1)S(1)}, u32[]{:S(2)}, u32[]{:S(2)}) %collective-permute-start.21) | collective-permute-done | bytes 393248 | tf_op jit(solution)/shard_map/ppermute | solution.py:297
  133.2 0.9 add_convert_fusion
  (34 shorter events, 0.2 us)
Async XLA Ops:
  0.6 22.6 %copy-start = (bf16[256,256]{1,0:T(8,128)(2,1)S(1)}, bf16[256,256]{1,0:T(8,128)(2,1)}, u32[]{:S(2)}) copy-start(bf16[256,256]{1,0:T(8,128)(2,1)} %param.13) | copy-start | bytes 393220
  0.6 22.5 %copy-start.3 = (bf16[256]{0:T(256)(128)(2,1)S(1)}, bf16[256]{0:T(256)(128)(2,1)}, u32[]{:S(2)}) copy-start(bf16[256]{0:T(256)(128)(2,1)} %param.14) | copy-start | bytes 1540
  0.7 13.0 %collective-permute-start = (bf16[64,3072]{1,0:T(8,128)(2,1)}, bf16[64,3072]{1,0:T(8,128)(2,1)S(1)}, u32[]{:S(2)}, u32[]{:S(2)}) collective-permute-start(bf16[64,3072]{1,0:T(8,128)(2,1)} %refs_0_.1), channel_id=1, source_target_pairs={{0,4},{4,0},{8,12},{12,8},{1,5},{5,1},{9,13},{13,9},{2,6},{6,2},{1... | collective-permute-start | bytes 1179656 | tf_op jit(solution)/shard_map/ppermute | solution.py:293
  1.2 12.5 %collective-permute-start.5 = (bf16[64,3072]{1,0:T(8,128)(2,1)}, bf16[64,3072]{1,0:T(8,128)(2,1)S(1)}, u32[]{:S(2)}, u32[]{:S(2)}) collective-permute-start(bf16[64,3072]{1,0:T(8,128)(2,1)} %refs_0_.1), channel_id=1, source_target_pairs={{8,0},{12,4},{0,8},{4,12},{9,1},{13,5},{1,9},{5,13},{10,2},{14,6},... | collective-permute-start | bytes 1179656 | tf_op jit(solution)/shard_map/ppermute | solution.py:297
  13.7 12.8 %collective-permute-start.6 = (bf16[64,3072]{1,0:T(8,128)(2,1)S(1)}, bf16[64,3072]{1,0:T(8,128)(2,1)S(1)}, u32[]{:S(2)}, u32[]{:S(2)}) collective-permute-start(bf16[64,3072]{1,0:T(8,128)(2,1)S(1)} %collective-permute-done.5.refs_0_), channel_id=1, source_target_pairs={{0,4},{4,0},{8,12},{12,8},{1,5},{5,1},{9,13},{13,9},{2,6},{6,2},{1... | collective-permute-start | bytes 1179656 | tf_op jit(solution)/shard_map/ppermute | solution.py:293
  13.7 1.0 copy-start.1
  14.7 45.5 %copy-start.2 = (bf16[768,256]{1,0:T(8,128)(2,1)S(1)}, bf16[768,256]{1,0:T(8,128)(2,1)}, u32[]{:S(2)}) copy-start(bf16[768,256]{1,0:T(8,128)(2,1)} %refs_10_.1) | copy-start | bytes 1179652
  19.7 15.8 %collective-permute-start.3 = (bf16[768,128]{1,0:T(8,128)(2,1)S(1)}, bf16[768,128]{1,0:T(8,128)(2,1)S(1)}, u32[]{:S(2)}, u32[]{:S(2)}) collective-permute-start(bf16[768,128]{1,0:T(8,128)(2,1)S(1)} %get-tuple-element.28), channel_id=1, source_target_pairs={{0,1},{3,2},{4,5},{7,6},{8,9},{11,10},{12,13},{15,14},{16,17},{19,... | collective-permute-start | bytes 589832 | tf_op jit(solution)/shard_map/ppermute | solution.py:300
  23.8 18.8 %collective-permute-start.1 = (bf16[768,128]{1,0:T(8,128)(2,1)S(1)}, bf16[768,128]{1,0:T(8,128)(2,1)S(1)}, u32[]{:S(2)}, u32[]{:S(2)}) collective-permute-start(bf16[768,128]{1,0:T(8,128)(2,1)S(1)} %get-tuple-element.25), channel_id=1, source_target_pairs={{0,1},{1,2},{2,3},{4,5},{5,6},{6,7},{8,9},{9,10},{10,11},{12,13},{... | collective-permute-start | bytes 589832 | tf_op jit(solution)/shard_map/ppermute | solution.py:300
  25.1 22.0 %collective-permute-start.2 = (bf16[768,128]{1,0:T(8,128)(2,1)S(1)}, bf16[768,128]{1,0:T(8,128)(2,1)S(1)}, u32[]{:S(2)}, u32[]{:S(2)}) collective-permute-start(bf16[768,128]{1,0:T(8,128)(2,1)S(1)} %get-tuple-element.26), channel_id=1, source_target_pairs={{1,0},{2,1},{3,2},{5,4},{6,5},{7,6},{9,8},{10,9},{11,10},{13,12},{... | collective-permute-start | bytes 589832 | tf_op jit(solution)/shard_map/ppermute | solution.py:300
  31.5 9.8 %collective-permute-start.9 = (bf16[768,128]{1,0:T(8,128)(2,1)S(1)}, bf16[768,128]{1,0:T(8,128)(2,1)S(1)}, u32[]{:S(2)}, u32[]{:S(2)}) collective-permute-start(bf16[768,128]{1,0:T(8,128)(2,1)S(1)} %get-tuple-element.33), channel_id=1, source_target_pairs={{0,1},{3,2},{4,5},{7,6},{8,9},{11,10},{12,13},{15,14},{16,17},{19,... | collective-permute-start | bytes 589832 | tf_op jit(solution)/shard_map/ppermute | solution.py:300
  35.7 11.5 %collective-permute-start.4 = (bf16[768,128]{1,0:T(8,128)(2,1)S(1)}, bf16[768,128]{1,0:T(8,128)(2,1)S(1)}, u32[]{:S(2)}, u32[]{:S(2)}) collective-permute-start(bf16[768,128]{1,0:T(8,128)(2,1)S(1)} %add_convert_fusion.3), channel_id=1, source_target_pairs={{0,2},{1,3},{2,0},{3,1},{4,6},{5,7},{6,4},{7,5},{8,10},{9,11},{10,... | collective-permute-start | bytes 589832 | tf_op jit(solution)/shard_map/ppermute | solution.py:300
  36.7 12.6 %collective-permute-start.7 = (bf16[768,128]{1,0:T(8,128)(2,1)S(1)}, bf16[768,128]{1,0:T(8,128)(2,1)S(1)}, u32[]{:S(2)}, u32[]{:S(2)}) collective-permute-start(bf16[768,128]{1,0:T(8,128)(2,1)S(1)} %get-tuple-element.30), channel_id=1, source_target_pairs={{0,1},{1,2},{2,3},{4,5},{5,6},{6,7},{8,9},{9,10},{10,11},{12,13},{... | collective-permute-start | bytes 589832 | tf_op jit(solution)/shard_map/ppermute | solution.py:300
  41.3 8.1 %collective-permute-start.8 = (bf16[768,128]{1,0:T(8,128)(2,1)S(1)}, bf16[768,128]{1,0:T(8,128)(2,1)S(1)}, u32[]{:S(2)}, u32[]{:S(2)}) collective-permute-start(bf16[768,128]{1,0:T(8,128)(2,1)S(1)} %get-tuple-element.31), channel_id=1, source_target_pairs={{1,0},{2,1},{3,2},{5,4},{6,5},{7,6},{9,8},{10,9},{11,10},{13,12},{... | collective-permute-start | bytes 589832 | tf_op jit(solution)/shard_map/ppermute | solution.py:300
  42.7 17.6 %collective-permute-start.10 = (bf16[768,128]{1,0:T(8,128)(2,1)S(1)}, bf16[768,128]{1,0:T(8,128)(2,1)S(1)}, u32[]{:S(2)}, u32[]{:S(2)}) collective-permute-start(bf16[768,128]{1,0:T(8,128)(2,1)S(1)} %add_convert_fusion.2), channel_id=1, source_target_pairs={{0,2},{1,3},{2,0},{3,1},{4,6},{5,7},{6,4},{7,5},{8,10},{9,11},{10,... | collective-permute-start | bytes 589832 | tf_op jit(solution)/shard_map/ppermute | solution.py:300
  62.9 7.3 %collective-permute-start.22 = (f32[2,72,256]{2,1,0:T(8,128)S(1)}, f32[2,72,256]{2,1,0:T(8,128)S(1)}, u32[]{:S(2)}, u32[]{:S(2)}) collective-permute-start(f32[2,72,256]{2,1,0:T(8,128)S(1)} %slice_bitcast_fusion), channel_id=1, source_target_pairs={{0,4},{4,0},{8,12},{12,8},{1,5},{5,1},{9,13},{13,9},{2,6},{6,2},{1... | collective-permute-start | bytes 442376 | tf_op jit(solution)/shard_map/ppermute | solution.py:293
  63.0 28.3 %collective-permute-start.16 = (bf16[128,768]{1,0:T(8,128)(2,1)S(1)}, bf16[128,768]{1,0:T(8,128)(2,1)S(1)}, u32[]{:S(2)}, u32[]{:S(2)}) collective-permute-start(bf16[128,768]{1,0:T(8,128)(2,1)S(1)} %get-tuple-element.38.refs_0_), channel_id=1, source_target_pairs={{0,1},{1,2},{2,3},{4,5},{5,6},{6,7},{8,9},{9,10},{10,11},{12,13},{... | collective-permute-start | bytes 589832 | tf_op jit(solution)/shard_map/ppermute | solution.py:300
  64.8 31.1 %collective-permute-start.17 = (bf16[128,768]{1,0:T(8,128)(2,1)S(1)}, bf16[128,768]{1,0:T(8,128)(2,1)S(1)}, u32[]{:S(2)}, u32[]{:S(2)}) collective-permute-start(bf16[128,768]{1,0:T(8,128)(2,1)S(1)} %get-tuple-element.38.refs_0_), channel_id=1, source_target_pairs={{1,0},{2,1},{3,2},{5,4},{6,5},{7,6},{9,8},{10,9},{11,10},{13,12},{... | collective-permute-start | bytes 589832 | tf_op jit(solution)/shard_map/ppermute | solution.py:300
  66.1 22.3 %collective-permute-start.18 = (bf16[128,768]{1,0:T(8,128)(2,1)S(1)}, bf16[128,768]{1,0:T(8,128)(2,1)S(1)}, u32[]{:S(2)}, u32[]{:S(2)}) collective-permute-start(bf16[128,768]{1,0:T(8,128)(2,1)S(1)} %get-tuple-element.38.refs_0_), channel_id=1, source_target_pairs={{0,2},{1,3},{2,0},{3,1},{4,6},{5,7},{6,4},{7,5},{8,10},{9,11},{10,... | collective-permute-start | bytes 589832 | tf_op jit(solution)/shard_map/ppermute | solution.py:300
  70.1 27.0 %collective-permute-start.13 = (bf16[128,768]{1,0:T(8,128)(2,1)S(1)}, bf16[128,768]{1,0:T(8,128)(2,1)S(1)}, u32[]{:S(2)}, u32[]{:S(2)}) collective-permute-start(bf16[128,768]{1,0:T(8,128)(2,1)S(1)} %get-tuple-element.35.refs_0_), channel_id=1, source_target_pairs={{0,2},{1,3},{2,0},{3,1},{4,6},{5,7},{6,4},{7,5},{8,10},{9,11},{10,... | collective-permute-start | bytes 589832 | tf_op jit(solution)/shard_map/ppermute | solution.py:300
  88.4 10.1 %collective-permute-start.19 = (bf16[128,768]{1,0:T(8,128)(2,1)S(1)}, bf16[128,768]{1,0:T(8,128)(2,1)S(1)}, u32[]{:S(2)}, u32[]{:S(2)}) collective-permute-start(bf16[128,768]{1,0:T(8,128)(2,1)S(1)} %collective-permute-done.18.refs_3_), channel_id=1, source_target_pairs={{2,3},{1,0},{6,7},{5,4},{10,11},{9,8},{14,15},{13,12},{18,19},{17,... | collective-permute-start | bytes 589832 | tf_op jit(solution)/shard_map/ppermute | solution.py:300
  89.7 13.9 %collective-permute-start.23 = (f32[72,256]{1,0:T(8,128)S(1)}, f32[72,256]{1,0:T(8,128)S(1)}, u32[]{:S(2)}, u32[]{:S(2)}) collective-permute-start(f32[72,256]{1,0:T(8,128)S(1)} %slice_bitcast_fusion.3), channel_id=1, source_target_pairs={{8,0},{12,4},{0,8},{4,12},{9,1},{13,5},{1,9},{5,13},{10,2},{14,6},... | collective-permute-start | bytes 221192 | tf_op jit(solution)/shard_map/ppermute | solution.py:297
  91.3 25.2 %collective-permute-start.11 = (bf16[128,768]{1,0:T(8,128)(2,1)S(1)}, bf16[128,768]{1,0:T(8,128)(2,1)S(1)}, u32[]{:S(2)}, u32[]{:S(2)}) collective-permute-start(bf16[128,768]{1,0:T(8,128)(2,1)S(1)} %get-tuple-element.35.refs_0_), channel_id=1, source_target_pairs={{0,1},{1,2},{2,3},{4,5},{5,6},{6,7},{8,9},{9,10},{10,11},{12,13},{... | collective-permute-start | bytes 589832 | tf_op jit(solution)/shard_map/ppermute | solution.py:300
  95.8 20.6 %collective-permute-start.12 = (bf16[128,768]{1,0:T(8,128)(2,1)S(1)}, bf16[128,768]{1,0:T(8,128)(2,1)S(1)}, u32[]{:S(2)}, u32[]{:S(2)}) collective-permute-start(bf16[128,768]{1,0:T(8,128)(2,1)S(1)} %get-tuple-element.35.refs_0_), channel_id=1, source_target_pairs={{1,0},{2,1},{3,2},{5,4},{6,5},{7,6},{9,8},{10,9},{11,10},{13,12},{... | collective-permute-start | bytes 589832 | tf_op jit(solution)/shard_map/ppermute | solution.py:300
  97.2 19.3 %collective-permute-start.14 = (bf16[128,768]{1,0:T(8,128)(2,1)S(1)}, bf16[128,768]{1,0:T(8,128)(2,1)S(1)}, u32[]{:S(2)}, u32[]{:S(2)}) collective-permute-start(bf16[128,768]{1,0:T(8,128)(2,1)S(1)} %collective-permute-done.13.refs_3_), channel_id=1, source_target_pairs={{2,3},{1,0},{6,7},{5,4},{10,11},{9,8},{14,15},{13,12},{18,19},{17,... | collective-permute-start | bytes 589832 | tf_op jit(solution)/shard_map/ppermute | solution.py:300
  103.5 18.1 %collective-permute-start.20 = (bf16[64,3072]{1,0:T(8,128)(2,1)S(1)}, bf16[64,3072]{1,0:T(8,128)(2,1)S(1)}, u32[]{:S(2)}, u32[]{:S(2)}) collective-permute-start(bf16[64,3072]{1,0:T(8,128)(2,1)S(1)} %get-tuple-element.40), channel_id=1, source_target_pairs={{0,4},{4,0},{8,12},{12,8},{1,5},{5,1},{9,13},{13,9},{2,6},{6,2},{1... | collective-permute-start | bytes 1179656 | tf_op jit(solution)/shard_map/ppermute | solution.py:293
  103.6 5.2 %collective-permute-start.24 = (f32[72,256]{1,0:T(8,128)S(1)}, f32[72,256]{1,0:T(8,128)S(1)}, u32[]{:S(2)}, u32[]{:S(2)}) collective-permute-start(f32[72,256]{1,0:T(8,128)S(1)} %fusion), channel_id=1, source_target_pairs={{0,1},{1,0},{2,3},{3,2},{4,5},{5,4},{6,7},{7,6},{8,9},{9,8},{10,11... | collective-permute-start | bytes 221192 | tf_op jit(solution)/shard_map/ppermute | solution.py:300
  108.8 6.7 %collective-permute-start.25 = (f32[72,256]{1,0:T(8,128)S(1)}, f32[72,256]{1,0:T(8,128)S(1)}, u32[]{:S(2)}, u32[]{:S(2)}) collective-permute-start(f32[72,256]{1,0:T(8,128)S(1)} %add.138), channel_id=1, source_target_pairs={{0,2},{1,3},{2,0},{3,1},{4,6},{5,7},{6,4},{7,5},{8,10},{9,11},{10,... | collective-permute-start | bytes 221192 | tf_op jit(solution)/shard_map/ppermute | solution.py:300
  115.6 7.4 %collective-permute-start.26 = (f32[72,256]{1,0:T(8,128)S(1)}, f32[72,256]{1,0:T(8,128)S(1)}, u32[]{:S(2)}, u32[]{:S(2)}) collective-permute-start(f32[72,256]{1,0:T(8,128)S(1)} %add.139.refs_0_), channel_id=1, source_target_pairs={{8,0},{12,4},{0,8},{4,12},{9,1},{13,5},{1,9},{5,13},{10,2},{14,6},... | collective-permute-start | bytes 221192 | tf_op jit(solution)/shard_map/ppermute | solution.py:297
  121.5 4.2 %collective-permute-start.15 = (bf16[64,3072]{1,0:T(8,128)(2,1)S(1)}, bf16[64,3072]{1,0:T(8,128)(2,1)S(1)}, u32[]{:S(2)}, u32[]{:S(2)}) collective-permute-start(bf16[64,3072]{1,0:T(8,128)(2,1)S(1)} %get-tuple-element.37), channel_id=1, source_target_pairs={{0,4},{4,0},{8,12},{12,8},{1,5},{5,1},{9,13},{13,9},{2,6},{6,2},{1... | collective-permute-start | bytes 1179656 | tf_op jit(solution)/shard_map/ppermute | solution.py:293
  121.6 11.6 %collective-permute-start.21 = (bf16[64,3072]{1,0:T(8,128)(2,1)S(1)}, bf16[64,3072]{1,0:T(8,128)(2,1)S(1)}, u32[]{:S(2)}, u32[]{:S(2)}) collective-permute-start(bf16[64,3072]{1,0:T(8,128)(2,1)S(1)} %add_convert_fusion.1), channel_id=1, source_target_pairs={{8,0},{12,4},{0,8},{4,12},{9,1},{13,5},{1,9},{5,13},{10,2},{14,6},... | collective-permute-start | bytes 1179656 | tf_op jit(solution)/shard_map/ppermute | solution.py:297
  122.9 1.4 %collective-permute-start.27 = (f32[2,72,256]{2,1,0:T(8,128)S(1)}, f32[2,72,256]{2,1,0:T(8,128)S(1)}, u32[]{:S(2)}, u32[]{:S(2)}) collective-permute-start(f32[2,72,256]{2,1,0:T(8,128)S(1)} %pad_maximum_fusion), channel_id=1, source_target_pairs={{0,4},{4,0},{8,12},{12,8},{1,5},{5,1},{9,13},{13,9},{2,6},{6,2},{1... | collective-permute-start | bytes 442376 | tf_op jit(solution)/shard_map/ppermute | solution.py:293

commit v2 on v1

v2 whole, which is shorter than its diff:
```python
import functools
import math

import jax
import jax.numpy as jnp
from jax import lax
from jax.experimental import pallas as pl
from jax.experimental.pallas import tpu as pltpu
from jax.sharding import PartitionSpec as P

BLK = 128
GROUP = 16
RS_FAR = "pair"
RS_NEAR = "pair"
AG_NEAR = "pair"
AG_FAR = "all"
TIE = 0
RING = 4
VMEM_BYTES = 48 * 1024 * 1024
ROOT = math.sqrt(2.0 / math.pi)
CUBIC = 0.044715
BF16 = jnp.bfloat16
F32 = jnp.float32

SMEM_SPEC = pl.BlockSpec(memory_space=pltpu.SMEM)
VMEM_SPEC = pl.BlockSpec(memory_space=pltpu.VMEM)
ANY_SPEC = pl.BlockSpec(memory_space=pl.ANY)


def bits_of(size):
    return max(1, int(size).bit_length())


def call(body, name, out_shape, in_specs, scratch, flops, nbytes):
    return pl.pallas_call(
        body,
        name=name,
        out_shape=out_shape,
        in_specs=in_specs,
        out_specs=jax.tree.map(lambda _: VMEM_SPEC, out_shape),
        scratch_shapes=scratch,
        compiler_params=pltpu.CompilerParams(vmem_limit_bytes=VMEM_BYTES),
        cost_estimate=pl.CostEstimate(flops=flops, bytes_accessed=nbytes, transcendentals=0),
    )


def each_tile(meta, wanted, picked, tiles, ring, sems, tile_bits, prepare, multiply, add):
    total = meta.shape[0]
    tile_mask = (1 << tile_bits) - 1

    def scan(step, found):
        for u in range(GROUP):
            entry = meta[step * GROUP + u]
            picked[found] = entry
            found = found + jnp.where(wanted(entry), 1, 0)
        return found

    found = lax.fori_loop(0, total // GROUP, scan, jnp.int32(0))
    for u in range(GROUP):
        picked[found + u] = jnp.int32(-1)
    groups = lax.div(found + (GROUP - 1), GROUP)

    def copies(group):
        base = lax.rem(group, RING) * GROUP
        for u in range(GROUP):
            tile = jnp.maximum(picked[group * GROUP + u], 0) & tile_mask
            yield pltpu.make_async_copy(tiles.at[tile], ring.at[base + u], sems.at[base + u])

    def start(group, carry):
        for copy in copies(group):
            copy.start()
        return carry

    lax.fori_loop(0, jnp.minimum(groups, RING), start, 0)
    prepare()

    def work(group, carry):
        for copy in copies(group):
            copy.wait()
        base = lax.rem(group, RING) * GROUP
        entries = [picked[group * GROUP + u] for u in range(GROUP)]
        products = [multiply(entries[u], ring.at[base + u]) for u in range(GROUP)]
        for u in range(GROUP):
            add(entries[u], products[u])

        @pl.when(group + RING < groups)
        def _():
            start(group + RING, 0)

        return carry

    lax.fori_loop(0, groups, work, 0)


def ring_scratch(slots):
    return [
        pltpu.SMEM((slots + GROUP,), jnp.int32),
        pltpu.VMEM((RING * GROUP, BLK, BLK), BF16),
        pltpu.SemaphoreType.DMA((RING * GROUP,)),
    ]


def row_at(shift):
    count = lax.axis_size("rows")
    return lax.rem(lax.axis_index("rows") + (shift % count), count)


def places_of(way, scatter):
    count = lax.axis_size("rows")
    if way == "all":
        return [(row, True) for row in range(count)]
    if way == "direct":
        return [(row_at(s if scatter else -s), True) for s in range(count)]
    row = lax.axis_index("rows")
    if scatter:
        return [(row ^ i, True) for i in (0, 3, 1, 2)]
    return [(row ^ i, True) for i in (0, 2, 1, 3)]


def aggregate(meta, tiles, parts, first, dests, chunk, tile_bits, source_bits, way):
    columns = sum(part.shape[0] for part in parts)
    sources = parts[0].shape[1] // BLK
    source_mask = (1 << source_bits) - 1
    if way == "all":
        shapes = [jax.ShapeDtypeStruct((dests * BLK, columns), BF16)]
    else:
        count = dests // chunk
        shapes = [
            jax.ShapeDtypeStruct((chunk * BLK, columns), F32 if i == 0 else BF16) for i in range(count)
        ]

    def body(meta_ref, tiles_ref, own_ref, *refs):
        part_refs = refs[: len(parts) - 1]
        outs = refs[len(parts) - 1 : len(parts) - 1 + len(shapes)]
        own, own_sem, turned, total, picked, ring, sems = refs[len(parts) - 1 + len(shapes) :]
        fetch = pltpu.make_async_copy(own_ref, own, own_sem)
        fetch.start()

        def prepare():
            fetch.wait()
            total[...] = jnp.zeros_like(total)
            for s in range(sources):
                now = slice(s * BLK, (s + 1) * BLK)
                block = jnp.concatenate([own[:, now]] + [ref[:, now] for ref in part_refs], axis=0)
                turned[s] = jnp.transpose(block)

        def multiply(entry, tile):
            source = (jnp.maximum(entry, 0) >> tile_bits) & source_mask
            return jnp.dot(tile[...], turned[source], preferred_element_type=F32)

        def add(entry, product):
            dest = (entry >> (tile_bits + source_bits)) - first
            total[jnp.where(entry < 0, dests, dest)] += product

        def wanted(entry):
            dest = entry >> (tile_bits + source_bits)
            return (dest >= first) & (dest < first + dests)

        each_tile(
            meta_ref, wanted, picked, tiles_ref, ring, sems, tile_bits, prepare, multiply, add
        )
        if way == "all":
            outs[0][...] = total[:dests].reshape(outs[0].shape).astype(BF16)
        else:
            for out, (place, _) in zip(outs, places_of(way, True)):
                out[...] = total[pl.ds(place * chunk, chunk)].reshape(out.shape).astype(out.dtype)

    slots = tiles.shape[0]
    return call(
        body,
        "aggregate",
        shapes,
        [SMEM_SPEC, ANY_SPEC, ANY_SPEC] + [VMEM_SPEC] * (len(parts) - 1),
        [
            pltpu.VMEM(parts[0].shape, BF16),
            pltpu.SemaphoreType.DMA,
            pltpu.VMEM((sources, BLK, columns), BF16),
            pltpu.VMEM((dests + 1, BLK, columns), F32),
        ]
        + ring_scratch(tiles.shape[0]),
        slots * BLK * BLK * columns,
        slots * BLK * BLK,
    )(meta, tiles, *parts)


def spread_back(meta, tiles, groups, columns, sources, tile_bits, source_bits, cols):
    source_mask = (1 << source_bits) - 1
    given = [piece for _, _, pieces in groups for piece in pieces]
    sizes = [blocks * lax.axis_size("rows") for blocks, _, _ in groups]
    spare = sum(sizes)

    def body(meta_ref, tiles_ref, *refs):
        part_refs = refs[: len(given)]
        keep, send, held, total, picked, ring, sems = refs[len(given) :]

        def prepare():
            total[...] = jnp.zeros_like(total)
            held[spare] = jnp.zeros_like(held[spare])
            start, at = 0, 0
            for (blocks, way, pieces), size in zip(groups, sizes):
                places = places_of(way, False)
                count = len(places) // len(pieces)
                for i, (place, there) in enumerate(places):
                    ref = part_refs[at + i // count]
                    low = (i % count) * (ref.shape[0] // count)

                    def take(ref=ref, low=low, place=place, blocks=blocks, start=start):
                        for q in range(blocks):
                            held[start + place * blocks + q] = ref[
                                low : low + columns, q * BLK : (q + 1) * BLK
                            ]

                    if there is True:
                        take()
                    else:
                        pl.when(there)(take)
                at += len(pieces)
                start += size

        def multiply(entry, tile):
            dest = jnp.where(entry < 0, spare, entry >> (tile_bits + source_bits))
            return jnp.dot(held[dest], tile[...], preferred_element_type=F32)

        def add(entry, product):
            source = (jnp.maximum(entry, 0) >> tile_bits) & source_mask
            total[source] += product

        each_tile(
            meta_ref, lambda entry: entry >= 0, picked, tiles_ref, ring, sems, tile_bits,
            prepare, multiply, add,
        )
        for s in range(sources):
            keep[:, s * BLK : (s + 1) * BLK] = total[s, :cols, :]
            send[:, s * BLK : (s + 1) * BLK] = total[s, cols:, :].astype(BF16)

    slots = tiles.shape[0]
    return call(
        body,
        "spread_back",
        [
            jax.ShapeDtypeStruct((cols, sources * BLK), F32),
            jax.ShapeDtypeStruct((cols, sources * BLK), BF16),
        ],
        [SMEM_SPEC, ANY_SPEC] + [VMEM_SPEC] * len(given),
        [
            pltpu.VMEM((spare + 1, columns, BLK), BF16),
            pltpu.VMEM((sources, columns, BLK), F32),
        ]
        + ring_scratch(tiles.shape[0]),
        slots * BLK * BLK * columns,
        slots * BLK * BLK,
    )(meta, tiles, *given)


def spot_order(chips):
    at = lax.axis_index("wide")
    chip, core = at >> 1, at & 1
    return [
        2 * lax.rem(chip + s, chips) + (core if k == 0 else 1 - core) for s in range(chips) for k in range(2)
    ]


def layer(near, far, weight, bias, cotangent, cols, chips):
    rows, hidden = cotangent.shape
    near_cols = near[0].shape[1]
    step = 2 * BLK if rows % (2 * BLK) == 0 else BLK

    def body(*refs):
        near_refs = refs[: len(near)]
        far_refs = refs[len(near) : len(near) + len(far)]
        weight_ref, bias_ref, cot_ref = refs[len(near) + len(far) : len(near) + len(far) + 3]
        act_ref, near_out, far_out, near_mix, far_mix, delta_ref, ordered = refs[
            len(near) + len(far) + 3 :
        ]
        for part, owner in enumerate(spot_order(chips)):
            low = pl.multiple_of(owner * cols, cols)
            ordered[part * cols : (part + 1) * cols, :] = weight_ref[pl.ds(low, cols), :]
        for low in range(0, rows, step):
            now = slice(low, low + step)
            mixed = []
            for group, out in ((near_refs, near_mix), (far_refs, far_mix)):
                value = group[0][now, :].astype(F32)
                for ref in group[1:]:
                    value = value + ref[now, :].astype(F32)
                mixed.append(value.astype(BF16))
                out[now, :] = mixed[-1]
            pre = jnp.dot(mixed[0], ordered[:near_cols, :], preferred_element_type=F32)
            pre = pre + jnp.dot(mixed[1], ordered[near_cols:, :], preferred_element_type=F32)
            pre = pre + bias_ref[...].astype(F32)
            square = pre * pre
            bend = jnp.tanh(ROOT * pre * (1.0 + CUBIC * square))
            half = 0.5 * (1.0 + bend)
            act_ref[now, :] = (pre * half).astype(BF16)
            slope = half + 0.5 * ROOT * pre * (1.0 - bend * bend) * (1.0 + 3.0 * CUBIC * square)
            delta = (cot_ref[now, :].astype(F32) * slope).astype(BF16)
            delta_ref[now, :] = delta
            turned = lax.dot_general(
                ordered[...], delta, (((1,), (1,)), ((), ())), preferred_element_type=F32
            ).astype(BF16)
            near_out[:, now] = turned[:near_cols, :]
            far_out[:, now] = turned[near_cols:, :]

    return call(
        body,
        "layer",
        [
            jax.ShapeDtypeStruct((rows, hidden), BF16),
            jax.ShapeDtypeStruct((near_cols, rows), BF16),
            jax.ShapeDtypeStruct((hidden - near_cols, rows), BF16),
            jax.ShapeDtypeStruct((rows, near_cols), BF16),
            jax.ShapeDtypeStruct((rows, hidden - near_cols), BF16),
            jax.ShapeDtypeStruct((rows, hidden), BF16),
        ],
        [VMEM_SPEC] * (len(near) + len(far) + 3),
        [pltpu.VMEM((hidden, hidden), BF16)],
        4 * rows * hidden * hidden,
        10 * rows * hidden,
    )(*near, *far, weight, bias, cotangent)


def weight_parts(near_mix, far_mix, delta, cols, chips):
    rows, near_cols = near_mix.shape
    hidden = delta.shape[1]
    lines = cols + 8

    def body(near_ref, far_ref, delta_ref, grad_ref):
        tail = jnp.broadcast_to(
            jnp.sum(delta_ref[...].astype(F32), axis=0, keepdims=True), (8, hidden)
        )
        grads = [
            lax.dot_general(
                ref[...], delta_ref[...], (((0,), (0,)), ((), ())), preferred_element_type=F32
            )
            for ref in (near_ref, far_ref)
        ]
        for part in range(2 * chips):
            source = grads[0] if part < 2 else grads[1]
            low = part * cols - (0 if part < 2 else near_cols)
            grad_ref[part % 2, part // 2, :cols, :] = source[low : low + cols, :]
            grad_ref[part % 2, part // 2, cols:, :] = tail

    return call(
        body,
        "weight_parts",
        [jax.ShapeDtypeStruct((2, chips, lines, hidden), F32)],
        [VMEM_SPEC] * 3,
        [],
        2 * rows * hidden * hidden,
        6 * rows * hidden,
    )(near_mix, far_mix, delta)[0]


def weight_sums(way, pieces, top, lines, packed, hidden):
    n_rows = lax.axis_size("rows")
    width = pieces[0].shape[1] // hidden

    def body(*refs):
        out, held = refs[-2:]
        places = places_of(way, False)
        count = len(places) // len(pieces)
        for i, (place, there) in enumerate(places):
            ref = refs[i // count]
            low = (i % count) * (ref.shape[0] // count) + top

            def take(ref=ref, low=low, place=place):
                for k in range(width):
                    rows = min(packed, lines - k * packed)
                    if rows > 0:
                        part = ref[low : low + packed, k * hidden : (k + 1) * hidden].astype(F32)
                        held[place, k * packed : k * packed + rows, :] = part[:rows]

            if there is True:
                take()
            else:
                pl.when(there)(take)
        value = held[0]
        for r in range(1, n_rows):
            value = value + held[r]
        out[...] = value

    return call(
        body,
        "weight_sums",
        [jax.ShapeDtypeStruct((lines, hidden), F32)],
        [VMEM_SPEC] * len(pieces),
        [pltpu.VMEM((n_rows, lines, hidden), F32)],
        0,
        8 * lines * hidden,
    )(*pieces)[0]


def assemble(mine, other, cols, chips):
    hidden = mine[0].shape[1]

    def body(*refs):
        out, bias_out = refs[-2:]
        for part, owner in enumerate(spot_order(chips)):
            low = pl.multiple_of(owner * cols, cols)
            out[pl.ds(low, cols), :] = refs[(part % 2) * chips + part // 2][:cols, :]
        bias_out[...] = refs[0][cols : cols + 1, :]

    return call(
        body,
        "assemble",
        [
            jax.ShapeDtypeStruct((2 * chips * cols, hidden), F32),
            jax.ShapeDtypeStruct((1, hidden), F32),
        ],
        [VMEM_SPEC] * (2 * chips),
        [],
        0,
        8 * chips * cols * hidden,
    )(*mine, *other)


def per_device(features, tile_weights, tile_source, tile_dest, tile_count, weight, bias, cotangent):
    cols, width = features.shape
    sources = width // BLK
    slots = tile_weights.shape[0]
    hidden = weight.shape[0]
    wide = lax.axis_size("wide")
    chips = wide // 2
    n_rows = lax.axis_size("rows")
    chunk = sources // wide
    near_cols = 2 * cols
    lines = cols + 8
    tile_bits, source_bits = bits_of(slots), bits_of(sources)

    at = lax.axis_index("wide")
    chip, core = at >> 1, at & 1

    def swap_cores(value):
        return lax.ppermute(value, "wide", [(i, i ^ 1) for i in range(wide)])

    def from_chip(value, shift):
        pairs = [(2 * ((i + shift) % chips) + k, 2 * i + k) for i in range(chips) for k in range(2)]
        return lax.ppermute(value, "wide", pairs)

    def along(value, pairs):
        return lax.ppermute(value, "rows", pairs)

    def around(value, shift):
        return along(value, [(i, (i + shift) % n_rows) for i in range(n_rows)])

    beside, across_pairs = [(0, 1), (1, 0), (2, 3), (3, 2)], [(0, 2), (1, 3), (2, 0), (3, 1)]

    def known(way):
        return way if n_rows == 4 or way == "all" else "direct"

    def scattered(way, first, blocks):
        outs = aggregate(
            meta, tile_weights, parts, first, n_rows * blocks, blocks, tile_bits, source_bits, way
        )
        if way == "direct":
            return [outs[0]] + [around(outs[s], s) for s in range(1, n_rows)]
        own, to_far, to_next, to_skip = outs
        passed = along(to_far, beside)
        got_next = along(to_next, beside)
        merged = (to_skip.astype(F32) + passed.astype(F32)).astype(BF16)
        got_skip = along(merged, across_pairs)
        return [own, got_next, got_skip]

    def gathered(way, value):
        if way == "all":
            return [lax.all_gather(value, "rows", axis=0, tiled=True)]
        if way == "direct":
            return [value] + [around(value, s) for s in range(1, n_rows)]
        got_skip = along(value, across_pairs)
        got_next = along(value, beside)
        return [value, got_skip, got_next, along(got_skip, beside)]

    parts = [features, swap_cores(features)]

    def split(value, size):
        whole = ((value.astype(F32) + 0.5) * (1.0 / size)).astype(jnp.int32)
        return whole, value - whole * size

    slot = jnp.arange(slots, dtype=jnp.int32)
    owner, within = split(tile_dest, sources)
    holder, nth = split(within, chunk)
    away = (holder >> 1) - chip
    away = jnp.where(away < 0, away + chips, away)
    far_blocks = (chips - 1) * chunk
    first_far = n_rows * chunk
    index = jnp.where(
        away == 0, owner * chunk + nth, first_far + owner * far_blocks + (away - 1) * chunk + nth
    )
    ours = (slot < tile_count[0]) & ((holder & 1) == core)
    high = source_bits + tile_bits
    meta = jnp.where(ours, (index << high) | (tile_source << tile_bits) | slot, -1)

    far_terms = scattered(known(RS_FAR), first_far, far_blocks)
    near = scattered(known(RS_NEAR), 0, chunk)
    passing = far_terms[0]
    for term in far_terms[1:]:
        passing = passing + term.astype(F32)
    passing = passing.astype(BF16).reshape(chips - 1, chunk * BLK, near_cols)
    far = [from_chip(passing[chips - s - 1], s) for s in range(1, chips)]
    far = far[0] if chips == 2 else jnp.concatenate(far, axis=1)

    activation, near_prop, far_prop, near_mix, far_mix, delta = layer(
        near, [far], weight, bias.reshape(1, hidden), cotangent, cols, chips
    )

    far_prop = far_prop.reshape(chips - 1, near_cols, chunk * BLK)
    coming = [from_chip(far_prop[chips - s - 1], s) for s in range(1, chips)]
    coming = coming[0] if chips == 2 else jnp.concatenate(coming, axis=1)
    near_all = gathered(known(AG_NEAR), near_prop)

    grads = weight_parts(near_mix, far_mix, delta, cols, chips)
    part = grads[0] + swap_cores(grads[1])
    quarter = part[0]
    for s in range(1, chips):
        quarter = quarter + from_chip(part[chips - s], s)
    across = coming.shape[1] // hidden
    packed = -(-lines // across)
    extra = jnp.pad(quarter.astype(BF16), ((0, across * packed - lines), (0, 0)))
    extra = jnp.concatenate([extra[k * packed : (k + 1) * packed] for k in range(across)], axis=1)
    spare = -(-packed // 16) * 16
    extra = jnp.pad(extra, ((0, spare - packed), (0, 0)))
    payload = jnp.concatenate([coming, extra], axis=0)
    if TIE == 1:
        payload = lax.optimization_barrier((payload, near_all[1]))[0]
    elif TIE == 2:
        payload = lax.optimization_barrier((payload, near_all[1:3]))[0]
    elif TIE == 3:
        payload = lax.optimization_barrier((payload, near_all[1:4]))[0]
    far_all = gathered(known(AG_FAR), payload)

    keep, send = spread_back(
        meta, tile_weights,
        [(chunk, known(AG_NEAR), near_all), (far_blocks, known(AG_FAR), far_all)],
        near_cols, sources, tile_bits, source_bits, cols,
    )
    grad_features = (keep + swap_cores(send).astype(F32)).astype(BF16)

    quarter = weight_sums(known(AG_FAR), far_all, near_cols, lines, packed, hidden)
    half = [quarter] + [from_chip(quarter, s) for s in range(1, chips)]
    other_half = swap_cores(jnp.stack(half))
    grad_weight, grad_bias = assemble(half, [other_half[s] for s in range(chips)], cols, chips)
    return (activation, grad_features, grad_weight, grad_bias.reshape(hidden))


def solution(mesh):
    in_specs = (
        P("wide", ("groups", "rows")),
        P(("groups", "rows"), None, None),
        P(("groups", "rows")),
        P(("groups", "rows")),
        P(("groups", "rows")),
        P(),
        P(),
        P(("groups", "rows", "wide"), None),
    )
    out_specs = (
        P(("groups", "rows", "wide"), None),
        P("wide", ("groups", "rows")),
        P("groups", None),
        P("groups"),
    )
    return jax.shard_map(
        per_device, mesh=mesh, in_specs=in_specs, out_specs=out_specs, check_vma=False
    )
```

time: 135 us -> 91.9 us (0.68)
  starting transfers between devices: 47.4 us -> 18 us
  waiting for transfers between devices: 56.7 us -> 31.5 us
  blocking collectives: 0 us -> 23 us
  Pallas kernels: 24 us -> 13.6 us
    ppermute x18 -> x9, starting transfers between devices: 40.2 us -> 11.1 us  [along(): return lax.ppermute(value, 'rows', pairs)]
    all_gather x0 -> x1, blocking collectives: none -> 23 us  [gathered(): return [lax.all_gather(value, 'rows', axis=0, tiled=True)]]
    ppermute x4, waiting for transfers between devices: 15.7 us -> 0.01 us  [from_chip(): return lax.ppermute(value, 'wide', pairs)]
    ppermute x18 -> x9, waiting for transfers between devices: 39.8 us -> 28.7 us  [along(): return lax.ppermute(value, 'rows', pairs)]
    pallas_call x4 -> x5, Pallas kernels: 20.1 us -> 10.8 us  [the longest x2 7.01 us: aggregate(): call(body, 'aggregate', shapes, [SMEM_SPEC, ANY_SPEC, ANY_SPEC] + [VMEM_S...]
    ppermute x6 -> x4, waiting for transfers between devices: 1.18 us -> 2.75 us  [swap_cores(): return lax.ppermute(value, 'wide', [(i, i ^ 1) for i in range(wide)])]
  transfers between devices with their start and end apart: 28 -> 17, of which waited for: 8 -> 7; matrix products, arithmetic and copies ran while one was open for 2% -> 1% of each run, Pallas kernels for 16% -> 9%
where the time goes in v2:
time: 91.9 us; the launch traced here: 90.4 us
  waiting for transfers between devices  31.5 us (34%)
  blocking collectives  23 us (25%)
  starting transfers between devices  18 us (20%)
  Pallas kernels  13.6 us (15%)
  other arithmetic  1.87 us (2%)
  between operations  1.45 us (2%)
  local copies, waits for them, and re-layouts  1.04 us (1%)
    ppermute x9, waiting for transfers between devices, along(): return lax.ppermute(value, 'rows', pairs)  28.7 us
    all_gather x1, blocking collectives, gathered(): return [lax.all_gather(value, 'rows', axis=0, tiled=True)]  23 us
    ppermute x9, starting transfers between devices, along(): return lax.ppermute(value, 'rows', pairs)  11.1 us
    pallas_call x2, Pallas kernels, aggregate(): call(body, 'aggregate', shapes, [SMEM_SPEC, ANY_SPEC, ANY_SPEC] + [VMEM_S...  7.01 us
    ppermute x4, starting transfers between devices, from_chip(): return lax.ppermute(value, 'wide', pairs)  5.76 us
    pallas_call x1, Pallas kernels, spread_back(): call(body, 'spread_back', [jax.ShapeDtypeStruct((cols, sources * BLK), F3...  3.48 us
    ppermute x4, waiting for transfers between devices, swap_cores(): return lax.ppermute(value, 'wide', [(i, i ^ 1) for i in range(wide)])  2.75 us
    pallas_call x1, Pallas kernels, layer(): call(body, 'layer', [jax.ShapeDtypeStruct((rows, hidden), BF16), jax.Shap...  2.05 us
  transfers between devices with their start and end apart: 17, of which 7 were waited for; matrix products, arithmetic and copies ran while one was open for 1% of the time, Pallas kernels for 9%

profile of v2, /device:TPU:0, one launch (start us, length us, event | category | flops | bytes accessed | tf_op | source)
XLA Modules:
  0.0 90.4 jit_solution(5826264803040289353)
XLA Ops:
  0.6 0.5 collective-permute-start
  1.8 0.8 and_select_fusion.meta_ref
  2.6 0.1 collective-permute-done.refs_0_
  2.7 0.0 copy-start
  2.7 1.0 %copy-done = bf16[64,3072]{1,0:T(8,128)(2,1)S(1)} copy-done((bf16[64,3072]{1,0:T(8,128)(2,1)S(1)}, bf16[64,3072]{1,0:T(8,128)(2,1)}, u32[]{:S(2)}) %copy-start) | copy-done | bytes 393240
  3.7 0.0 copy-start.3
  3.7 0.0 copy-start.1
  3.7 0.0 copy-start.2
  3.7 3.5 %aggregate.3 = (f32[768,128]{1,0:T(8,128)S(1)}, bf16[768,128]{1,0:T(8,128)(2,1)S(1)}, bf16[768,128]{1,0:T(8,128)(2,1)S(1)}, bf16[768,128]{1,0:T(8,128)(2,1)S(1)}) custom-call(s32[240]{0:T(256)S(1)} %and_select_fusion.meta_ref, bf16[240,128,128]{2,1,0:T(8,128)(2,1)} %tiles_ref.5, bf16[64,3072]{1,0:T(8,128)(2,1)S(1)} %copy-done, ...), custom_call_target="tpu_custom_call" | custom-call | flops 503316480 | bytes 3932160 | tf_op jit(solution)/shard_map/aggregate/pallas_call | solution.py:169
  7.2 4.0 %collective-permute-start.5 = (bf16[768,128]{1,0:T(8,128)(2,1)S(1)}, bf16[768,128]{1,0:T(8,128)(2,1)S(1)}, u32[]{:S(2)}, u32[]{:S(2)}) collective-permute-start(bf16[768,128]{1,0:T(8,128)(2,1)S(1)} %get-tuple-element.29), channel_id=1, source_target_pairs={{0,1},{1,0},{2,3},{3,2},{4,5},{5,4},{6,7},{7,6},{8,9},{9,8},{10,11... | collective-permute-start | bytes 589832 | tf_op jit(solution)/shard_map/ppermute | solution.py:440
  11.2 3.5 %aggregate.2 = (f32[768,128]{1,0:T(8,128)S(1)}, bf16[768,128]{1,0:T(8,128)(2,1)S(1)}, bf16[768,128]{1,0:T(8,128)(2,1)S(1)}, bf16[768,128]{1,0:T(8,128)(2,1)S(1)}) custom-call(s32[240]{0:T(256)S(1)} %and_select_fusion.meta_ref, bf16[240,128,128]{2,1,0:T(8,128)(2,1)} %tiles_ref.5, bf16[64,3072]{1,0:T(8,128)(2,1)S(1)} %copy-done, ...), custom_call_target="tpu_custom_call" | custom-call | flops 503316480 | bytes 3932160 | tf_op jit(solution)/shard_map/aggregate/pallas_call | solution.py:169
  14.8 1.1 %collective-permute-start.1 = (bf16[768,128]{1,0:T(8,128)(2,1)S(1)}, bf16[768,128]{1,0:T(8,128)(2,1)S(1)}, u32[]{:S(2)}, u32[]{:S(2)}) collective-permute-start(bf16[768,128]{1,0:T(8,128)(2,1)S(1)} %get-tuple-element.23), channel_id=1, source_target_pairs={{0,1},{1,0},{2,3},{3,2},{4,5},{5,4},{6,7},{7,6},{8,9},{9,8},{10,11... | collective-permute-start | bytes 589832 | tf_op jit(solution)/shard_map/ppermute | solution.py:440
  15.9 1.0 %collective-permute-start.2 = (bf16[768,128]{1,0:T(8,128)(2,1)S(1)}, bf16[768,128]{1,0:T(8,128)(2,1)S(1)}, u32[]{:S(2)}, u32[]{:S(2)}) collective-permute-start(bf16[768,128]{1,0:T(8,128)(2,1)S(1)} %get-tuple-element.25), channel_id=1, source_target_pairs={{0,1},{1,0},{2,3},{3,2},{4,5},{5,4},{6,7},{7,6},{8,9},{9,8},{10,11... | collective-permute-start | bytes 589832 | tf_op jit(solution)/shard_map/ppermute | solution.py:440
  16.8 1.0 %collective-permute-start.4 = (bf16[768,128]{1,0:T(8,128)(2,1)S(1)}, bf16[768,128]{1,0:T(8,128)(2,1)S(1)}, u32[]{:S(2)}, u32[]{:S(2)}) collective-permute-start(bf16[768,128]{1,0:T(8,128)(2,1)S(1)} %get-tuple-element.27), channel_id=1, source_target_pairs={{0,1},{1,0},{2,3},{3,2},{4,5},{5,4},{6,7},{7,6},{8,9},{9,8},{10,11... | collective-permute-start | bytes 589832 | tf_op jit(solution)/shard_map/ppermute | solution.py:440
  17.9 0.0 collective-permute-done.5
  17.9 0.1 add_convert_fusion.2
  17.9 2.7 %collective-permute-start.6 = (bf16[768,128]{1,0:T(8,128)(2,1)S(1)}, bf16[768,128]{1,0:T(8,128)(2,1)S(1)}, u32[]{:S(2)}, u32[]{:S(2)}) collective-permute-start(bf16[768,128]{1,0:T(8,128)(2,1)S(1)} %add_convert_fusion.2), channel_id=1, source_target_pairs={{0,2},{1,3},{2,0},{3,1},{4,6},{5,7},{6,4},{7,5},{8,10},{9,11},{10,... | collective-permute-start | bytes 589832 | tf_op jit(solution)/shard_map/ppermute | solution.py:440
  20.6 10.4 %collective-permute-done.2 = bf16[768,128]{1,0:T(8,128)(2,1)S(1)} collective-permute-done((bf16[768,128]{1,0:T(8,128)(2,1)S(1)}, bf16[768,128]{1,0:T(8,128)(2,1)S(1)}, u32[]{:S(2)}, u32[]{:S(2)}) %collective-permute-start.2) | collective-permute-done | bytes 196640 | tf_op jit(solution)/shard_map/ppermute | solution.py:440
  31.0 0.1 add_convert_fusion.3
  31.1 1.2 %collective-permute-start.3 = (bf16[768,128]{1,0:T(8,128)(2,1)S(1)}, bf16[768,128]{1,0:T(8,128)(2,1)S(1)}, u32[]{:S(2)}, u32[]{:S(2)}) collective-permute-start(bf16[768,128]{1,0:T(8,128)(2,1)S(1)} %add_convert_fusion.3), channel_id=1, source_target_pairs={{0,2},{1,3},{2,0},{3,1},{4,6},{5,7},{6,4},{7,5},{8,10},{9,11},{10,... | collective-permute-start | bytes 589832 | tf_op jit(solution)/shard_map/ppermute | solution.py:440
  32.3 2.1 %collective-permute-done.4 = bf16[768,128]{1,0:T(8,128)(2,1)S(1)} collective-permute-done((bf16[768,128]{1,0:T(8,128)(2,1)S(1)}, bf16[768,128]{1,0:T(8,128)(2,1)S(1)}, u32[]{:S(2)}, u32[]{:S(2)}) %collective-permute-start.4) | collective-permute-done | bytes 196640 | tf_op jit(solution)/shard_map/ppermute | solution.py:440
  34.4 0.0 collective-permute-done.6
  34.4 0.1 add_convert_fusion.1
  34.5 1.8 %collective-permute-start.7 = (bf16[768,128]{1,0:T(8,128)(2,1)S(1)}, bf16[768,128]{1,0:T(8,128)(2,1)S(1)}, u32[]{:S(2)}, u32[]{:S(2)}) collective-permute-start(bf16[768,128]{1,0:T(8,128)(2,1)S(1)} %add_convert_fusion.1), channel_id=1, source_target_pairs={{8,0},{12,4},{0,8},{4,12},{9,1},{13,5},{1,9},{5,13},{10,2},{14,6},... | collective-permute-start | bytes 589832 | tf_op jit(solution)/shard_map/ppermute | solution.py:437
  36.2 0.0 copy-done.3
  36.3 0.0 collective-permute-done.1.refs_1_
  36.3 8.6 %collective-permute-done.3.refs_2_ = bf16[768,128]{1,0:T(8,128)(2,1)S(1)} collective-permute-done((bf16[768,128]{1,0:T(8,128)(2,1)S(1)}, bf16[768,128]{1,0:T(8,128)(2,1)S(1)}, u32[]{:S(2)}, u32[]{:S(2)}) %collective-permute-start.3) | collective-permute-done | bytes 196640 | tf_op jit(solution)/shard_map/ppermute | solution.py:440
  44.8 0.0 collective-permute-done.7.refs_3_
  44.8 0.0 copy-done.1
  44.8 0.0 copy-done.2
  44.8 2.1 %layer.1 = (bf16[768,256]{1,0:T(8,128)(2,1)}, bf16[128,768]{1,0:T(8,128)(2,1)S(1)}, bf16[128,768]{1,0:T(8,128)(2,1)S(1)}, bf16[768,128]{1,0:T(8,128)(2,1)S(1)}, ...) custom-call(f32[768,128]{1,0:T(8,128)S(1)} %get-tuple-element.22.refs_0_, ...), custom_call_target="tpu_custom_call" | custom-call | flops 201326592 | bytes 1966080 | tf_op jit(solution)/shard_map/layer/pallas_call | solution.py:303
  46.9 0.3 weight_parts.1
  47.2 0.1 collective-permute-start.12
  47.3 0.1 collective-permute-start.8
  47.4 1.3 %collective-permute-done.12 = f32[2,72,256]{2,1,0:T(8,128)S(1)} collective-permute-done((f32[2,72,256]{2,1,0:T(8,128)S(1)}, f32[2,72,256]{2,1,0:T(8,128)S(1)}, u32[]{:S(2)}, u32[]{:S(2)}) %collective-permute-start.12) | collective-permute-done | bytes 147488 | tf_op jit(solution)/shard_map/ppermute | solution.py:433
  48.7 2.0 %collective-permute-start.13 = (f32[72,256]{1,0:T(8,128)S(1)}, f32[72,256]{1,0:T(8,128)S(1)}, u32[]{:S(2)}, u32[]{:S(2)}) collective-permute-start(f32[72,256]{1,0:T(8,128)S(1)} %slice_bitcast_fusion.4), channel_id=1, source_target_pairs={{8,0},{12,4},{0,8},{4,12},{9,1},{13,5},{1,9},{5,13},{10,2},{14,6},... | collective-permute-start | bytes 221192 | tf_op jit(solution)/shard_map/ppermute | solution.py:437
  50.7 0.0 collective-permute-start.9
  50.7 0.2 collective-permute-start.11
  50.9 7.6 %collective-permute-done.8.refs_1_ = bf16[128,768]{1,0:T(8,128)(2,1)S(1)} collective-permute-done((bf16[128,768]{1,0:T(8,128)(2,1)S(1)}, bf16[128,768]{1,0:T(8,128)(2,1)S(1)}, u32[]{:S(2)}, u32[]{:S(2)}) %collective-permute-start.8) | collective-permute-done | bytes 196640 | tf_op jit(solution)/shard_map/ppermute | solution.py:440
  58.5 0.0 collective-permute-start.10
  58.5 0.0 collective-permute-done.13
  58.5 0.0 collective-permute-done.11
  58.6 23.0 %all_gather.3.refs_4_.refs_0_ = bf16[640,768]{1,0:T(8,128)(2,1)S(1)} all-gather(bf16[160,768]{1,0:T(8,128)(2,1)S(1)} %pad_maximum_fusion), channel_id=1, replica_groups=mesh['groups'=2,'wide'=4,'rows'=4] {'rows'}, dimensions={0}, use_global_device_ids=true | all-gather | bytes 1228800 | tf_op jit(solution)/shard_map/all_gather | solution.py:465
  81.6 1.8 %collective-permute-start.15 = (f32[72,256]{1,0:T(8,128)S(1)}, f32[72,256]{1,0:T(8,128)S(1)}, u32[]{:S(2)}, u32[]{:S(2)}) collective-permute-start(f32[72,256]{1,0:T(8,128)S(1)} %weight_sums.1.refs_0_), channel_id=1, source_target_pairs={{8,0},{12,4},{0,8},{4,12},{9,1},{13,5},{1,9},{5,13},{10,2},{14,6},... | collective-permute-start | bytes 221192 | tf_op jit(solution)/shard_map/ppermute | solution.py:437
  83.4 0.0 collective-permute-done.9.refs_2_
  83.4 0.0 collective-permute-done.10.refs_3_
  83.4 3.5 %spread_back.1 = (f32[64,3072]{1,0:T(8,128)S(1)}, bf16[64,3072]{1,0:T(8,128)(2,1)S(1)}) custom-call(s32[240]{0:T(256)S(1)} %and_select_fusion.meta_ref, bf16[240,128,128]{2,1,0:T(8,128)(2,1)} %tiles_ref.5, bf16[128,768]{1,0:T(8,128)(2,1)S(1)} %get-tuple-element.31.refs_0_, bf16[128,768]{1,0:T(8,128)(2,1)S(1)} %collective-permute-done.8.refs_1_, ...), custom_call_target="tpu_custom_call" | custom-call | flops 503316480 | bytes 3932160 | tf_op jit(solution)/shard_map/spread_back/pallas_call | solution.py:237
  86.8 0.1 collective-permute-start.14
  86.9 0.0 collective-permute-done.15.refs_1_
  87.0 0.5 collective-permute-start.16
  87.5 1.3 %collective-permute-done.16 = f32[2,72,256]{2,1,0:T(8,128)S(1)} collective-permute-done((f32[2,72,256]{2,1,0:T(8,128)S(1)}, f32[2,72,256]{2,1,0:T(8,128)S(1)}, u32[]{:S(2)}, u32[]{:S(2)}) %collective-permute-start.16) | collective-permute-done | bytes 147488 | tf_op jit(solution)/shard_map/ppermute | solution.py:433
  88.9 0.7 assemble.1
  89.6 0.0 collective-permute-done.14
  89.6 0.8 add_convert_fusion
  (11 shorter events, 0.1 us)
Async XLA Ops:
  0.6 2.1 %collective-permute-start = (bf16[64,3072]{1,0:T(8,128)(2,1)}, bf16[64,3072]{1,0:T(8,128)(2,1)S(1)}, u32[]{:S(2)}, u32[]{:S(2)}) collective-permute-start(bf16[64,3072]{1,0:T(8,128)(2,1)} %own_ref.3), channel_id=1, source_target_pairs={{0,4},{4,0},{8,12},{12,8},{1,5},{5,1},{9,13},{13,9},{2,6},{6,2},{1... | collective-permute-start | bytes 1179656 | tf_op jit(solution)/shard_map/ppermute | solution.py:433
  2.7 1.0 %copy-start = (bf16[64,3072]{1,0:T(8,128)(2,1)S(1)}, bf16[64,3072]{1,0:T(8,128)(2,1)}, u32[]{:S(2)}) copy-start(bf16[64,3072]{1,0:T(8,128)(2,1)} %own_ref.3) | copy-start | bytes 1179652
  3.7 32.5 %copy-start.3 = (bf16[256]{0:T(256)(128)(2,1)S(1)}, bf16[256]{0:T(256)(128)(2,1)}, u32[]{:S(2)}) copy-start(bf16[256]{0:T(256)(128)(2,1)} %param.14) | copy-start | bytes 1540
  3.7 41.1 %copy-start.1 = (bf16[768,256]{1,0:T(8,128)(2,1)S(1)}, bf16[768,256]{1,0:T(8,128)(2,1)}, u32[]{:S(2)}) copy-start(bf16[768,256]{1,0:T(8,128)(2,1)} %refs_6_.1) | copy-start | bytes 1179652
  3.7 41.1 %copy-start.2 = (bf16[256,256]{1,0:T(8,128)(2,1)S(1)}, bf16[256,256]{1,0:T(8,128)(2,1)}, u32[]{:S(2)}) copy-start(bf16[256,256]{1,0:T(8,128)(2,1)} %refs_4_.1) | copy-start | bytes 393220
  7.2 10.7 %collective-permute-start.5 = (bf16[768,128]{1,0:T(8,128)(2,1)S(1)}, bf16[768,128]{1,0:T(8,128)(2,1)S(1)}, u32[]{:S(2)}, u32[]{:S(2)}) collective-permute-start(bf16[768,128]{1,0:T(8,128)(2,1)S(1)} %get-tuple-element.29), channel_id=1, source_target_pairs={{0,1},{1,0},{2,3},{3,2},{4,5},{5,4},{6,7},{7,6},{8,9},{9,8},{10,11... | collective-permute-start | bytes 589832 | tf_op jit(solution)/shard_map/ppermute | solution.py:440
  14.8 21.5 %collective-permute-start.1 = (bf16[768,128]{1,0:T(8,128)(2,1)S(1)}, bf16[768,128]{1,0:T(8,128)(2,1)S(1)}, u32[]{:S(2)}, u32[]{:S(2)}) collective-permute-start(bf16[768,128]{1,0:T(8,128)(2,1)S(1)} %get-tuple-element.23), channel_id=1, source_target_pairs={{0,1},{1,0},{2,3},{3,2},{4,5},{5,4},{6,7},{7,6},{8,9},{9,8},{10,11... | collective-permute-start | bytes 589832 | tf_op jit(solution)/shard_map/ppermute | solution.py:440
  15.9 15.2 %collective-permute-start.2 = (bf16[768,128]{1,0:T(8,128)(2,1)S(1)}, bf16[768,128]{1,0:T(8,128)(2,1)S(1)}, u32[]{:S(2)}, u32[]{:S(2)}) collective-permute-start(bf16[768,128]{1,0:T(8,128)(2,1)S(1)} %get-tuple-element.25), channel_id=1, source_target_pairs={{0,1},{1,0},{2,3},{3,2},{4,5},{5,4},{6,7},{7,6},{8,9},{9,8},{10,11... | collective-permute-start | bytes 589832 | tf_op jit(solution)/shard_map/ppermute | solution.py:440
  16.8 17.6 %collective-permute-start.4 = (bf16[768,128]{1,0:T(8,128)(2,1)S(1)}, bf16[768,128]{1,0:T(8,128)(2,1)S(1)}, u32[]{:S(2)}, u32[]{:S(2)}) collective-permute-start(bf16[768,128]{1,0:T(8,128)(2,1)S(1)} %get-tuple-element.27), channel_id=1, source_target_pairs={{0,1},{1,0},{2,3},{3,2},{4,5},{5,4},{6,7},{7,6},{8,9},{9,8},{10,11... | collective-permute-start | bytes 589832 | tf_op jit(solution)/shard_map/ppermute | solution.py:440
  17.9 16.5 %collective-permute-start.6 = (bf16[768,128]{1,0:T(8,128)(2,1)S(1)}, bf16[768,128]{1,0:T(8,128)(2,1)S(1)}, u32[]{:S(2)}, u32[]{:S(2)}) collective-permute-start(bf16[768,128]{1,0:T(8,128)(2,1)S(1)} %add_convert_fusion.2), channel_id=1, source_target_pairs={{0,2},{1,3},{2,0},{3,1},{4,6},{5,7},{6,4},{7,5},{8,10},{9,11},{10,... | collective-permute-start | bytes 589832 | tf_op jit(solution)/shard_map/ppermute | solution.py:440
  31.1 13.7 %collective-permute-start.3 = (bf16[768,128]{1,0:T(8,128)(2,1)S(1)}, bf16[768,128]{1,0:T(8,128)(2,1)S(1)}, u32[]{:S(2)}, u32[]{:S(2)}) collective-permute-start(bf16[768,128]{1,0:T(8,128)(2,1)S(1)} %add_convert_fusion.3), channel_id=1, source_target_pairs={{0,2},{1,3},{2,0},{3,1},{4,6},{5,7},{6,4},{7,5},{8,10},{9,11},{10,... | collective-permute-start | bytes 589832 | tf_op jit(solution)/shard_map/ppermute | solution.py:440
  34.5 10.3 %collective-permute-start.7 = (bf16[768,128]{1,0:T(8,128)(2,1)S(1)}, bf16[768,128]{1,0:T(8,128)(2,1)S(1)}, u32[]{:S(2)}, u32[]{:S(2)}) collective-permute-start(bf16[768,128]{1,0:T(8,128)(2,1)S(1)} %add_convert_fusion.1), channel_id=1, source_target_pairs={{8,0},{12,4},{0,8},{4,12},{9,1},{13,5},{1,9},{5,13},{10,2},{14,6},... | collective-permute-start | bytes 589832 | tf_op jit(solution)/shard_map/ppermute | solution.py:437
  47.2 1.4 %collective-permute-start.12 = (f32[2,72,256]{2,1,0:T(8,128)S(1)}, f32[2,72,256]{2,1,0:T(8,128)S(1)}, u32[]{:S(2)}, u32[]{:S(2)}) collective-permute-start(f32[2,72,256]{2,1,0:T(8,128)S(1)} %slice_bitcast_fusion), channel_id=1, source_target_pairs={{0,4},{4,0},{8,12},{12,8},{1,5},{5,1},{9,13},{13,9},{2,6},{6,2},{1... | collective-permute-start | bytes 442376 | tf_op jit(solution)/shard_map/ppermute | solution.py:433
  47.3 11.2 %collective-permute-start.8 = (bf16[128,768]{1,0:T(8,128)(2,1)S(1)}, bf16[128,768]{1,0:T(8,128)(2,1)S(1)}, u32[]{:S(2)}, u32[]{:S(2)}) collective-permute-start(bf16[128,768]{1,0:T(8,128)(2,1)S(1)} %get-tuple-element.31.refs_0_), channel_id=1, source_target_pairs={{0,2},{1,3},{2,0},{3,1},{4,6},{5,7},{6,4},{7,5},{8,10},{9,11},{10,... | collective-permute-start | bytes 589832 | tf_op jit(solution)/shard_map/ppermute | solution.py:440
  48.7 9.8 %collective-permute-start.13 = (f32[72,256]{1,0:T(8,128)S(1)}, f32[72,256]{1,0:T(8,128)S(1)}, u32[]{:S(2)}, u32[]{:S(2)}) collective-permute-start(f32[72,256]{1,0:T(8,128)S(1)} %slice_bitcast_fusion.4), channel_id=1, source_target_pairs={{8,0},{12,4},{0,8},{4,12},{9,1},{13,5},{1,9},{5,13},{10,2},{14,6},... | collective-permute-start | bytes 221192 | tf_op jit(solution)/shard_map/ppermute | solution.py:437
  50.7 32.7 %collective-permute-start.9 = (bf16[128,768]{1,0:T(8,128)(2,1)S(1)}, bf16[128,768]{1,0:T(8,128)(2,1)S(1)}, u32[]{:S(2)}, u32[]{:S(2)}) collective-permute-start(bf16[128,768]{1,0:T(8,128)(2,1)S(1)} %get-tuple-element.31.refs_0_), channel_id=1, source_target_pairs={{0,1},{1,0},{2,3},{3,2},{4,5},{5,4},{6,7},{7,6},{8,9},{9,8},{10,11... | collective-permute-start | bytes 589832 | tf_op jit(solution)/shard_map/ppermute | solution.py:440
  50.7 7.8 %collective-permute-start.11 = (bf16[128,768]{1,0:T(8,128)(2,1)S(1)}, bf16[128,768]{1,0:T(8,128)(2,1)S(1)}, u32[]{:S(2)}, u32[]{:S(2)}) collective-permute-start(bf16[128,768]{1,0:T(8,128)(2,1)S(1)} %get-tuple-element.32), channel_id=1, source_target_pairs={{8,0},{12,4},{0,8},{4,12},{9,1},{13,5},{1,9},{5,13},{10,2},{14,6},... | collective-permute-start | bytes 589832 | tf_op jit(solution)/shard_map/ppermute | solution.py:437
  58.5 24.9 %collective-permute-start.10 = (bf16[128,768]{1,0:T(8,128)(2,1)S(1)}, bf16[128,768]{1,0:T(8,128)(2,1)S(1)}, u32[]{:S(2)}, u32[]{:S(2)}) collective-permute-start(bf16[128,768]{1,0:T(8,128)(2,1)S(1)} %collective-permute-done.8.refs_1_), channel_id=1, source_target_pairs={{0,1},{1,0},{2,3},{3,2},{4,5},{5,4},{6,7},{7,6},{8,9},{9,8},{10,11... | collective-permute-start | bytes 589832 | tf_op jit(solution)/shard_map/ppermute | solution.py:440
  81.6 5.4 %collective-permute-start.15 = (f32[72,256]{1,0:T(8,128)S(1)}, f32[72,256]{1,0:T(8,128)S(1)}, u32[]{:S(2)}, u32[]{:S(2)}) collective-permute-start(f32[72,256]{1,0:T(8,128)S(1)} %weight_sums.1.refs_0_), channel_id=1, source_target_pairs={{8,0},{12,4},{0,8},{4,12},{9,1},{13,5},{1,9},{5,13},{10,2},{14,6},... | collective-permute-start | bytes 221192 | tf_op jit(solution)/shard_map/ppermute | solution.py:437
  86.8 2.8 %collective-permute-start.14 = (bf16[64,3072]{1,0:T(8,128)(2,1)S(1)}, bf16[64,3072]{1,0:T(8,128)(2,1)S(1)}, u32[]{:S(2)}, u32[]{:S(2)}) collective-permute-start(bf16[64,3072]{1,0:T(8,128)(2,1)S(1)} %get-tuple-element.37), channel_id=1, source_target_pairs={{0,4},{4,0},{8,12},{12,8},{1,5},{5,1},{9,13},{13,9},{2,6},{6,2},{1... | collective-permute-start | bytes 1179656 | tf_op jit(solution)/shard_map/ppermute | solution.py:433
  87.0 1.9 %collective-permute-start.16 = (f32[2,72,256]{2,1,0:T(8,128)S(1)}, f32[2,72,256]{2,1,0:T(8,128)S(1)}, u32[]{:S(2)}, u32[]{:S(2)}) collective-permute-start(f32[2,72,256]{2,1,0:T(8,128)S(1)} %pad_maximum_fusion.1), channel_id=1, source_target_pairs={{0,4},{4,0},{8,12},{12,8},{1,5},{5,1},{9,13},{13,9},{2,6},{6,2},{1... | collective-permute-start | bytes 442376 | tf_op jit(solution)/shard_map/ppermute | solution.py:433

commit v3 on v2

--- a/solution.py
+++ b/solution.py
@@ -10,11 +10,13 @@
 
 BLK = 128
 GROUP = 16
-RS_FAR = "pair"
-RS_NEAR = "pair"
 AG_NEAR = "pair"
-AG_FAR = "all"
+AG_FAR = 'all'
 TIE = 0
+QTIE = 0
+COST = 1
+XG = False
+SPLIT = False
 RING = 4
 VMEM_BYTES = 48 * 1024 * 1024
 ROOT = math.sqrt(2.0 / math.pi)
@@ -24,7 +26,7 @@
 
 SMEM_SPEC = pl.BlockSpec(memory_space=pltpu.SMEM)
 VMEM_SPEC = pl.BlockSpec(memory_space=pltpu.VMEM)
-ANY_SPEC = pl.BlockSpec(memory_space=pl.ANY)
+HBM_SPEC = pl.BlockSpec(memory_space=pltpu.HBM)
 
 
 def bits_of(size):
@@ -40,7 +42,7 @@
         out_specs=jax.tree.map(lambda _: VMEM_SPEC, out_shape),
         scratch_shapes=scratch,
         compiler_params=pltpu.CompilerParams(vmem_limit_bytes=VMEM_BYTES),
-        cost_estimate=pl.CostEstimate(flops=flops, bytes_accessed=nbytes, transcendentals=0),
+        cost_estimate=pl.CostEstimate(flops=COST * flops, bytes_accessed=COST * nbytes, transcendentals=0),
     )
 
 
@@ -100,34 +102,29 @@
     ]
 
 
-def row_at(shift):
+def row_at(way, i):
     count = lax.axis_size("rows")
-    return lax.rem(lax.axis_index("rows") + (shift % count), count)
-
-
-def places_of(way, scatter):
-    count = lax.axis_size("rows")
+    row = lax.axis_index("rows")
     if way == "all":
-        return [(row, True) for row in range(count)]
+        return i
     if way == "direct":
-        return [(row_at(s if scatter else -s), True) for s in range(count)]
-    row = lax.axis_index("rows")
-    if scatter:
-        return [(row ^ i, True) for i in (0, 3, 1, 2)]
-    return [(row ^ i, True) for i in (0, 2, 1, 3)]
-
-
-def aggregate(meta, tiles, parts, first, dests, chunk, tile_bits, source_bits, way):
+        return lax.rem(row + (i % count), count)
+    return row ^ i
+
+
+def aggregate(meta, tiles, parts, owners, way, cuts, layout):
+    tile_bits, source_bits, nth_bits = layout
     columns = sum(part.shape[0] for part in parts)
     sources = parts[0].shape[1] // BLK
-    source_mask = (1 << source_bits) - 1
-    if way == "all":
-        shapes = [jax.ShapeDtypeStruct((dests * BLK, columns), BF16)]
-    else:
-        count = dests // chunk
-        shapes = [
-            jax.ShapeDtypeStruct((chunk * BLK, columns), F32 if i == 0 else BF16) for i in range(count)
-        ]
+    n_rows, per_row = lax.axis_size("rows"), cuts[-1]
+    dead = n_rows * per_row
+    pieces = list(zip(cuts[:-1], cuts[1:]))
+    shapes = [
+        jax.ShapeDtypeStruct(((high - low) * BLK, columns), F32 if i == 0 else BF16)
+        for i in owners
+        for low, high in pieces
+    ]
+    many = len(owners) == n_rows
 
     def body(meta_ref, tiles_ref, own_ref, *refs):
         part_refs = refs[: len(parts) - 1]
@@ -135,47 +132,57 @@
         own, own_sem, turned, total, picked, ring, sems = refs[len(parts) - 1 + len(shapes) :]
         fetch = pltpu.make_async_copy(own_ref, own, own_sem)
         fetch.start()
+        rows = [row_at(way, i) for i in owners]
 
         def prepare():
             fetch.wait()
-            total[...] = jnp.zeros_like(total)
+            if many:
+                total[...] = jnp.zeros_like(total)
+            else:
+                total[dead] = jnp.zeros_like(total[dead])
+                for row in rows:
+                    total[pl.ds(row * per_row, per_row)] = jnp.zeros((per_row, BLK, columns), F32)
             for s in range(sources):
                 now = slice(s * BLK, (s + 1) * BLK)
                 block = jnp.concatenate([own[:, now]] + [ref[:, now] for ref in part_refs], axis=0)
                 turned[s] = jnp.transpose(block)
 
         def multiply(entry, tile):
-            source = (jnp.maximum(entry, 0) >> tile_bits) & source_mask
+            source = (jnp.maximum(entry, 0) >> tile_bits) & ((1 << source_bits) - 1)
             return jnp.dot(tile[...], turned[source], preferred_element_type=F32)
 
         def add(entry, product):
-            dest = (entry >> (tile_bits + source_bits)) - first
-            total[jnp.where(entry < 0, dests, dest)] += product
+            rest = entry >> (tile_bits + source_bits)
+            dest = (rest >> nth_bits) * per_row + (rest & ((1 << nth_bits) - 1))
+            total[jnp.where(entry < 0, dead, dest)] += product
 
         def wanted(entry):
-            dest = entry >> (tile_bits + source_bits)
-            return (dest >= first) & (dest < first + dests)
+            if many:
+                return entry >= 0
+            owner = entry >> (tile_bits + source_bits + nth_bits)
+            found = owner == rows[0]
+            for row in rows[1:]:
+                found = found | (owner == row)
+            return found
 
         each_tile(
             meta_ref, wanted, picked, tiles_ref, ring, sems, tile_bits, prepare, multiply, add
         )
-        if way == "all":
-            outs[0][...] = total[:dests].reshape(outs[0].shape).astype(BF16)
-        else:
-            for out, (place, _) in zip(outs, places_of(way, True)):
-                out[...] = total[pl.ds(place * chunk, chunk)].reshape(out.shape).astype(out.dtype)
+        spots = [(row * per_row + low, high - low) for row in rows for low, high in pieces]
+        for out, (low, count) in zip(outs, spots):
+            out[...] = total[pl.ds(low, count)].reshape(out.shape).astype(out.dtype)
 
     slots = tiles.shape[0]
     return call(
         body,
         "aggregate",
         shapes,
-        [SMEM_SPEC, ANY_SPEC, ANY_SPEC] + [VMEM_SPEC] * (len(parts) - 1),
+        [SMEM_SPEC, HBM_SPEC, HBM_SPEC] + [VMEM_SPEC] * (len(parts) - 1),
         [
             pltpu.VMEM(parts[0].shape, BF16),
             pltpu.SemaphoreType.DMA,
             pltpu.VMEM((sources, BLK, columns), BF16),
-            pltpu.VMEM((dests + 1, BLK, columns), F32),
+            pltpu.VMEM((dead + 1, BLK, columns), F32),
         ]
         + ring_scratch(tiles.shape[0]),
         slots * BLK * BLK * columns,
@@ -183,73 +190,84 @@
     )(meta, tiles, *parts)
 
 
-def spread_back(meta, tiles, groups, columns, sources, tile_bits, source_bits, cols):
-    source_mask = (1 << source_bits) - 1
-    given = [piece for _, _, pieces in groups for piece in pieces]
-    sizes = [blocks * lax.axis_size("rows") for blocks, _, _ in groups]
-    spare = sum(sizes)
+def spread_back(meta, tiles, pieces, before, columns, sources, per_row, layout, cols, last):
+    tile_bits, source_bits, nth_bits = layout
+    given = []
+    for piece in pieces:
+        if not any(piece[0] is other for other in given):
+            given.append(piece[0])
+    extra = [] if before is None else [before]
+    spare = lax.axis_size("rows") * per_row
 
     def body(meta_ref, tiles_ref, *refs):
-        part_refs = refs[: len(given)]
-        keep, send, held, total, picked, ring, sems = refs[len(given) :]
+        rest = refs[len(given) + len(extra) :]
+        if last:
+            keep, send, held, total, picked, ring, sems = rest
+        else:
+            total, held, picked, ring, sems = rest
+        rows = [row_at(way, i) for _, _, way, i, _, _ in pieces]
 
         def prepare():
-            total[...] = jnp.zeros_like(total)
+            if before is None:
+                total[...] = jnp.zeros_like(total)
+            else:
+                total[...] = refs[len(given)][...]
             held[spare] = jnp.zeros_like(held[spare])
-            start, at = 0, 0
-            for (blocks, way, pieces), size in zip(groups, sizes):
-                places = places_of(way, False)
-                count = len(places) // len(pieces)
-                for i, (place, there) in enumerate(places):
-                    ref = part_refs[at + i // count]
-                    low = (i % count) * (ref.shape[0] // count)
-
-                    def take(ref=ref, low=low, place=place, blocks=blocks, start=start):
-                        for q in range(blocks):
-                            held[start + place * blocks + q] = ref[
-                                low : low + columns, q * BLK : (q + 1) * BLK
-                            ]
-
-                    if there is True:
-                        take()
-                    else:
-                        pl.when(there)(take)
-                at += len(pieces)
-                start += size
+            for (array, line, _, _, first, count), row in zip(pieces, rows):
+                ref = next(ref for ref, other in zip(refs, given) if other is array)
+                for q in range(count):
+                    held[row * per_row + first + q] = ref[
+                        line : line + columns, q * BLK : (q + 1) * BLK
+                    ]
+
+        def wanted(entry):
+            rest = entry >> (tile_bits + source_bits)
+            owner, nth = rest >> nth_bits, rest & ((1 << nth_bits) - 1)
+            found = owner < 0
+            for (_, _, _, _, first, count), row in zip(pieces, rows):
+                found = found | ((owner == row) & (nth >= first) & (nth < first + count))
+            return found & (entry >= 0)
 
         def multiply(entry, tile):
-            dest = jnp.where(entry < 0, spare, entry >> (tile_bits + source_bits))
+            rest = entry >> (tile_bits + source_bits)
+            dest = (rest >> nth_bits) * per_row + (rest & ((1 << nth_bits) - 1))
+            dest = jnp.where(entry < 0, spare, dest)
             return jnp.dot(held[dest], tile[...], preferred_element_type=F32)
 
         def add(entry, product):
-            source = (jnp.maximum(entry, 0) >> tile_bits) & source_mask
+            source = (jnp.maximum(entry, 0) >> tile_bits) & ((1 << source_bits) - 1)
             total[source] += product
 
         each_tile(
-            meta_ref, lambda entry: entry >= 0, picked, tiles_ref, ring, sems, tile_bits,
-            prepare, multiply, add,
+            meta_ref,
+            (lambda entry: entry >= 0) if last and before is None else wanted,
+            picked, tiles_ref, ring, sems, tile_bits, prepare, multiply, add,
         )
-        for s in range(sources):
-            keep[:, s * BLK : (s + 1) * BLK] = total[s, :cols, :]
-            send[:, s * BLK : (s + 1) * BLK] = total[s, cols:, :].astype(BF16)
+        if last:
+            for s in range(sources):
+                keep[:, s * BLK : (s + 1) * BLK] = total[s, :cols, :]
+                send[:, s * BLK : (s + 1) * BLK] = total[s, cols:, :].astype(BF16)
 
     slots = tiles.shape[0]
+    sums = (sources, columns, BLK)
+    if last:
+        outs = [
+            jax.ShapeDtypeStruct((cols, sources * BLK), F32),
+            jax.ShapeDtypeStruct((cols, sources * BLK), BF16),
+        ]
+    else:
+        outs = [jax.ShapeDtypeStruct(sums, F32)]
     return call(
         body,
         "spread_back",
-        [
-            jax.ShapeDtypeStruct((cols, sources * BLK), F32),
-            jax.ShapeDtypeStruct((cols, sources * BLK), BF16),
-        ],
-        [SMEM_SPEC, ANY_SPEC] + [VMEM_SPEC] * len(given),
-        [
-            pltpu.VMEM((spare + 1, columns, BLK), BF16),
-            pltpu.VMEM((sources, columns, BLK), F32),
-        ]
+        outs,
+        [SMEM_SPEC, HBM_SPEC] + [VMEM_SPEC] * (len(given) + len(extra)),
+        [pltpu.VMEM((spare + 1, columns, BLK), BF16)]
+        + ([pltpu.VMEM(sums, F32)] if last else [])
         + ring_scratch(tiles.shape[0]),
         slots * BLK * BLK * columns,
         slots * BLK * BLK,
-    )(meta, tiles, *given)
+    )(meta, tiles, *given, *extra)
 
 
 def spot_order(chips):
@@ -356,23 +374,15 @@
 
     def body(*refs):
         out, held = refs[-2:]
-        places = places_of(way, False)
-        count = len(places) // len(pieces)
-        for i, (place, there) in enumerate(places):
-            ref = refs[i // count]
-            low = (i % count) * (ref.shape[0] // count) + top
-
-            def take(ref=ref, low=low, place=place):
-                for k in range(width):
-                    rows = min(packed, lines - k * packed)
-                    if rows > 0:
-                        part = ref[low : low + packed, k * hidden : (k + 1) * hidden].astype(F32)
-                        held[place, k * packed : k * packed + rows, :] = part[:rows]
-
-            if there is True:
-                take()
-            else:
-                pl.when(there)(take)
+        for i in range(n_rows):
+            ref = refs[i // (n_rows // len(pieces))]
+            low = (i % (n_rows // len(pieces))) * (ref.shape[0] // (n_rows // len(pieces))) + top
+            place = row_at(way, i)
+            for k in range(width):
+                rows = min(packed, lines - k * packed)
+                if rows > 0:
+                    part = ref[low : low + packed, k * hidden : (k + 1) * hidden].astype(F32)
+                    held[place, k * packed : k * packed + rows, :] = part[:rows]
         value = held[0]
         for r in range(1, n_rows):
             value = value + held[r]
@@ -447,27 +457,17 @@
     def known(way):
         return way if n_rows == 4 or way == "all" else "direct"
 
-    def scattered(way, first, blocks):
-        outs = aggregate(
-            meta, tile_weights, parts, first, n_rows * blocks, blocks, tile_bits, source_bits, way
-        )
-        if way == "direct":
-            return [outs[0]] + [around(outs[s], s) for s in range(1, n_rows)]
-        own, to_far, to_next, to_skip = outs
-        passed = along(to_far, beside)
-        got_next = along(to_next, beside)
-        merged = (to_skip.astype(F32) + passed.astype(F32)).astype(BF16)
-        got_skip = along(merged, across_pairs)
-        return [own, got_next, got_skip]
-
     def gathered(way, value):
         if way == "all":
             return [lax.all_gather(value, "rows", axis=0, tiled=True)]
         if way == "direct":
-            return [value] + [around(value, s) for s in range(1, n_rows)]
+            return [value] + [around(value, -s) for s in range(1, n_rows)]
         got_skip = along(value, across_pairs)
         got_next = along(value, beside)
-        return [value, got_skip, got_next, along(got_skip, beside)]
+        return [value, got_next, got_skip, along(got_skip, beside)]
+
+    def tied(value, other):
+        return lax.optimization_barrier((value, other))[0]
 
     parts = [features, swap_cores(features)]
 
@@ -480,17 +480,44 @@
     holder, nth = split(within, chunk)
     away = (holder >> 1) - chip
     away = jnp.where(away < 0, away + chips, away)
-    far_blocks = (chips - 1) * chunk
-    first_far = n_rows * chunk
-    index = jnp.where(
-        away == 0, owner * chunk + nth, first_far + owner * far_blocks + (away - 1) * chunk + nth
-    )
+    per_row = chips * chunk
+    nth_bits = bits_of(per_row)
+    layout = (tile_bits, source_bits, nth_bits)
+    place = (owner << nth_bits) | (away * chunk + nth)
     ours = (slot < tile_count[0]) & ((holder & 1) == core)
-    high = source_bits + tile_bits
-    meta = jnp.where(ours, (index << high) | (tile_source << tile_bits) | slot, -1)
-
-    far_terms = scattered(known(RS_FAR), first_far, far_blocks)
-    near = scattered(known(RS_NEAR), 0, chunk)
+    meta = (place << (source_bits + tile_bits)) | (tile_source << tile_bits) | slot
+    meta = jnp.where(ours, meta, -1)
+
+    def partial_sums(owners, way, cuts):
+        return aggregate(meta, tile_weights, parts, owners, way, cuts, layout)
+
+    cuts = (0, chunk, per_row)
+    if known("pair") == "pair":
+        (relayed,) = partial_sums([3], "pair", (0, per_row))
+        next_near, next_far, skip_near, skip_far = partial_sums([1, 2], "pair", cuts)
+        own_near, own_far = partial_sums([0], "pair", cuts)
+        passed = along(relayed, beside)
+        if QTIE:
+            next_near, next_far = tied((next_near, next_far), passed)
+        edge = chunk * BLK
+
+        def merged(value, other):
+            return (value.astype(F32) + other.astype(F32)).astype(BF16)
+
+        far_terms = [
+            own_far,
+            along(next_far, beside),
+            along(merged(skip_far, passed[edge:]), across_pairs),
+        ]
+        near = [
+            own_near,
+            along(next_near, beside),
+            along(merged(skip_near, passed[:edge]), across_pairs),
+        ]
+    else:
+        outs = partial_sums(list(range(n_rows)), "direct", cuts)
+        near = [outs[0]] + [around(outs[2 * s], s) for s in range(1, n_rows)]
+        far_terms = [outs[1]] + [around(outs[2 * s + 1], s) for s in range(1, n_rows)]
     passing = far_terms[0]
     for term in far_terms[1:]:
         passing = passing + term.astype(F32)
@@ -502,36 +529,53 @@
         near, [far], weight, bias.reshape(1, hidden), cotangent, cols, chips
     )
 
+    near_all = gathered(known(AG_NEAR), near_prop)
     far_prop = far_prop.reshape(chips - 1, near_cols, chunk * BLK)
-    coming = [from_chip(far_prop[chips - s - 1], s) for s in range(1, chips)]
-    coming = coming[0] if chips == 2 else jnp.concatenate(coming, axis=1)
-    near_all = gathered(known(AG_NEAR), near_prop)
+    across = (chips - 1) * chunk * BLK // hidden
+    packed = -(-lines // across)
+    spare = -(-packed // 16) * 16
+
+    def pack(value):
+        value = jnp.pad(value.astype(BF16), ((0, across * packed - lines), (0, 0)))
+        value = jnp.concatenate([value[k * packed : (k + 1) * packed] for k in range(across)], axis=1)
+        return jnp.pad(value, ((0, spare - packed), (0, 0)))
 
     grads = weight_parts(near_mix, far_mix, delta, cols, chips)
     part = grads[0] + swap_cores(grads[1])
-    quarter = part[0]
-    for s in range(1, chips):
-        quarter = quarter + from_chip(part[chips - s], s)
-    across = coming.shape[1] // hidden
-    packed = -(-lines // across)
-    extra = jnp.pad(quarter.astype(BF16), ((0, across * packed - lines), (0, 0)))
-    extra = jnp.concatenate([extra[k * packed : (k + 1) * packed] for k in range(across)], axis=1)
-    spare = -(-packed // 16) * 16
-    extra = jnp.pad(extra, ((0, spare - packed), (0, 0)))
-    payload = jnp.concatenate([coming, extra], axis=0)
-    if TIE == 1:
-        payload = lax.optimization_barrier((payload, near_all[1]))[0]
-    elif TIE == 2:
-        payload = lax.optimization_barrier((payload, near_all[1:3]))[0]
-    elif TIE == 3:
-        payload = lax.optimization_barrier((payload, near_all[1:4]))[0]
-    far_all = gathered(known(AG_FAR), payload)
-
-    keep, send = spread_back(
-        meta, tile_weights,
-        [(chunk, known(AG_NEAR), near_all), (far_blocks, known(AG_FAR), far_all)],
-        near_cols, sources, tile_bits, source_bits, cols,
-    )
+    if XG and chips == 2:
+        both = from_chip(jnp.concatenate([far_prop[0], pack(part[1])], axis=0), 1)
+        extra = (both[near_cols:].astype(F32) + pack(part[0]).astype(F32)).astype(BF16)
+        payload = jnp.concatenate([both[:near_cols], extra], axis=0)
+    else:
+        coming = [from_chip(far_prop[chips - s - 1], s) for s in range(1, chips)]
+        coming = coming[0] if chips == 2 else jnp.concatenate(coming, axis=1)
+        quarter = part[0]
+        for s in range(1, chips):
+            quarter = quarter + from_chip(part[chips - s], s)
+        payload = jnp.concatenate([coming, pack(quarter)], axis=0)
+    if TIE:
+        payload = tied(payload, near_all[2:3] if TIE == 1 else near_all[1:3])
+    far_way = known(AG_FAR)
+    far_all = gathered(far_way, payload)
+
+    def pieces_of(way, arrays, first, count, only=None):
+        each = n_rows // len(arrays)
+        found = []
+        for i in range(n_rows) if only is None else only:
+            array = arrays[i // each]
+            found.append((array, (i % each) * (array.shape[0] // each), way, i, first, count))
+        return found
+
+    near_pieces = pieces_of(known(AG_NEAR), near_all, 0, chunk)
+    common = (near_cols, sources, per_row, layout, cols)
+    if SPLIT and far_way == "pair":
+        early = near_pieces + pieces_of(far_way, far_all, chunk, per_row - chunk, (0, 1, 2))
+        late = pieces_of(far_way, far_all, chunk, per_row - chunk, (3,))
+        (before,) = spread_back(meta, tile_weights, early, None, *common, False)
+        keep, send = spread_back(meta, tile_weights, late, before, *common, True)
+    else:
+        every = near_pieces + pieces_of(far_way, far_all, chunk, per_row - chunk)
+        keep, send = spread_back(meta, tile_weights, every, None, *common, True)
     grad_features = (keep + swap_cores(send).astype(F32)).astype(BF16)
 
     quarter = weight_sums(known(AG_FAR), far_all, near_cols, lines, packed, hidden)

time: 91.9 us -> 88.5 us (0.963)
  waiting for transfers between devices: 31.5 us -> 21.7 us
  starting transfers between devices: 18 us -> 22 us
  Pallas kernels: 13.6 us -> 17 us
    ppermute x9 -> x8, waiting for transfers between devices: 28.7 us -> 16.8 us  [along(): return lax.ppermute(value, 'rows', pairs)]
    ppermute x9 -> x8, starting transfers between devices: 11.1 us -> 15.2 us  [along(): return lax.ppermute(value, 'rows', pairs)]
    pallas_call x3 -> x4, Pallas kernels: 10.5 us -> 13.8 us  [the longest x3 10.7 us: aggregate(): call(body, 'aggregate', shapes, [SMEM_SPEC, HBM_SPEC, HBM_SPEC] + [VMEM_S...]
    ppermute x4, waiting for transfers between devices: 0.01 us -> 2.18 us  [from_chip(): return lax.ppermute(value, 'wide', pairs)]
  transfers between devices with their start and end apart: 17 -> 16, of which waited for: 7 -> 9; matrix products, arithmetic and copies ran while one was open for 1% -> 1% of each run, Pallas kernels for 9% -> 13%
where the time goes in v3:
time: 88.5 us; the launch traced here: 87.2 us
  blocking collectives  22.1 us (25%)
  starting transfers between devices  22 us (25%)
  waiting for transfers between devices  21.7 us (25%)
  Pallas kernels  17 us (19%)
  other arithmetic  1.87 us (2%)
  between operations  1.46 us (2%)
  local copies, waits for them, and re-layouts  1.05 us (1%)
    all_gather x1, blocking collectives, gathered(): return [lax.all_gather(value, 'rows', axis=0, tiled=True)]  22.1 us
    ppermute x8, waiting for transfers between devices, along(): return lax.ppermute(value, 'rows', pairs)  16.8 us
    ppermute x8, starting transfers between devices, along(): return lax.ppermute(value, 'rows', pairs)  15.2 us
    pallas_call x3, Pallas kernels, aggregate(): call(body, 'aggregate', shapes, [SMEM_SPEC, HBM_SPEC, HBM_SPEC] + [VMEM_S...  10.7 us
    ppermute x4, starting transfers between devices, from_chip(): return lax.ppermute(value, 'wide', pairs)  5.59 us
    pallas_call x1, Pallas kernels, spread_back(): call(body, 'spread_back', outs, [SMEM_SPEC, HBM_SPEC] + [VMEM_SPEC] * (le...  3.15 us
    ppermute x4, waiting for transfers between devices, swap_cores(): return lax.ppermute(value, 'wide', [(i, i ^ 1) for i in range(wide)])  2.75 us
    ppermute x4, waiting for transfers between devices, from_chip(): return lax.ppermute(value, 'wide', pairs)  2.18 us
  transfers between devices with their start and end apart: 16, of which 9 were waited for; matrix products, arithmetic and copies ran while one was open for 1% of the time, Pallas kernels for 13%

profile of v3, /device:TPU:0, one launch (start us, length us, event | category | flops | bytes accessed | tf_op | source)
XLA Modules:
  0.0 87.2 jit_solution(11363659521022890364)
XLA Ops:
  0.6 0.5 collective-permute-start
  1.8 0.8 and_select_fusion.meta_ref
  2.6 0.1 collective-permute-done.refs_0_
  2.7 0.0 copy-start
  2.7 1.0 %copy-done = bf16[64,3072]{1,0:T(8,128)(2,1)S(1)} copy-done((bf16[64,3072]{1,0:T(8,128)(2,1)S(1)}, bf16[64,3072]{1,0:T(8,128)(2,1)}, u32[]{:S(2)}) %copy-start) | copy-done | bytes 393240
  3.7 3.5 %aggregate.5 = bf16[1536,128]{1,0:T(8,128)(2,1)S(1)} custom-call(s32[240]{0:T(256)S(1)} %and_select_fusion.meta_ref, bf16[240,128,128]{2,1,0:T(8,128)(2,1)} %tiles_ref.7, bf16[64,3072]{1,0:T(8,128)(2,1)S(1)} %copy-done, bf16[64,3072]{1,0:T(8,128)(2,1)S(1)} %collective-permute-done.refs_0_), custom_call_target="tpu_custom_call" | custom-call | flops 503316480 | bytes 3932160 | tf_op jit(solution)/shard_map/aggregate/pallas_call | solution.py:176
  7.2 0.0 copy-start.3
  7.2 0.0 copy-start.1
  7.3 0.0 copy-start.2
  7.3 2.8 %collective-permute-start.2 = (bf16[1536,128]{1,0:T(8,128)(2,1)S(1)}, bf16[1536,128]{1,0:T(8,128)(2,1)S(1)}, u32[]{:S(2)}, u32[]{:S(2)}) collective-permute-start(bf16[1536,128]{1,0:T(8,128)(2,1)S(1)} %aggregate.5), channel_id=1, source_target_pairs={{0,1},{1,0},{2,3},{3,2},{4,5},{5,4},{6,7},{7,6},{8,9},{9,8},{10,11... | collective-permute-start | bytes 1179656 | tf_op jit(solution)/shard_map/ppermute | solution.py:450
  10.1 3.8 %aggregate.4 = (bf16[768,128]{1,0:T(8,128)(2,1)S(1)}, bf16[768,128]{1,0:T(8,128)(2,1)S(1)}, bf16[768,128]{1,0:T(8,128)(2,1)S(1)}, bf16[768,128]{1,0:T(8,128)(2,1)S(1)}) custom-call(s32[240]{0:T(256)S(1)} %and_select_fusion.meta_ref, bf16[240,128,128]{2,1,0:T(8,128)(2,1)} %tiles_ref.7, bf16[64,3072]{1,0:T(8,128)(2,1)S(1)} %copy-done, ...), custom_call_target="tpu_custom_call" | custom-call | flops 503316480 | bytes 3932160 | tf_op jit(solution)/shard_map/aggregate/pallas_call | solution.py:176
  13.9 0.2 collective-permute-start.4
  14.0 6.0 %collective-permute-done.2 = bf16[1536,128]{1,0:T(8,128)(2,1)S(1)} collective-permute-done((bf16[1536,128]{1,0:T(8,128)(2,1)S(1)}, bf16[1536,128]{1,0:T(8,128)(2,1)S(1)}, u32[]{:S(2)}, u32[]{:S(2)}) %collective-permute-start.2) | collective-permute-done | bytes 393248 | tf_op jit(solution)/shard_map/ppermute | solution.py:450
  20.0 0.1 add_convert_fusion.2
  20.1 3.1 %collective-permute-start.5 = (bf16[768,128]{1,0:T(8,128)(2,1)S(1)}, bf16[768,128]{1,0:T(8,128)(2,1)S(1)}, u32[]{:S(2)}, u32[]{:S(2)}) collective-permute-start(bf16[768,128]{1,0:T(8,128)(2,1)S(1)} %get-tuple-element.36), channel_id=1, source_target_pairs={{0,2},{1,3},{2,0},{3,1},{4,6},{5,7},{6,4},{7,5},{8,10},{9,11},{10,... | collective-permute-start | bytes 589832 | tf_op jit(solution)/shard_map/ppermute | solution.py:450
  23.2 1.6 %collective-permute-start.1 = (bf16[768,128]{1,0:T(8,128)(2,1)S(1)}, bf16[768,128]{1,0:T(8,128)(2,1)S(1)}, u32[]{:S(2)}, u32[]{:S(2)}) collective-permute-start(bf16[768,128]{1,0:T(8,128)(2,1)S(1)} %get-tuple-element.21), channel_id=1, source_target_pairs={{0,1},{1,0},{2,3},{3,2},{4,5},{5,4},{6,7},{7,6},{8,9},{9,8},{10,11... | collective-permute-start | bytes 589832 | tf_op jit(solution)/shard_map/ppermute | solution.py:450
  24.8 3.4 %aggregate.3 = (f32[768,128]{1,0:T(8,128)S(1)}, f32[768,128]{1,0:T(8,128)S(1)}) custom-call(s32[240]{0:T(256)S(1)} %and_select_fusion.meta_ref, bf16[240,128,128]{2,1,0:T(8,128)(2,1)} %tiles_ref.7, bf16[64,3072]{1,0:T(8,128)(2,1)S(1)} %copy-done, bf16[64,3072]{1,0:T(8,128)(2,1)S(1)} %collective-permute-done.refs_0_), custom_call_target="tpu_custom_call" | custom-call | flops 503316480 | bytes 3932160 | tf_op jit(solution)/shard_map/aggregate/pallas_call | solution.py:176
  28.2 2.2 %collective-permute-start.3 = (bf16[768,128]{1,0:T(8,128)(2,1)S(1)}, bf16[768,128]{1,0:T(8,128)(2,1)S(1)}, u32[]{:S(2)}, u32[]{:S(2)}) collective-permute-start(bf16[768,128]{1,0:T(8,128)(2,1)S(1)} %get-tuple-element.37), channel_id=1, source_target_pairs={{0,2},{1,3},{2,0},{3,1},{4,6},{5,7},{6,4},{7,5},{8,10},{9,11},{10,... | collective-permute-start | bytes 589832 | tf_op jit(solution)/shard_map/ppermute | solution.py:450
  30.4 0.0 collective-permute-done.4
  30.4 1.8 %collective-permute-done.5 = bf16[768,128]{1,0:T(8,128)(2,1)S(1)} collective-permute-done((bf16[768,128]{1,0:T(8,128)(2,1)S(1)}, bf16[768,128]{1,0:T(8,128)(2,1)S(1)}, u32[]{:S(2)}, u32[]{:S(2)}) %collective-permute-start.5) | collective-permute-done | bytes 196640 | tf_op jit(solution)/shard_map/ppermute | solution.py:450
  32.2 0.1 add_convert_fusion.1
  32.3 2.0 %collective-permute-start.6 = (bf16[768,128]{1,0:T(8,128)(2,1)S(1)}, bf16[768,128]{1,0:T(8,128)(2,1)S(1)}, u32[]{:S(2)}, u32[]{:S(2)}) collective-permute-start(bf16[768,128]{1,0:T(8,128)(2,1)S(1)} %add_convert_fusion.1), channel_id=1, source_target_pairs={{8,0},{12,4},{0,8},{4,12},{9,1},{13,5},{1,9},{5,13},{10,2},{14,6},... | collective-permute-start | bytes 589832 | tf_op jit(solution)/shard_map/ppermute | solution.py:447
  34.3 0.0 copy-done.3
  34.3 0.9 %collective-permute-done.1.refs_1_ = bf16[768,128]{1,0:T(8,128)(2,1)S(1)} collective-permute-done((bf16[768,128]{1,0:T(8,128)(2,1)S(1)}, bf16[768,128]{1,0:T(8,128)(2,1)S(1)}, u32[]{:S(2)}, u32[]{:S(2)}) %collective-permute-start.1) | collective-permute-done | bytes 196640 | tf_op jit(solution)/shard_map/ppermute | solution.py:450
  35.2 4.5 %collective-permute-done.3.refs_2_ = bf16[768,128]{1,0:T(8,128)(2,1)S(1)} collective-permute-done((bf16[768,128]{1,0:T(8,128)(2,1)S(1)}, bf16[768,128]{1,0:T(8,128)(2,1)S(1)}, u32[]{:S(2)}, u32[]{:S(2)}) %collective-permute-start.3) | collective-permute-done | bytes 196640 | tf_op jit(solution)/shard_map/ppermute | solution.py:450
  39.8 0.0 collective-permute-done.6.refs_3_
  39.8 0.0 copy-done.1
  39.8 0.0 copy-done.2
  39.8 2.1 %layer.1 = (bf16[768,256]{1,0:T(8,128)(2,1)}, bf16[128,768]{1,0:T(8,128)(2,1)S(1)}, bf16[128,768]{1,0:T(8,128)(2,1)S(1)}, bf16[768,128]{1,0:T(8,128)(2,1)S(1)}, ...) custom-call(f32[768,128]{1,0:T(8,128)S(1)} %get-tuple-element.20.refs_0_, ...), custom_call_target="tpu_custom_call" | custom-call | flops 201326592 | bytes 1966080 | tf_op jit(solution)/shard_map/layer/pallas_call | solution.py:321
  41.8 0.3 weight_parts.1
  42.1 0.1 collective-permute-start.11
  42.2 0.1 collective-permute-start.8
  42.3 1.3 %collective-permute-done.11 = f32[2,72,256]{2,1,0:T(8,128)S(1)} collective-permute-done((f32[2,72,256]{2,1,0:T(8,128)S(1)}, f32[2,72,256]{2,1,0:T(8,128)S(1)}, u32[]{:S(2)}, u32[]{:S(2)}) %collective-permute-start.11) | collective-permute-done | bytes 147488 | tf_op jit(solution)/shard_map/ppermute | solution.py:443
  43.6 1.8 %collective-permute-start.12 = (f32[72,256]{1,0:T(8,128)S(1)}, f32[72,256]{1,0:T(8,128)S(1)}, u32[]{:S(2)}, u32[]{:S(2)}) collective-permute-start(f32[72,256]{1,0:T(8,128)S(1)} %slice_bitcast_fusion.4), channel_id=1, source_target_pairs={{8,0},{12,4},{0,8},{4,12},{9,1},{13,5},{1,9},{5,13},{10,2},{14,6},... | collective-permute-start | bytes 221192 | tf_op jit(solution)/shard_map/ppermute | solution.py:447
  45.4 5.2 %collective-permute-start.7 = (bf16[128,768]{1,0:T(8,128)(2,1)S(1)}, bf16[128,768]{1,0:T(8,128)(2,1)S(1)}, u32[]{:S(2)}, u32[]{:S(2)}) collective-permute-start(bf16[128,768]{1,0:T(8,128)(2,1)S(1)} %get-tuple-element.27.refs_0_), channel_id=1, source_target_pairs={{0,1},{1,0},{2,3},{3,2},{4,5},{5,4},{6,7},{7,6},{8,9},{9,8},{10,11... | collective-permute-start | bytes 589832 | tf_op jit(solution)/shard_map/ppermute | solution.py:450
  50.6 0.5 collective-permute-start.10
  51.1 3.6 %collective-permute-done.8.refs_2_ = bf16[128,768]{1,0:T(8,128)(2,1)S(1)} collective-permute-done((bf16[128,768]{1,0:T(8,128)(2,1)S(1)}, bf16[128,768]{1,0:T(8,128)(2,1)S(1)}, u32[]{:S(2)}, u32[]{:S(2)}) %collective-permute-start.8) | collective-permute-done | bytes 196640 | tf_op jit(solution)/shard_map/ppermute | solution.py:450
  54.8 0.0 collective-permute-start.9
  54.8 0.0 collective-permute-done.12
  54.8 2.2 %collective-permute-done.10 = bf16[128,768]{1,0:T(8,128)(2,1)S(1)} collective-permute-done((bf16[128,768]{1,0:T(8,128)(2,1)S(1)}, bf16[128,768]{1,0:T(8,128)(2,1)S(1)}, u32[]{:S(2)}, u32[]{:S(2)}) %collective-permute-start.10) | collective-permute-done | bytes 196640 | tf_op jit(solution)/shard_map/ppermute | solution.py:447
  57.0 22.1 %all_gather.3.refs_4_.refs_0_ = bf16[640,768]{1,0:T(8,128)(2,1)S(1)} all-gather(bf16[160,768]{1,0:T(8,128)(2,1)S(1)} %pad_maximum_fusion), channel_id=1, replica_groups=mesh['groups'=2,'wide'=4,'rows'=4] {'rows'}, dimensions={0}, use_global_device_ids=true | all-gather | bytes 1228800 | tf_op jit(solution)/shard_map/all_gather | solution.py:462
  79.2 1.2 %collective-permute-start.14 = (f32[72,256]{1,0:T(8,128)S(1)}, f32[72,256]{1,0:T(8,128)S(1)}, u32[]{:S(2)}, u32[]{:S(2)}) collective-permute-start(f32[72,256]{1,0:T(8,128)S(1)} %weight_sums.1.refs_0_), channel_id=1, source_target_pairs={{8,0},{12,4},{0,8},{4,12},{9,1},{13,5},{1,9},{5,13},{10,2},{14,6},... | collective-permute-start | bytes 221192 | tf_op jit(solution)/shard_map/ppermute | solution.py:447
  80.4 0.0 collective-permute-done.7.refs_1_
  80.4 0.0 collective-permute-done.9.refs_3_
  80.4 3.2 %spread_back.1 = (f32[64,3072]{1,0:T(8,128)S(1)}, bf16[64,3072]{1,0:T(8,128)(2,1)S(1)}) custom-call(s32[240]{0:T(256)S(1)} %and_select_fusion.meta_ref, bf16[240,128,128]{2,1,0:T(8,128)(2,1)} %tiles_ref.7, bf16[128,768]{1,0:T(8,128)(2,1)S(1)} %get-tuple-element.27.refs_0_, bf16[128,768]{1,0:T(8,128)(2,1)S(1)} %collective-permute-done.7.refs_1_, ...), custom_call_target="tpu_custom_call" | custom-call | flops 503316480 | bytes 3932160 | tf_op jit(solution)/shard_map/spread_back/pallas_call | solution.py:260
  83.6 0.1 collective-permute-start.13
  83.7 0.0 collective-permute-done.14.refs_1_
  83.7 0.5 collective-permute-start.15
  84.2 1.3 %collective-permute-done.15 = f32[2,72,256]{2,1,0:T(8,128)S(1)} collective-permute-done((f32[2,72,256]{2,1,0:T(8,128)S(1)}, f32[2,72,256]{2,1,0:T(8,128)S(1)}, u32[]{:S(2)}, u32[]{:S(2)}) %collective-permute-start.15) | collective-permute-done | bytes 147488 | tf_op jit(solution)/shard_map/ppermute | solution.py:443
  85.6 0.7 assemble.1
  86.3 0.0 collective-permute-done.13
  86.3 0.8 add_convert_fusion
  (11 shorter events, 0.1 us)
Async XLA Ops:
  0.6 2.1 %collective-permute-start = (bf16[64,3072]{1,0:T(8,128)(2,1)}, bf16[64,3072]{1,0:T(8,128)(2,1)S(1)}, u32[]{:S(2)}, u32[]{:S(2)}) collective-permute-start(bf16[64,3072]{1,0:T(8,128)(2,1)} %own_ref.5), channel_id=1, source_target_pairs={{0,4},{4,0},{8,12},{12,8},{1,5},{5,1},{9,13},{13,9},{2,6},{6,2},{1... | collective-permute-start | bytes 1179656 | tf_op jit(solution)/shard_map/ppermute | solution.py:443
  2.7 1.0 %copy-start = (bf16[64,3072]{1,0:T(8,128)(2,1)S(1)}, bf16[64,3072]{1,0:T(8,128)(2,1)}, u32[]{:S(2)}) copy-start(bf16[64,3072]{1,0:T(8,128)(2,1)} %own_ref.5) | copy-start | bytes 1179652
  7.2 27.1 %copy-start.3 = (bf16[256]{0:T(256)(128)(2,1)S(1)}, bf16[256]{0:T(256)(128)(2,1)}, u32[]{:S(2)}) copy-start(bf16[256]{0:T(256)(128)(2,1)} %param.14) | copy-start | bytes 1540
  7.2 32.5 %copy-start.1 = (bf16[768,256]{1,0:T(8,128)(2,1)S(1)}, bf16[768,256]{1,0:T(8,128)(2,1)}, u32[]{:S(2)}) copy-start(bf16[768,256]{1,0:T(8,128)(2,1)} %refs_6_.1) | copy-start | bytes 1179652
  7.3 32.5 %copy-start.2 = (bf16[256,256]{1,0:T(8,128)(2,1)S(1)}, bf16[256,256]{1,0:T(8,128)(2,1)}, u32[]{:S(2)}) copy-start(bf16[256,256]{1,0:T(8,128)(2,1)} %refs_4_.1) | copy-start | bytes 393220
  7.3 12.7 %collective-permute-start.2 = (bf16[1536,128]{1,0:T(8,128)(2,1)S(1)}, bf16[1536,128]{1,0:T(8,128)(2,1)S(1)}, u32[]{:S(2)}, u32[]{:S(2)}) collective-permute-start(bf16[1536,128]{1,0:T(8,128)(2,1)S(1)} %aggregate.5), channel_id=1, source_target_pairs={{0,1},{1,0},{2,3},{3,2},{4,5},{5,4},{6,7},{7,6},{8,9},{9,8},{10,11... | collective-permute-start | bytes 1179656 | tf_op jit(solution)/shard_map/ppermute | solution.py:450
  13.9 16.6 %collective-permute-start.4 = (bf16[768,128]{1,0:T(8,128)(2,1)S(1)}, bf16[768,128]{1,0:T(8,128)(2,1)S(1)}, u32[]{:S(2)}, u32[]{:S(2)}) collective-permute-start(bf16[768,128]{1,0:T(8,128)(2,1)S(1)} %get-tuple-element.24), channel_id=1, source_target_pairs={{0,1},{1,0},{2,3},{3,2},{4,5},{5,4},{6,7},{7,6},{8,9},{9,8},{10,11... | collective-permute-start | bytes 589832 | tf_op jit(solution)/shard_map/ppermute | solution.py:450
  20.1 12.1 %collective-permute-start.5 = (bf16[768,128]{1,0:T(8,128)(2,1)S(1)}, bf16[768,128]{1,0:T(8,128)(2,1)S(1)}, u32[]{:S(2)}, u32[]{:S(2)}) collective-permute-start(bf16[768,128]{1,0:T(8,128)(2,1)S(1)} %get-tuple-element.36), channel_id=1, source_target_pairs={{0,2},{1,3},{2,0},{3,1},{4,6},{5,7},{6,4},{7,5},{8,10},{9,11},{10,... | collective-permute-start | bytes 589832 | tf_op jit(solution)/shard_map/ppermute | solution.py:450
  23.2 12.0 %collective-permute-start.1 = (bf16[768,128]{1,0:T(8,128)(2,1)S(1)}, bf16[768,128]{1,0:T(8,128)(2,1)S(1)}, u32[]{:S(2)}, u32[]{:S(2)}) collective-permute-start(bf16[768,128]{1,0:T(8,128)(2,1)S(1)} %get-tuple-element.21), channel_id=1, source_target_pairs={{0,1},{1,0},{2,3},{3,2},{4,5},{5,4},{6,7},{7,6},{8,9},{9,8},{10,11... | collective-permute-start | bytes 589832 | tf_op jit(solution)/shard_map/ppermute | solution.py:450
  28.2 11.5 %collective-permute-start.3 = (bf16[768,128]{1,0:T(8,128)(2,1)S(1)}, bf16[768,128]{1,0:T(8,128)(2,1)S(1)}, u32[]{:S(2)}, u32[]{:S(2)}) collective-permute-start(bf16[768,128]{1,0:T(8,128)(2,1)S(1)} %get-tuple-element.37), channel_id=1, source_target_pairs={{0,2},{1,3},{2,0},{3,1},{4,6},{5,7},{6,4},{7,5},{8,10},{9,11},{10,... | collective-permute-start | bytes 589832 | tf_op jit(solution)/shard_map/ppermute | solution.py:450
  32.3 7.5 %collective-permute-start.6 = (bf16[768,128]{1,0:T(8,128)(2,1)S(1)}, bf16[768,128]{1,0:T(8,128)(2,1)S(1)}, u32[]{:S(2)}, u32[]{:S(2)}) collective-permute-start(bf16[768,128]{1,0:T(8,128)(2,1)S(1)} %add_convert_fusion.1), channel_id=1, source_target_pairs={{8,0},{12,4},{0,8},{4,12},{9,1},{13,5},{1,9},{5,13},{10,2},{14,6},... | collective-permute-start | bytes 589832 | tf_op jit(solution)/shard_map/ppermute | solution.py:447
  42.1 1.4 %collective-permute-start.11 = (f32[2,72,256]{2,1,0:T(8,128)S(1)}, f32[2,72,256]{2,1,0:T(8,128)S(1)}, u32[]{:S(2)}, u32[]{:S(2)}) collective-permute-start(f32[2,72,256]{2,1,0:T(8,128)S(1)} %slice_bitcast_fusion), channel_id=1, source_target_pairs={{0,4},{4,0},{8,12},{12,8},{1,5},{5,1},{9,13},{13,9},{2,6},{6,2},{1... | collective-permute-start | bytes 442376 | tf_op jit(solution)/shard_map/ppermute | solution.py:443
  42.2 12.5 %collective-permute-start.8 = (bf16[128,768]{1,0:T(8,128)(2,1)S(1)}, bf16[128,768]{1,0:T(8,128)(2,1)S(1)}, u32[]{:S(2)}, u32[]{:S(2)}) collective-permute-start(bf16[128,768]{1,0:T(8,128)(2,1)S(1)} %get-tuple-element.27.refs_0_), channel_id=1, source_target_pairs={{0,2},{1,3},{2,0},{3,1},{4,6},{5,7},{6,4},{7,5},{8,10},{9,11},{10,... | collective-permute-start | bytes 589832 | tf_op jit(solution)/shard_map/ppermute | solution.py:450
  43.6 11.2 %collective-permute-start.12 = (f32[72,256]{1,0:T(8,128)S(1)}, f32[72,256]{1,0:T(8,128)S(1)}, u32[]{:S(2)}, u32[]{:S(2)}) collective-permute-start(f32[72,256]{1,0:T(8,128)S(1)} %slice_bitcast_fusion.4), channel_id=1, source_target_pairs={{8,0},{12,4},{0,8},{4,12},{9,1},{13,5},{1,9},{5,13},{10,2},{14,6},... | collective-permute-start | bytes 221192 | tf_op jit(solution)/shard_map/ppermute | solution.py:447
  45.4 35.0 %collective-permute-start.7 = (bf16[128,768]{1,0:T(8,128)(2,1)S(1)}, bf16[128,768]{1,0:T(8,128)(2,1)S(1)}, u32[]{:S(2)}, u32[]{:S(2)}) collective-permute-start(bf16[128,768]{1,0:T(8,128)(2,1)S(1)} %get-tuple-element.27.refs_0_), channel_id=1, source_target_pairs={{0,1},{1,0},{2,3},{3,2},{4,5},{5,4},{6,7},{7,6},{8,9},{9,8},{10,11... | collective-permute-start | bytes 589832 | tf_op jit(solution)/shard_map/ppermute | solution.py:450
  50.6 6.4 %collective-permute-start.10 = (bf16[128,768]{1,0:T(8,128)(2,1)S(1)}, bf16[128,768]{1,0:T(8,128)(2,1)S(1)}, u32[]{:S(2)}, u32[]{:S(2)}) collective-permute-start(bf16[128,768]{1,0:T(8,128)(2,1)S(1)} %get-tuple-element.28), channel_id=1, source_target_pairs={{8,0},{12,4},{0,8},{4,12},{9,1},{13,5},{1,9},{5,13},{10,2},{14,6},... | collective-permute-start | bytes 589832 | tf_op jit(solution)/shard_map/ppermute | solution.py:447
  54.8 25.7 %collective-permute-start.9 = (bf16[128,768]{1,0:T(8,128)(2,1)S(1)}, bf16[128,768]{1,0:T(8,128)(2,1)S(1)}, u32[]{:S(2)}, u32[]{:S(2)}) collective-permute-start(bf16[128,768]{1,0:T(8,128)(2,1)S(1)} %collective-permute-done.8.refs_2_), channel_id=1, source_target_pairs={{0,1},{1,0},{2,3},{3,2},{4,5},{5,4},{6,7},{7,6},{8,9},{9,8},{10,11... | collective-permute-start | bytes 589832 | tf_op jit(solution)/shard_map/ppermute | solution.py:450
  79.2 4.5 %collective-permute-start.14 = (f32[72,256]{1,0:T(8,128)S(1)}, f32[72,256]{1,0:T(8,128)S(1)}, u32[]{:S(2)}, u32[]{:S(2)}) collective-permute-start(f32[72,256]{1,0:T(8,128)S(1)} %weight_sums.1.refs_0_), channel_id=1, source_target_pairs={{8,0},{12,4},{0,8},{4,12},{9,1},{13,5},{1,9},{5,13},{10,2},{14,6},... | collective-permute-start | bytes 221192 | tf_op jit(solution)/shard_map/ppermute | solution.py:447
  83.6 2.8 %collective-permute-start.13 = (bf16[64,3072]{1,0:T(8,128)(2,1)S(1)}, bf16[64,3072]{1,0:T(8,128)(2,1)S(1)}, u32[]{:S(2)}, u32[]{:S(2)}) collective-permute-start(bf16[64,3072]{1,0:T(8,128)(2,1)S(1)} %get-tuple-element.33), channel_id=1, source_target_pairs={{0,4},{4,0},{8,12},{12,8},{1,5},{5,1},{9,13},{13,9},{2,6},{6,2},{1... | collective-permute-start | bytes 1179656 | tf_op jit(solution)/shard_map/ppermute | solution.py:443
  83.7 1.9 %collective-permute-start.15 = (f32[2,72,256]{2,1,0:T(8,128)S(1)}, f32[2,72,256]{2,1,0:T(8,128)S(1)}, u32[]{:S(2)}, u32[]{:S(2)}) collective-permute-start(f32[2,72,256]{2,1,0:T(8,128)S(1)} %pad_maximum_fusion.1), channel_id=1, source_target_pairs={{0,4},{4,0},{8,12},{12,8},{1,5},{5,1},{9,13},{13,9},{2,6},{6,2},{1... | collective-permute-start | bytes 442376 | tf_op jit(solution)/shard_map/ppermute | solution.py:443

commit v4 on v3

--- a/solution.py
+++ b/solution.py
@@ -10,6 +10,9 @@
 
 BLK = 128
 GROUP = 16
+GROUP_BACK = 16
+ROWS_UNIT = 8
+LATE = False
 AG_NEAR = "pair"
 AG_FAR = 'all'
 TIE = 0
@@ -46,8 +49,11 @@
     )
 
 
-def each_tile(meta, wanted, picked, tiles, ring, sems, tile_bits, prepare, multiply, add):
+def each_tile(
+    meta, wanted, picked, tiles, ring, sems, tile_bits, prepare, multiply, add, size=GROUP
+):
     total = meta.shape[0]
+    depth = ring.shape[0] // size
     tile_mask = (1 << tile_bits) - 1
 
     def scan(step, found):
@@ -58,14 +64,14 @@
         return found
 
     found = lax.fori_loop(0, total // GROUP, scan, jnp.int32(0))
-    for u in range(GROUP):
+    for u in range(size):
         picked[found + u] = jnp.int32(-1)
-    groups = lax.div(found + (GROUP - 1), GROUP)
+    groups = lax.div(found + (size - 1), size)
 
     def copies(group):
-        base = lax.rem(group, RING) * GROUP
-        for u in range(GROUP):
-            tile = jnp.maximum(picked[group * GROUP + u], 0) & tile_mask
+        base = lax.rem(group, depth) * size
+        for u in range(size):
+            tile = jnp.maximum(picked[group * size + u], 0) & tile_mask
             yield pltpu.make_async_copy(tiles.at[tile], ring.at[base + u], sems.at[base + u])
 
     def start(group, carry):
@@ -73,21 +79,21 @@
             copy.start()
         return carry
 
-    lax.fori_loop(0, jnp.minimum(groups, RING), start, 0)
+    lax.fori_loop(0, jnp.minimum(groups, depth), start, 0)
     prepare()
 
     def work(group, carry):
         for copy in copies(group):
             copy.wait()
-        base = lax.rem(group, RING) * GROUP
-        entries = [picked[group * GROUP + u] for u in range(GROUP)]
-        products = [multiply(entries[u], ring.at[base + u]) for u in range(GROUP)]
-        for u in range(GROUP):
+        base = lax.rem(group, depth) * size
+        entries = [picked[group * size + u] for u in range(size)]
+        products = [multiply(entries[u], ring.at[base + u]) for u in range(size)]
+        for u in range(size):
             add(entries[u], products[u])
 
-        @pl.when(group + RING < groups)
+        @pl.when(group + depth < groups)
         def _():
-            start(group + RING, 0)
+            start(group + depth, 0)
 
         return carry
 
@@ -96,7 +102,7 @@
 
 def ring_scratch(slots):
     return [
-        pltpu.SMEM((slots + GROUP,), jnp.int32),
+        pltpu.SMEM((slots + 2 * GROUP,), jnp.int32),
         pltpu.VMEM((RING * GROUP, BLK, BLK), BF16),
         pltpu.SemaphoreType.DMA((RING * GROUP,)),
     ]
@@ -242,6 +248,7 @@
             meta_ref,
             (lambda entry: entry >= 0) if last and before is None else wanted,
             picked, tiles_ref, ring, sems, tile_bits, prepare, multiply, add,
+            GROUP_BACK,
         )
         if last:
             for s in range(sources):
@@ -399,11 +406,12 @@
     )(*pieces)[0]
 
 
-def assemble(mine, other, cols, chips):
+def assemble(keep, got, mine, other, cols, chips):
     hidden = mine[0].shape[1]
 
-    def body(*refs):
-        out, bias_out = refs[-2:]
+    def body(keep_ref, got_ref, *refs):
+        grad_ref, out, bias_out = refs[-3:]
+        grad_ref[...] = (keep_ref[...] + got_ref[...].astype(F32)).astype(BF16)
         for part, owner in enumerate(spot_order(chips)):
             low = pl.multiple_of(owner * cols, cols)
             out[pl.ds(low, cols), :] = refs[(part % 2) * chips + part // 2][:cols, :]
@@ -413,14 +421,15 @@
         body,
         "assemble",
         [
+            jax.ShapeDtypeStruct(keep.shape, BF16),
             jax.ShapeDtypeStruct((2 * chips * cols, hidden), F32),
             jax.ShapeDtypeStruct((1, hidden), F32),
         ],
-        [VMEM_SPEC] * (2 * chips),
+        [VMEM_SPEC] * (2 + 2 * chips),
         [],
         0,
         8 * chips * cols * hidden,
-    )(*mine, *other)
+    )(keep, got, *mine, *other)
 
 
 def per_device(features, tile_weights, tile_source, tile_dest, tile_count, weight, bias, cotangent):
@@ -464,7 +473,9 @@
             return [value] + [around(value, -s) for s in range(1, n_rows)]
         got_skip = along(value, across_pairs)
         got_next = along(value, beside)
-        return [value, got_next, got_skip, along(got_skip, beside)]
+        return [value, got_next, got_skip, along(got_skip, beside)] if not LATE else [
+            value, got_next, got_skip
+        ]
 
     def tied(value, other):
         return lax.optimization_barrier((value, other))[0]
@@ -533,7 +544,7 @@
     far_prop = far_prop.reshape(chips - 1, near_cols, chunk * BLK)
     across = (chips - 1) * chunk * BLK // hidden
     packed = -(-lines // across)
-    spare = -(-packed // 16) * 16
+    spare = -(-packed // ROWS_UNIT) * ROWS_UNIT
 
     def pack(value):
         value = jnp.pad(value.astype(BF16), ((0, across * packed - lines), (0, 0)))
@@ -557,6 +568,8 @@
         payload = tied(payload, near_all[2:3] if TIE == 1 else near_all[1:3])
     far_way = known(AG_FAR)
     far_all = gathered(far_way, payload)
+    if LATE and known(AG_NEAR) == "pair":
+        near_all.append(along(tied(near_all[2], far_all[0]), beside))
 
     def pieces_of(way, arrays, first, count, only=None):
         each = n_rows // len(arrays)
@@ -576,12 +589,13 @@
     else:
         every = near_pieces + pieces_of(far_way, far_all, chunk, per_row - chunk)
         keep, send = spread_back(meta, tile_weights, every, None, *common, True)
-    grad_features = (keep + swap_cores(send).astype(F32)).astype(BF16)
-
+    got = swap_cores(send)
     quarter = weight_sums(known(AG_FAR), far_all, near_cols, lines, packed, hidden)
     half = [quarter] + [from_chip(quarter, s) for s in range(1, chips)]
     other_half = swap_cores(jnp.stack(half))
-    grad_weight, grad_bias = assemble(half, [other_half[s] for s in range(chips)], cols, chips)
+    grad_features, grad_weight, grad_bias = assemble(
+        keep, got, half, [other_half[s] for s in range(chips)], cols, chips
+    )
     return (activation, grad_features, grad_weight, grad_bias.reshape(hidden))
 
 

time: 88.5 us -> 87.1 us (0.984)
  starting transfers between devices: 22 us -> 20.5 us
  waiting for transfers between devices: 21.7 us -> 23.2 us
    ppermute x8, waiting for transfers between devices: 16.8 us -> 18.3 us  [along(): return lax.ppermute(value, 'rows', pairs)]
    ppermute x8, starting transfers between devices: 15.2 us -> 13.8 us  [along(): return lax.ppermute(value, 'rows', pairs)]
  transfers between devices with their start and end apart: 16 -> 16, of which waited for: 9 -> 9; matrix products, arithmetic and copies ran while one was open for 1% -> 1% of each run, Pallas kernels for 13% -> 12%
where the time goes in v4:
time: 87.1 us; the launch traced here: 86.3 us
  waiting for transfers between devices  23.2 us (27%)
  blocking collectives  21.5 us (25%)
  starting transfers between devices  20.5 us (24%)
  Pallas kernels  17.5 us (20%)
  between operations  1.47 us (2%)
  local copies, waits for them, and re-layouts  1.05 us (1%)
  other arithmetic  1.02 us (1%)
    all_gather x1, blocking collectives, gathered(): return [lax.all_gather(value, 'rows', axis=0, tiled=True)]  21.5 us
    ppermute x8, waiting for transfers between devices, along(): return lax.ppermute(value, 'rows', pairs)  18.3 us
    ppermute x8, starting transfers between devices, along(): return lax.ppermute(value, 'rows', pairs)  13.8 us
    pallas_call x3, Pallas kernels, aggregate(): call(body, 'aggregate', shapes, [SMEM_SPEC, HBM_SPEC, HBM_SPEC] + [VMEM_S...  11 us
    ppermute x4, starting transfers between devices, from_chip(): return lax.ppermute(value, 'wide', pairs)  5.51 us
    pallas_call x1, Pallas kernels, spread_back(): call(body, 'spread_back', outs, [SMEM_SPEC, HBM_SPEC] + [VMEM_SPEC] * (le...  3.28 us
    ppermute x4, waiting for transfers between devices, swap_cores(): return lax.ppermute(value, 'wide', [(i, i ^ 1) for i in range(wide)])  2.75 us
    ppermute x4, waiting for transfers between devices, from_chip(): return lax.ppermute(value, 'wide', pairs)  2.2 us
  transfers between devices with their start and end apart: 16, of which 9 were waited for; matrix products, arithmetic and copies ran while one was open for 1% of the time, Pallas kernels for 12%

profile of v4, /device:TPU:0, one launch (start us, length us, event | category | flops | bytes accessed | tf_op | source)
XLA Modules:
  0.0 86.3 jit_solution(18108843123860061974)
XLA Ops:
  0.6 0.5 collective-permute-start
  1.8 0.8 and_select_fusion.meta_ref
  2.6 0.1 collective-permute-done.refs_0_
  2.7 0.0 copy-start
  2.7 1.0 %copy-done = bf16[64,3072]{1,0:T(8,128)(2,1)S(1)} copy-done((bf16[64,3072]{1,0:T(8,128)(2,1)S(1)}, bf16[64,3072]{1,0:T(8,128)(2,1)}, u32[]{:S(2)}) %copy-start) | copy-done | bytes 393240
  3.7 3.6 %aggregate.5 = bf16[1536,128]{1,0:T(8,128)(2,1)S(1)} custom-call(s32[240]{0:T(256)S(1)} %and_select_fusion.meta_ref, bf16[240,128,128]{2,1,0:T(8,128)(2,1)} %tiles_ref.7, bf16[64,3072]{1,0:T(8,128)(2,1)S(1)} %copy-done, bf16[64,3072]{1,0:T(8,128)(2,1)S(1)} %collective-permute-done.refs_0_), custom_call_target="tpu_custom_call" | custom-call | flops 503316480 | bytes 3932160 | tf_op jit(solution)/shard_map/aggregate/pallas_call | solution.py:182
  7.3 0.0 copy-start.3
  7.3 0.0 copy-start.1
  7.3 0.0 copy-start.2
  7.3 2.8 %collective-permute-start.2 = (bf16[1536,128]{1,0:T(8,128)(2,1)S(1)}, bf16[1536,128]{1,0:T(8,128)(2,1)S(1)}, u32[]{:S(2)}, u32[]{:S(2)}) collective-permute-start(bf16[1536,128]{1,0:T(8,128)(2,1)S(1)} %aggregate.5), channel_id=1, source_target_pairs={{0,1},{1,0},{2,3},{3,2},{4,5},{5,4},{6,7},{7,6},{8,9},{9,8},{10,11... | collective-permute-start | bytes 1179656 | tf_op jit(solution)/shard_map/ppermute | solution.py:459
  10.1 3.8 %aggregate.4 = (bf16[768,128]{1,0:T(8,128)(2,1)S(1)}, bf16[768,128]{1,0:T(8,128)(2,1)S(1)}, bf16[768,128]{1,0:T(8,128)(2,1)S(1)}, bf16[768,128]{1,0:T(8,128)(2,1)S(1)}) custom-call(s32[240]{0:T(256)S(1)} %and_select_fusion.meta_ref, bf16[240,128,128]{2,1,0:T(8,128)(2,1)} %tiles_ref.7, bf16[64,3072]{1,0:T(8,128)(2,1)S(1)} %copy-done, ...), custom_call_target="tpu_custom_call" | custom-call | flops 503316480 | bytes 3932160 | tf_op jit(solution)/shard_map/aggregate/pallas_call | solution.py:182
  13.9 0.1 collective-permute-start.4
  14.0 6.0 %collective-permute-done.2 = bf16[1536,128]{1,0:T(8,128)(2,1)S(1)} collective-permute-done((bf16[1536,128]{1,0:T(8,128)(2,1)S(1)}, bf16[1536,128]{1,0:T(8,128)(2,1)S(1)}, u32[]{:S(2)}, u32[]{:S(2)}) %collective-permute-start.2) | collective-permute-done | bytes 393248 | tf_op jit(solution)/shard_map/ppermute | solution.py:459
  20.1 0.1 add_convert_fusion.1
  20.2 3.5 %collective-permute-start.5 = (bf16[768,128]{1,0:T(8,128)(2,1)S(1)}, bf16[768,128]{1,0:T(8,128)(2,1)S(1)}, u32[]{:S(2)}, u32[]{:S(2)}) collective-permute-start(bf16[768,128]{1,0:T(8,128)(2,1)S(1)} %get-tuple-element.38), channel_id=1, source_target_pairs={{0,2},{1,3},{2,0},{3,1},{4,6},{5,7},{6,4},{7,5},{8,10},{9,11},{10,... | collective-permute-start | bytes 589832 | tf_op jit(solution)/shard_map/ppermute | solution.py:459
  23.7 1.1 %collective-permute-start.1 = (bf16[768,128]{1,0:T(8,128)(2,1)S(1)}, bf16[768,128]{1,0:T(8,128)(2,1)S(1)}, u32[]{:S(2)}, u32[]{:S(2)}) collective-permute-start(bf16[768,128]{1,0:T(8,128)(2,1)S(1)} %get-tuple-element.22), channel_id=1, source_target_pairs={{0,1},{1,0},{2,3},{3,2},{4,5},{5,4},{6,7},{7,6},{8,9},{9,8},{10,11... | collective-permute-start | bytes 589832 | tf_op jit(solution)/shard_map/ppermute | solution.py:459
  24.8 3.6 %aggregate.3 = (f32[768,128]{1,0:T(8,128)S(1)}, f32[768,128]{1,0:T(8,128)S(1)}) custom-call(s32[240]{0:T(256)S(1)} %and_select_fusion.meta_ref, bf16[240,128,128]{2,1,0:T(8,128)(2,1)} %tiles_ref.7, bf16[64,3072]{1,0:T(8,128)(2,1)S(1)} %copy-done, bf16[64,3072]{1,0:T(8,128)(2,1)S(1)} %collective-permute-done.refs_0_), custom_call_target="tpu_custom_call" | custom-call | flops 503316480 | bytes 3932160 | tf_op jit(solution)/shard_map/aggregate/pallas_call | solution.py:182
  28.4 0.9 %collective-permute-start.3 = (bf16[768,128]{1,0:T(8,128)(2,1)S(1)}, bf16[768,128]{1,0:T(8,128)(2,1)S(1)}, u32[]{:S(2)}, u32[]{:S(2)}) collective-permute-start(bf16[768,128]{1,0:T(8,128)(2,1)S(1)} %get-tuple-element.39), channel_id=1, source_target_pairs={{0,2},{1,3},{2,0},{3,1},{4,6},{5,7},{6,4},{7,5},{8,10},{9,11},{10,... | collective-permute-start | bytes 589832 | tf_op jit(solution)/shard_map/ppermute | solution.py:459
  29.3 0.0 collective-permute-done.4
  29.3 2.7 %collective-permute-done.5 = bf16[768,128]{1,0:T(8,128)(2,1)S(1)} collective-permute-done((bf16[768,128]{1,0:T(8,128)(2,1)S(1)}, bf16[768,128]{1,0:T(8,128)(2,1)S(1)}, u32[]{:S(2)}, u32[]{:S(2)}) %collective-permute-start.5) | collective-permute-done | bytes 196640 | tf_op jit(solution)/shard_map/ppermute | solution.py:459
  32.0 0.1 add_convert_fusion
  32.0 1.8 %collective-permute-start.6 = (bf16[768,128]{1,0:T(8,128)(2,1)S(1)}, bf16[768,128]{1,0:T(8,128)(2,1)S(1)}, u32[]{:S(2)}, u32[]{:S(2)}) collective-permute-start(bf16[768,128]{1,0:T(8,128)(2,1)S(1)} %add_convert_fusion), channel_id=1, source_target_pairs={{8,0},{12,4},{0,8},{4,12},{9,1},{13,5},{1,9},{5,13},{10,2},{14,6},... | collective-permute-start | bytes 589832 | tf_op jit(solution)/shard_map/ppermute | solution.py:456
  33.8 0.0 copy-done.3
  33.8 1.0 %collective-permute-done.1.refs_1_ = bf16[768,128]{1,0:T(8,128)(2,1)S(1)} collective-permute-done((bf16[768,128]{1,0:T(8,128)(2,1)S(1)}, bf16[768,128]{1,0:T(8,128)(2,1)S(1)}, u32[]{:S(2)}, u32[]{:S(2)}) %collective-permute-start.1) | collective-permute-done | bytes 196640 | tf_op jit(solution)/shard_map/ppermute | solution.py:459
  34.8 4.9 %collective-permute-done.3.refs_2_ = bf16[768,128]{1,0:T(8,128)(2,1)S(1)} collective-permute-done((bf16[768,128]{1,0:T(8,128)(2,1)S(1)}, bf16[768,128]{1,0:T(8,128)(2,1)S(1)}, u32[]{:S(2)}, u32[]{:S(2)}) %collective-permute-start.3) | collective-permute-done | bytes 196640 | tf_op jit(solution)/shard_map/ppermute | solution.py:459
  39.7 0.0 collective-permute-done.6.refs_3_
  39.7 0.0 copy-done.1
  39.7 0.0 copy-done.2
  39.7 2.1 %layer.1 = (bf16[768,256]{1,0:T(8,128)(2,1)}, bf16[128,768]{1,0:T(8,128)(2,1)S(1)}, bf16[128,768]{1,0:T(8,128)(2,1)S(1)}, bf16[768,128]{1,0:T(8,128)(2,1)S(1)}, ...) custom-call(f32[768,128]{1,0:T(8,128)S(1)} %get-tuple-element.21.refs_0_, ...), custom_call_target="tpu_custom_call" | custom-call | flops 201326592 | bytes 1966080 | tf_op jit(solution)/shard_map/layer/pallas_call | solution.py:328
  41.8 0.3 weight_parts.1
  42.1 0.1 collective-permute-start.11
  42.2 0.1 collective-permute-start.8
  42.3 1.3 %collective-permute-done.11 = f32[2,72,256]{2,1,0:T(8,128)S(1)} collective-permute-done((f32[2,72,256]{2,1,0:T(8,128)S(1)}, f32[2,72,256]{2,1,0:T(8,128)S(1)}, u32[]{:S(2)}, u32[]{:S(2)}) %collective-permute-start.11) | collective-permute-done | bytes 147488 | tf_op jit(solution)/shard_map/ppermute | solution.py:452
  43.6 1.7 %collective-permute-start.12 = (f32[72,256]{1,0:T(8,128)S(1)}, f32[72,256]{1,0:T(8,128)S(1)}, u32[]{:S(2)}, u32[]{:S(2)}) collective-permute-start(f32[72,256]{1,0:T(8,128)S(1)} %slice_bitcast_fusion.4), channel_id=1, source_target_pairs={{8,0},{12,4},{0,8},{4,12},{9,1},{13,5},{1,9},{5,13},{10,2},{14,6},... | collective-permute-start | bytes 221192 | tf_op jit(solution)/shard_map/ppermute | solution.py:456
  45.3 5.3 %collective-permute-start.7 = (bf16[128,768]{1,0:T(8,128)(2,1)S(1)}, bf16[128,768]{1,0:T(8,128)(2,1)S(1)}, u32[]{:S(2)}, u32[]{:S(2)}) collective-permute-start(bf16[128,768]{1,0:T(8,128)(2,1)S(1)} %get-tuple-element.28.refs_0_), channel_id=1, source_target_pairs={{0,1},{1,0},{2,3},{3,2},{4,5},{5,4},{6,7},{7,6},{8,9},{9,8},{10,11... | collective-permute-start | bytes 589832 | tf_op jit(solution)/shard_map/ppermute | solution.py:459
  50.6 0.5 collective-permute-start.10
  51.1 3.6 %collective-permute-done.8.refs_2_ = bf16[128,768]{1,0:T(8,128)(2,1)S(1)} collective-permute-done((bf16[128,768]{1,0:T(8,128)(2,1)S(1)}, bf16[128,768]{1,0:T(8,128)(2,1)S(1)}, u32[]{:S(2)}, u32[]{:S(2)}) %collective-permute-start.8) | collective-permute-done | bytes 196640 | tf_op jit(solution)/shard_map/ppermute | solution.py:459
  54.7 0.0 collective-permute-start.9
  54.8 0.0 collective-permute-done.12
  54.8 2.2 %collective-permute-done.10 = bf16[128,768]{1,0:T(8,128)(2,1)S(1)} collective-permute-done((bf16[128,768]{1,0:T(8,128)(2,1)S(1)}, bf16[128,768]{1,0:T(8,128)(2,1)S(1)}, u32[]{:S(2)}, u32[]{:S(2)}) %collective-permute-start.10) | collective-permute-done | bytes 196640 | tf_op jit(solution)/shard_map/ppermute | solution.py:456
  57.0 21.5 %all_gather.3.refs_4_.refs_0_ = bf16[608,768]{1,0:T(8,128)(2,1)S(1)} all-gather(bf16[152,768]{1,0:T(8,128)(2,1)S(1)} %maximum_maximum_fusion), channel_id=1, replica_groups=mesh['groups'=2,'wide'=4,'rows'=4] {'rows'}, dimensions={0}, use_global_device_ids=true | all-gather | bytes 1167360 | tf_op jit(solution)/shard_map/all_gather | solution.py:471
  78.5 1.6 %collective-permute-start.14 = (f32[72,256]{1,0:T(8,128)S(1)}, f32[72,256]{1,0:T(8,128)S(1)}, u32[]{:S(2)}, u32[]{:S(2)}) collective-permute-start(f32[72,256]{1,0:T(8,128)S(1)} %weight_sums.1.refs_0_), channel_id=1, source_target_pairs={{8,0},{12,4},{0,8},{4,12},{9,1},{13,5},{1,9},{5,13},{10,2},{14,6},... | collective-permute-start | bytes 221192 | tf_op jit(solution)/shard_map/ppermute | solution.py:456
  80.1 0.0 collective-permute-done.7.refs_1_
  80.1 0.0 collective-permute-done.9.refs_3_
  80.1 3.3 %spread_back.1 = (f32[64,3072]{1,0:T(8,128)S(1)}, bf16[64,3072]{1,0:T(8,128)(2,1)S(1)}) custom-call(s32[240]{0:T(256)S(1)} %and_select_fusion.meta_ref, bf16[240,128,128]{2,1,0:T(8,128)(2,1)} %tiles_ref.7, bf16[128,768]{1,0:T(8,128)(2,1)S(1)} %get-tuple-element.28.refs_0_, bf16[128,768]{1,0:T(8,128)(2,1)S(1)} %collective-permute-done.7.refs_1_, ...), custom_call_target="tpu_custom_call" | custom-call | flops 503316480 | bytes 3932160 | tf_op jit(solution)/shard_map/spread_back/pallas_call | solution.py:267
  83.4 0.1 collective-permute-start.13
  83.5 0.0 collective-permute-done.14.refs_1_
  83.5 0.5 collective-permute-start.15
  84.0 1.3 %collective-permute-done.15 = f32[2,72,256]{2,1,0:T(8,128)S(1)} collective-permute-done((f32[2,72,256]{2,1,0:T(8,128)S(1)}, f32[2,72,256]{2,1,0:T(8,128)S(1)}, u32[]{:S(2)}, u32[]{:S(2)}) %collective-permute-start.15) | collective-permute-done | bytes 147488 | tf_op jit(solution)/shard_map/ppermute | solution.py:452
  85.4 0.0 collective-permute-done.13.got_ref
  85.4 0.9 %assemble.1 = (bf16[64,3072]{1,0:T(8,128)(2,1)}, f32[256,256]{1,0:T(8,128)}, f32[1,256]{1,0:T(1,128)}) custom-call(f32[64,3072]{1,0:T(8,128)S(1)} %get-tuple-element.33.keep_ref, bf16[64,3072]{1,0:T(8,128)(2,1)S(1)} %collective-permute-done.13.got_ref, f32[72,256]{1,0:T(8,128)S(1)} %weight_sums.1.refs_0_, f32[72,256]{1,0:T(8,128)S(1)} %collective-permute-done.14.refs_1_, ...), custom_call_target="tpu_custom_call" | custom-call | bytes 262144 | tf_op jit(solution)/shard_map/assemble/pallas_call | solution.py:420
  (10 shorter events, 0.1 us)
Async XLA Ops:
  0.6 2.1 %collective-permute-start = (bf16[64,3072]{1,0:T(8,128)(2,1)}, bf16[64,3072]{1,0:T(8,128)(2,1)S(1)}, u32[]{:S(2)}, u32[]{:S(2)}) collective-permute-start(bf16[64,3072]{1,0:T(8,128)(2,1)} %own_ref.5), channel_id=1, source_target_pairs={{0,4},{4,0},{8,12},{12,8},{1,5},{5,1},{9,13},{13,9},{2,6},{6,2},{1... | collective-permute-start | bytes 1179656 | tf_op jit(solution)/shard_map/ppermute | solution.py:452
  2.7 1.0 %copy-start = (bf16[64,3072]{1,0:T(8,128)(2,1)S(1)}, bf16[64,3072]{1,0:T(8,128)(2,1)}, u32[]{:S(2)}) copy-start(bf16[64,3072]{1,0:T(8,128)(2,1)} %own_ref.5) | copy-start | bytes 1179652
  7.3 26.5 %copy-start.3 = (bf16[256]{0:T(256)(128)(2,1)S(1)}, bf16[256]{0:T(256)(128)(2,1)}, u32[]{:S(2)}) copy-start(bf16[256]{0:T(256)(128)(2,1)} %param.14) | copy-start | bytes 1540
  7.3 32.4 %copy-start.1 = (bf16[768,256]{1,0:T(8,128)(2,1)S(1)}, bf16[768,256]{1,0:T(8,128)(2,1)}, u32[]{:S(2)}) copy-start(bf16[768,256]{1,0:T(8,128)(2,1)} %refs_6_.1) | copy-start | bytes 1179652
  7.3 32.4 %copy-start.2 = (bf16[256,256]{1,0:T(8,128)(2,1)S(1)}, bf16[256,256]{1,0:T(8,128)(2,1)}, u32[]{:S(2)}) copy-start(bf16[256,256]{1,0:T(8,128)(2,1)} %refs_4_.1) | copy-start | bytes 393220
  7.3 12.7 %collective-permute-start.2 = (bf16[1536,128]{1,0:T(8,128)(2,1)S(1)}, bf16[1536,128]{1,0:T(8,128)(2,1)S(1)}, u32[]{:S(2)}, u32[]{:S(2)}) collective-permute-start(bf16[1536,128]{1,0:T(8,128)(2,1)S(1)} %aggregate.5), channel_id=1, source_target_pairs={{0,1},{1,0},{2,3},{3,2},{4,5},{5,4},{6,7},{7,6},{8,9},{9,8},{10,11... | collective-permute-start | bytes 1179656 | tf_op jit(solution)/shard_map/ppermute | solution.py:459
  13.9 15.4 %collective-permute-start.4 = (bf16[768,128]{1,0:T(8,128)(2,1)S(1)}, bf16[768,128]{1,0:T(8,128)(2,1)S(1)}, u32[]{:S(2)}, u32[]{:S(2)}) collective-permute-start(bf16[768,128]{1,0:T(8,128)(2,1)S(1)} %get-tuple-element.25), channel_id=1, source_target_pairs={{0,1},{1,0},{2,3},{3,2},{4,5},{5,4},{6,7},{7,6},{8,9},{9,8},{10,11... | collective-permute-start | bytes 589832 | tf_op jit(solution)/shard_map/ppermute | solution.py:459
  20.2 11.8 %collective-permute-start.5 = (bf16[768,128]{1,0:T(8,128)(2,1)S(1)}, bf16[768,128]{1,0:T(8,128)(2,1)S(1)}, u32[]{:S(2)}, u32[]{:S(2)}) collective-permute-start(bf16[768,128]{1,0:T(8,128)(2,1)S(1)} %get-tuple-element.38), channel_id=1, source_target_pairs={{0,2},{1,3},{2,0},{3,1},{4,6},{5,7},{6,4},{7,5},{8,10},{9,11},{10,... | collective-permute-start | bytes 589832 | tf_op jit(solution)/shard_map/ppermute | solution.py:459
  23.7 11.1 %collective-permute-start.1 = (bf16[768,128]{1,0:T(8,128)(2,1)S(1)}, bf16[768,128]{1,0:T(8,128)(2,1)S(1)}, u32[]{:S(2)}, u32[]{:S(2)}) collective-permute-start(bf16[768,128]{1,0:T(8,128)(2,1)S(1)} %get-tuple-element.22), channel_id=1, source_target_pairs={{0,1},{1,0},{2,3},{3,2},{4,5},{5,4},{6,7},{7,6},{8,9},{9,8},{10,11... | collective-permute-start | bytes 589832 | tf_op jit(solution)/shard_map/ppermute | solution.py:459
  28.4 11.3 %collective-permute-start.3 = (bf16[768,128]{1,0:T(8,128)(2,1)S(1)}, bf16[768,128]{1,0:T(8,128)(2,1)S(1)}, u32[]{:S(2)}, u32[]{:S(2)}) collective-permute-start(bf16[768,128]{1,0:T(8,128)(2,1)S(1)} %get-tuple-element.39), channel_id=1, source_target_pairs={{0,2},{1,3},{2,0},{3,1},{4,6},{5,7},{6,4},{7,5},{8,10},{9,11},{10,... | collective-permute-start | bytes 589832 | tf_op jit(solution)/shard_map/ppermute | solution.py:459
  32.0 7.7 %collective-permute-start.6 = (bf16[768,128]{1,0:T(8,128)(2,1)S(1)}, bf16[768,128]{1,0:T(8,128)(2,1)S(1)}, u32[]{:S(2)}, u32[]{:S(2)}) collective-permute-start(bf16[768,128]{1,0:T(8,128)(2,1)S(1)} %add_convert_fusion), channel_id=1, source_target_pairs={{8,0},{12,4},{0,8},{4,12},{9,1},{13,5},{1,9},{5,13},{10,2},{14,6},... | collective-permute-start | bytes 589832 | tf_op jit(solution)/shard_map/ppermute | solution.py:456
  42.1 1.4 %collective-permute-start.11 = (f32[2,72,256]{2,1,0:T(8,128)S(1)}, f32[2,72,256]{2,1,0:T(8,128)S(1)}, u32[]{:S(2)}, u32[]{:S(2)}) collective-permute-start(f32[2,72,256]{2,1,0:T(8,128)S(1)} %slice_bitcast_fusion), channel_id=1, source_target_pairs={{0,4},{4,0},{8,12},{12,8},{1,5},{5,1},{9,13},{13,9},{2,6},{6,2},{1... | collective-permute-start | bytes 442376 | tf_op jit(solution)/shard_map/ppermute | solution.py:452
  42.2 12.5 %collective-permute-start.8 = (bf16[128,768]{1,0:T(8,128)(2,1)S(1)}, bf16[128,768]{1,0:T(8,128)(2,1)S(1)}, u32[]{:S(2)}, u32[]{:S(2)}) collective-permute-start(bf16[128,768]{1,0:T(8,128)(2,1)S(1)} %get-tuple-element.28.refs_0_), channel_id=1, source_target_pairs={{0,2},{1,3},{2,0},{3,1},{4,6},{5,7},{6,4},{7,5},{8,10},{9,11},{10,... | collective-permute-start | bytes 589832 | tf_op jit(solution)/shard_map/ppermute | solution.py:459
  43.6 11.2 %collective-permute-start.12 = (f32[72,256]{1,0:T(8,128)S(1)}, f32[72,256]{1,0:T(8,128)S(1)}, u32[]{:S(2)}, u32[]{:S(2)}) collective-permute-start(f32[72,256]{1,0:T(8,128)S(1)} %slice_bitcast_fusion.4), channel_id=1, source_target_pairs={{8,0},{12,4},{0,8},{4,12},{9,1},{13,5},{1,9},{5,13},{10,2},{14,6},... | collective-permute-start | bytes 221192 | tf_op jit(solution)/shard_map/ppermute | solution.py:456
  45.3 34.8 %collective-permute-start.7 = (bf16[128,768]{1,0:T(8,128)(2,1)S(1)}, bf16[128,768]{1,0:T(8,128)(2,1)S(1)}, u32[]{:S(2)}, u32[]{:S(2)}) collective-permute-start(bf16[128,768]{1,0:T(8,128)(2,1)S(1)} %get-tuple-element.28.refs_0_), channel_id=1, source_target_pairs={{0,1},{1,0},{2,3},{3,2},{4,5},{5,4},{6,7},{7,6},{8,9},{9,8},{10,11... | collective-permute-start | bytes 589832 | tf_op jit(solution)/shard_map/ppermute | solution.py:459
  50.6 6.4 %collective-permute-start.10 = (bf16[128,768]{1,0:T(8,128)(2,1)S(1)}, bf16[128,768]{1,0:T(8,128)(2,1)S(1)}, u32[]{:S(2)}, u32[]{:S(2)}) collective-permute-start(bf16[128,768]{1,0:T(8,128)(2,1)S(1)} %get-tuple-element.29), channel_id=1, source_target_pairs={{8,0},{12,4},{0,8},{4,12},{9,1},{13,5},{1,9},{5,13},{10,2},{14,6},... | collective-permute-start | bytes 589832 | tf_op jit(solution)/shard_map/ppermute | solution.py:456
  54.7 25.3 %collective-permute-start.9 = (bf16[128,768]{1,0:T(8,128)(2,1)S(1)}, bf16[128,768]{1,0:T(8,128)(2,1)S(1)}, u32[]{:S(2)}, u32[]{:S(2)}) collective-permute-start(bf16[128,768]{1,0:T(8,128)(2,1)S(1)} %collective-permute-done.8.refs_2_), channel_id=1, source_target_pairs={{0,1},{1,0},{2,3},{3,2},{4,5},{5,4},{6,7},{7,6},{8,9},{9,8},{10,11... | collective-permute-start | bytes 589832 | tf_op jit(solution)/shard_map/ppermute | solution.py:459
  78.5 4.9 %collective-permute-start.14 = (f32[72,256]{1,0:T(8,128)S(1)}, f32[72,256]{1,0:T(8,128)S(1)}, u32[]{:S(2)}, u32[]{:S(2)}) collective-permute-start(f32[72,256]{1,0:T(8,128)S(1)} %weight_sums.1.refs_0_), channel_id=1, source_target_pairs={{8,0},{12,4},{0,8},{4,12},{9,1},{13,5},{1,9},{5,13},{10,2},{14,6},... | collective-permute-start | bytes 221192 | tf_op jit(solution)/shard_map/ppermute | solution.py:456
  83.4 2.0 %collective-permute-start.13 = (bf16[64,3072]{1,0:T(8,128)(2,1)S(1)}, bf16[64,3072]{1,0:T(8,128)(2,1)S(1)}, u32[]{:S(2)}, u32[]{:S(2)}) collective-permute-start(bf16[64,3072]{1,0:T(8,128)(2,1)S(1)} %get-tuple-element.34), channel_id=1, source_target_pairs={{0,4},{4,0},{8,12},{12,8},{1,5},{5,1},{9,13},{13,9},{2,6},{6,2},{1... | collective-permute-start | bytes 1179656 | tf_op jit(solution)/shard_map/ppermute | solution.py:452
  83.5 1.9 %collective-permute-start.15 = (f32[2,72,256]{2,1,0:T(8,128)S(1)}, f32[2,72,256]{2,1,0:T(8,128)S(1)}, u32[]{:S(2)}, u32[]{:S(2)}) collective-permute-start(f32[2,72,256]{2,1,0:T(8,128)S(1)} %pad_maximum_fusion), channel_id=1, source_target_pairs={{0,4},{4,0},{8,12},{12,8},{1,5},{5,1},{9,13},{13,9},{2,6},{6,2},{1... | collective-permute-start | bytes 442376 | tf_op jit(solution)/shard_map/ppermute | solution.py:452

commit v5 on v3

--- a/solution.py
+++ b/solution.py
@@ -1,4 +1,3 @@
-import functools
 import math
 
 import jax
@@ -10,13 +9,6 @@
 
 BLK = 128
 GROUP = 16
-AG_NEAR = "pair"
-AG_FAR = 'all'
-TIE = 0
-QTIE = 0
-COST = 1
-XG = False
-SPLIT = False
 RING = 4
 VMEM_BYTES = 48 * 1024 * 1024
 ROOT = math.sqrt(2.0 / math.pi)
@@ -42,25 +34,12 @@
         out_specs=jax.tree.map(lambda _: VMEM_SPEC, out_shape),
         scratch_shapes=scratch,
         compiler_params=pltpu.CompilerParams(vmem_limit_bytes=VMEM_BYTES),
-        cost_estimate=pl.CostEstimate(flops=COST * flops, bytes_accessed=COST * nbytes, transcendentals=0),
+        cost_estimate=pl.CostEstimate(flops=flops, bytes_accessed=nbytes, transcendentals=0),
     )
 
 
 def each_tile(meta, wanted, picked, tiles, ring, sems, tile_bits, prepare, multiply, add):
-    total = meta.shape[0]
     tile_mask = (1 << tile_bits) - 1
-
-    def scan(step, found):
-        for u in range(GROUP):
-            entry = meta[step * GROUP + u]
-            picked[found] = entry
-            found = found + jnp.where(wanted(entry), 1, 0)
-        return found
-
-    found = lax.fori_loop(0, total // GROUP, scan, jnp.int32(0))
-    for u in range(GROUP):
-        picked[found + u] = jnp.int32(-1)
-    groups = lax.div(found + (GROUP - 1), GROUP)
 
     def copies(group):
         base = lax.rem(group, RING) * GROUP
@@ -73,7 +52,26 @@
             copy.start()
         return carry
 
-    lax.fori_loop(0, jnp.minimum(groups, RING), start, 0)
+    def scan(step, state):
+        found, begun = state
+        for u in range(GROUP):
+            entry = meta[step * GROUP + u]
+            picked[found] = entry
+            found = found + jnp.where(wanted(entry), 1, 0)
+        full = (found >= (begun + 1) * GROUP) & (begun < RING)
+
+        @pl.when(full)
+        def _():
+            start(begun, 0)
+
+        return found, begun + jnp.where(full, 1, 0)
+
+    zero = jnp.int32(0)
+    found, begun = lax.fori_loop(0, meta.shape[0] // GROUP, scan, (zero, zero))
+    for u in range(GROUP):
+        picked[found + u] = jnp.int32(-1)
+    groups = lax.div(found + (GROUP - 1), GROUP)
+    lax.fori_loop(begun, jnp.minimum(groups, RING), start, 0)
     prepare()
 
     def work(group, carry):
@@ -190,43 +188,27 @@
     )(meta, tiles, *parts)
 
 
-def spread_back(meta, tiles, pieces, before, columns, sources, per_row, layout, cols, last):
+def spread_back(meta, tiles, pieces, columns, sources, per_row, layout, cols):
     tile_bits, source_bits, nth_bits = layout
     given = []
     for piece in pieces:
         if not any(piece[0] is other for other in given):
             given.append(piece[0])
-    extra = [] if before is None else [before]
     spare = lax.axis_size("rows") * per_row
 
     def body(meta_ref, tiles_ref, *refs):
-        rest = refs[len(given) + len(extra) :]
-        if last:
-            keep, send, held, total, picked, ring, sems = rest
-        else:
-            total, held, picked, ring, sems = rest
-        rows = [row_at(way, i) for _, _, way, i, _, _ in pieces]
+        keep, send, held, total, picked, ring, sems = refs[len(given) :]
 
         def prepare():
-            if before is None:
-                total[...] = jnp.zeros_like(total)
-            else:
-                total[...] = refs[len(given)][...]
+            total[...] = jnp.zeros_like(total)
             held[spare] = jnp.zeros_like(held[spare])
-            for (array, line, _, _, first, count), row in zip(pieces, rows):
+            for array, line, way, i, first, count in pieces:
                 ref = next(ref for ref, other in zip(refs, given) if other is array)
+                row = row_at(way, i)
                 for q in range(count):
                     held[row * per_row + first + q] = ref[
                         line : line + columns, q * BLK : (q + 1) * BLK
                     ]
-
-        def wanted(entry):
-            rest = entry >> (tile_bits + source_bits)
-            owner, nth = rest >> nth_bits, rest & ((1 << nth_bits) - 1)
-            found = owner < 0
-            for (_, _, _, _, first, count), row in zip(pieces, rows):
-                found = found | ((owner == row) & (nth >= first) & (nth < first + count))
-            return found & (entry >= 0)
 
         def multiply(entry, tile):
             rest = entry >> (tile_bits + source_bits)
@@ -239,35 +221,30 @@
             total[source] += product
 
         each_tile(
-            meta_ref,
-            (lambda entry: entry >= 0) if last and before is None else wanted,
-            picked, tiles_ref, ring, sems, tile_bits, prepare, multiply, add,
+            meta_ref, lambda entry: entry >= 0, picked, tiles_ref, ring, sems, tile_bits,
+            prepare, multiply, add,
         )
-        if last:
-            for s in range(sources):
-                keep[:, s * BLK : (s + 1) * BLK] = total[s, :cols, :]
-                send[:, s * BLK : (s + 1) * BLK] = total[s, cols:, :].astype(BF16)
+        for s in range(sources):
+            keep[:, s * BLK : (s + 1) * BLK] = total[s, :cols, :]
+            send[:, s * BLK : (s + 1) * BLK] = total[s, cols:, :].astype(BF16)
 
     slots = tiles.shape[0]
-    sums = (sources, columns, BLK)
-    if last:
-        outs = [
+    return call(
+        body,
+        "spread_back",
+        [
             jax.ShapeDtypeStruct((cols, sources * BLK), F32),
             jax.ShapeDtypeStruct((cols, sources * BLK), BF16),
+        ],
+        [SMEM_SPEC, HBM_SPEC] + [VMEM_SPEC] * len(given),
+        [
+            pltpu.VMEM((spare + 1, columns, BLK), BF16),
+            pltpu.VMEM((sources, columns, BLK), F32),
         ]
-    else:
-        outs = [jax.ShapeDtypeStruct(sums, F32)]
-    return call(
-        body,
-        "spread_back",
-        outs,
-        [SMEM_SPEC, HBM_SPEC] + [VMEM_SPEC] * (len(given) + len(extra)),
-        [pltpu.VMEM((spare + 1, columns, BLK), BF16)]
-        + ([pltpu.VMEM(sums, F32)] if last else [])
         + ring_scratch(tiles.shape[0]),
         slots * BLK * BLK * columns,
         slots * BLK * BLK,
-    )(meta, tiles, *given, *extra)
+    )(meta, tiles, *given)
 
 
 def spot_order(chips):
@@ -368,42 +345,37 @@
     )(near_mix, far_mix, delta)[0]
 
 
-def weight_sums(way, pieces, top, lines, packed, hidden):
-    n_rows = lax.axis_size("rows")
-    width = pieces[0].shape[1] // hidden
-
-    def body(*refs):
-        out, held = refs[-2:]
-        for i in range(n_rows):
-            ref = refs[i // (n_rows // len(pieces))]
-            low = (i % (n_rows // len(pieces))) * (ref.shape[0] // (n_rows // len(pieces))) + top
-            place = row_at(way, i)
-            for k in range(width):
-                rows = min(packed, lines - k * packed)
-                if rows > 0:
-                    part = ref[low : low + packed, k * hidden : (k + 1) * hidden].astype(F32)
-                    held[place, k * packed : k * packed + rows, :] = part[:rows]
-        value = held[0]
-        for r in range(1, n_rows):
-            value = value + held[r]
-        out[...] = value
+def weight_sums(gathered, n_rows, top, lines, packed, hidden):
+    tall, width = gathered.shape[0] // n_rows, gathered.shape[1] // hidden
+
+    def body(ref, out):
+        for k in range(width):
+            rows = min(packed, lines - k * packed)
+            if rows > 0:
+                value = jnp.zeros((packed, hidden), F32)
+                for row in range(n_rows):
+                    low = row * tall + top
+                    part = ref[low : low + packed, k * hidden : (k + 1) * hidden]
+                    value = value + part.astype(F32)
+                out[k * packed : k * packed + rows, :] = value[:rows]
 
     return call(
         body,
         "weight_sums",
         [jax.ShapeDtypeStruct((lines, hidden), F32)],
-        [VMEM_SPEC] * len(pieces),
-        [pltpu.VMEM((n_rows, lines, hidden), F32)],
+        [VMEM_SPEC],
+        [],
         0,
         8 * lines * hidden,
-    )(*pieces)[0]
-
-
-def assemble(mine, other, cols, chips):
+    )(gathered)[0]
+
+
+def assemble(keep, got, mine, other, cols, chips):
     hidden = mine[0].shape[1]
 
-    def body(*refs):
-        out, bias_out = refs[-2:]
+    def body(keep_ref, got_ref, *refs):
+        grad_ref, out, bias_out = refs[-3:]
+        grad_ref[...] = (keep_ref[...] + got_ref[...].astype(F32)).astype(BF16)
         for part, owner in enumerate(spot_order(chips)):
             low = pl.multiple_of(owner * cols, cols)
             out[pl.ds(low, cols), :] = refs[(part % 2) * chips + part // 2][:cols, :]
@@ -413,14 +385,15 @@
         body,
         "assemble",
         [
+            jax.ShapeDtypeStruct(keep.shape, BF16),
             jax.ShapeDtypeStruct((2 * chips * cols, hidden), F32),
             jax.ShapeDtypeStruct((1, hidden), F32),
         ],
-        [VMEM_SPEC] * (2 * chips),
+        [VMEM_SPEC] * (2 + 2 * chips),
         [],
         0,
         8 * chips * cols * hidden,
-    )(*mine, *other)
+    )(keep, got, *mine, *other)
 
 
 def per_device(features, tile_weights, tile_source, tile_dest, tile_count, weight, bias, cotangent):
@@ -431,10 +404,11 @@
     wide = lax.axis_size("wide")
     chips = wide // 2
     n_rows = lax.axis_size("rows")
+    paired = n_rows == 4
     chunk = sources // wide
+    per_row = chips * chunk
     near_cols = 2 * cols
     lines = cols + 8
-    tile_bits, source_bits = bits_of(slots), bits_of(sources)
 
     at = lax.axis_index("wide")
     chip, core = at >> 1, at & 1
@@ -446,30 +420,20 @@
         pairs = [(2 * ((i + shift) % chips) + k, 2 * i + k) for i in range(chips) for k in range(2)]
         return lax.ppermute(value, "wide", pairs)
 
-    def along(value, pairs):
-        return lax.ppermute(value, "rows", pairs)
-
     def around(value, shift):
-        return along(value, [(i, (i + shift) % n_rows) for i in range(n_rows)])
-
-    beside, across_pairs = [(0, 1), (1, 0), (2, 3), (3, 2)], [(0, 2), (1, 3), (2, 0), (3, 1)]
-
-    def known(way):
-        return way if n_rows == 4 or way == "all" else "direct"
-
-    def gathered(way, value):
-        if way == "all":
-            return [lax.all_gather(value, "rows", axis=0, tiled=True)]
-        if way == "direct":
-            return [value] + [around(value, -s) for s in range(1, n_rows)]
-        got_skip = along(value, across_pairs)
-        got_next = along(value, beside)
-        return [value, got_next, got_skip, along(got_skip, beside)]
+        return lax.ppermute(value, "rows", [(i, (i + shift) % n_rows) for i in range(n_rows)])
+
+    def beside(value):
+        return lax.ppermute(value, "rows", [(i, i ^ 1) for i in range(n_rows)])
+
+    def across(value):
+        return lax.ppermute(value, "rows", [(i, i ^ 2) for i in range(n_rows)])
 
     def tied(value, other):
         return lax.optimization_barrier((value, other))[0]
 
     parts = [features, swap_cores(features)]
+    layout = tile_bits, source_bits, nth_bits = bits_of(slots), bits_of(sources), bits_of(per_row)
 
     def split(value, size):
         whole = ((value.astype(F32) + 0.5) * (1.0 / size)).astype(jnp.int32)
@@ -480,9 +444,6 @@
     holder, nth = split(within, chunk)
     away = (holder >> 1) - chip
     away = jnp.where(away < 0, away + chips, away)
-    per_row = chips * chunk
-    nth_bits = bits_of(per_row)
-    layout = (tile_bits, source_bits, nth_bits)
     place = (owner << nth_bits) | (away * chunk + nth)
     ours = (slot < tile_count[0]) & ((holder & 1) == core)
     meta = (place << (source_bits + tile_bits)) | (tile_source << tile_bits) | slot
@@ -492,28 +453,18 @@
         return aggregate(meta, tile_weights, parts, owners, way, cuts, layout)
 
     cuts = (0, chunk, per_row)
-    if known("pair") == "pair":
-        (relayed,) = partial_sums([3], "pair", (0, per_row))
-        next_near, next_far, skip_near, skip_far = partial_sums([1, 2], "pair", cuts)
-        own_near, own_far = partial_sums([0], "pair", cuts)
-        passed = along(relayed, beside)
-        if QTIE:
-            next_near, next_far = tied((next_near, next_far), passed)
-        edge = chunk * BLK
+    if paired:
 
         def merged(value, other):
             return (value.astype(F32) + other.astype(F32)).astype(BF16)
 
-        far_terms = [
-            own_far,
-            along(next_far, beside),
-            along(merged(skip_far, passed[edge:]), across_pairs),
-        ]
-        near = [
-            own_near,
-            along(next_near, beside),
-            along(merged(skip_near, passed[:edge]), across_pairs),
-        ]
+        (relayed,) = partial_sums([3], "pair", (0, per_row))
+        near_1, far_1, near_2, far_2 = partial_sums([1, 2], "pair", cuts)
+        near_0, far_0 = partial_sums([0], "pair", cuts)
+        passed = beside(relayed)
+        edge = chunk * BLK
+        far_terms = [far_0, beside(far_1), across(merged(far_2, passed[edge:]))]
+        near = [near_0, beside(near_1), across(merged(near_2, passed[:edge]))]
     else:
         outs = partial_sums(list(range(n_rows)), "direct", cuts)
         near = [outs[0]] + [around(outs[2 * s], s) for s in range(1, n_rows)]
@@ -529,59 +480,43 @@
         near, [far], weight, bias.reshape(1, hidden), cotangent, cols, chips
     )
 
-    near_all = gathered(known(AG_NEAR), near_prop)
     far_prop = far_prop.reshape(chips - 1, near_cols, chunk * BLK)
-    across = (chips - 1) * chunk * BLK // hidden
-    packed = -(-lines // across)
-    spare = -(-packed // 16) * 16
-
-    def pack(value):
-        value = jnp.pad(value.astype(BF16), ((0, across * packed - lines), (0, 0)))
-        value = jnp.concatenate([value[k * packed : (k + 1) * packed] for k in range(across)], axis=1)
-        return jnp.pad(value, ((0, spare - packed), (0, 0)))
+    coming = [from_chip(far_prop[chips - s - 1], s) for s in range(1, chips)]
+    coming = coming[0] if chips == 2 else jnp.concatenate(coming, axis=1)
+    if paired:
+        got_skip = across(near_prop)
+        got_next = beside(near_prop)
+        got_last = beside(tied(got_skip, coming))
+        near_all = [near_prop, got_next, got_skip, got_last]
+    else:
+        near_all = [near_prop] + [around(near_prop, -s) for s in range(1, n_rows)]
 
     grads = weight_parts(near_mix, far_mix, delta, cols, chips)
     part = grads[0] + swap_cores(grads[1])
-    if XG and chips == 2:
-        both = from_chip(jnp.concatenate([far_prop[0], pack(part[1])], axis=0), 1)
-        extra = (both[near_cols:].astype(F32) + pack(part[0]).astype(F32)).astype(BF16)
-        payload = jnp.concatenate([both[:near_cols], extra], axis=0)
-    else:
-        coming = [from_chip(far_prop[chips - s - 1], s) for s in range(1, chips)]
-        coming = coming[0] if chips == 2 else jnp.concatenate(coming, axis=1)
-        quarter = part[0]
-        for s in range(1, chips):
-            quarter = quarter + from_chip(part[chips - s], s)
-        payload = jnp.concatenate([coming, pack(quarter)], axis=0)
-    if TIE:
-        payload = tied(payload, near_all[2:3] if TIE == 1 else near_all[1:3])
-    far_way = known(AG_FAR)
-    far_all = gathered(far_way, payload)
-
-    def pieces_of(way, arrays, first, count, only=None):
-        each = n_rows // len(arrays)
-        found = []
-        for i in range(n_rows) if only is None else only:
-            array = arrays[i // each]
-            found.append((array, (i % each) * (array.shape[0] // each), way, i, first, count))
-        return found
-
-    near_pieces = pieces_of(known(AG_NEAR), near_all, 0, chunk)
-    common = (near_cols, sources, per_row, layout, cols)
-    if SPLIT and far_way == "pair":
-        early = near_pieces + pieces_of(far_way, far_all, chunk, per_row - chunk, (0, 1, 2))
-        late = pieces_of(far_way, far_all, chunk, per_row - chunk, (3,))
-        (before,) = spread_back(meta, tile_weights, early, None, *common, False)
-        keep, send = spread_back(meta, tile_weights, late, before, *common, True)
-    else:
-        every = near_pieces + pieces_of(far_way, far_all, chunk, per_row - chunk)
-        keep, send = spread_back(meta, tile_weights, every, None, *common, True)
-    grad_features = (keep + swap_cores(send).astype(F32)).astype(BF16)
-
-    quarter = weight_sums(known(AG_FAR), far_all, near_cols, lines, packed, hidden)
+    quarter = part[0]
+    for s in range(1, chips):
+        quarter = quarter + from_chip(part[chips - s], s)
+    width_in = coming.shape[1] // hidden
+    packed = -(-lines // width_in)
+    extra = jnp.pad(quarter.astype(BF16), ((0, width_in * packed - lines), (0, 0)))
+    extra = jnp.concatenate([extra[k * packed : (k + 1) * packed] for k in range(width_in)], axis=1)
+    extra = jnp.pad(extra, ((0, -packed % 8), (0, 0)))
+    tall = near_cols + extra.shape[0]
+    far_all = lax.all_gather(jnp.concatenate([coming, extra], axis=0), "rows", axis=0, tiled=True)
+
+    way = "pair" if paired else "direct"
+    pieces = [(array, 0, way, i, 0, chunk) for i, array in enumerate(near_all)]
+    pieces += [(far_all, i * tall, "all", i, chunk, per_row - chunk) for i in range(n_rows)]
+    keep, send = spread_back(
+        meta, tile_weights, pieces, near_cols, sources, per_row, layout, cols
+    )
+    got = swap_cores(send)
+    quarter = weight_sums(far_all, n_rows, near_cols, lines, packed, hidden)
     half = [quarter] + [from_chip(quarter, s) for s in range(1, chips)]
-    other_half = swap_cores(jnp.stack(half))
-    grad_weight, grad_bias = assemble(half, [other_half[s] for s in range(chips)], cols, chips)
+    other = swap_cores(jnp.stack(half))
+    grad_features, grad_weight, grad_bias = assemble(
+        keep, got, half, [other[s] for s in range(chips)], cols, chips
+    )
     return (activation, grad_features, grad_weight, grad_bias.reshape(hidden))
 
 

time: 88.5 us -> 87.3 us (0.986)
  waiting for transfers between devices: 21.7 us -> 19.3 us
  starting transfers between devices: 22 us -> 24.2 us
  Pallas kernels: 17 us -> 18.7 us
  blocking collectives: 22.1 us -> 21 us
    ppermute x4, waiting for transfers between devices: 2.18 us -> 0.01 us  [from_chip(): return lax.ppermute(value, 'wide', pairs)]
    pallas_call x2, Pallas kernels: 3.89 us -> 5.19 us  [the longest x1 4.27 us: spread_back(): call(body, 'spread_back', [jax.ShapeDtypeStruct((cols, sources * BLK), F3...]
    ppermute x4, waiting for transfers between devices: 2.75 us -> 1.47 us  [swap_cores(): return lax.ppermute(value, 'wide', [(i, i ^ 1) for i in range(wide)])]
    ppermute x8, starting transfers between devices: 15.2 us -> 16.4 us  [the longest x5 12.7 us: beside(): return lax.ppermute(value, 'rows', [(i, i ^ 1) for i in range(n_rows)])]
    all_gather x1, blocking collectives: 22.1 us -> 21 us  [per_device(): lax.all_gather(jnp.concatenate([coming, extra], axis=0), 'rows', axis=0,...]
    ppermute x8, waiting for transfers between devices: 16.8 us -> 17.9 us  [the longest x3 10.5 us: across(): return lax.ppermute(value, 'rows', [(i, i ^ 2) for i in range(n_rows)])]
    ppermute x4, starting transfers between devices: 5.59 us -> 6.63 us  [from_chip(): return lax.ppermute(value, 'wide', pairs)]
  transfers between devices with their start and end apart: 16 -> 16, of which waited for: 9 -> 7; matrix products, arithmetic and copies ran while one was open for 1% -> 1% of each run, Pallas kernels for 13% -> 14%
where the time goes in v5:
time: 87.3 us; the launch traced here: 86.8 us
  starting transfers between devices  24.2 us (28%)
  blocking collectives  21 us (24%)
  waiting for transfers between devices  19.3 us (22%)
  Pallas kernels  18.7 us (21%)
  between operations  1.47 us (2%)
  local copies, waits for them, and re-layouts  1.05 us (1%)
  other arithmetic  1.02 us (1%)
    all_gather x1, blocking collectives, per_device(): lax.all_gather(jnp.concatenate([coming, extra], axis=0), 'rows', axis=0,...  21 us
    ppermute x5, starting transfers between devices, beside(): return lax.ppermute(value, 'rows', [(i, i ^ 1) for i in range(n_rows)])  12.7 us
    pallas_call x3, Pallas kernels, aggregate(): call(body, 'aggregate', shapes, [SMEM_SPEC, HBM_SPEC, HBM_SPEC] + [VMEM_S...  11.1 us
    ppermute x3, waiting for transfers between devices, across(): return lax.ppermute(value, 'rows', [(i, i ^ 2) for i in range(n_rows)])  10.5 us
    ppermute x5, waiting for transfers between devices, beside(): return lax.ppermute(value, 'rows', [(i, i ^ 1) for i in range(n_rows)])  7.34 us
    ppermute x4, starting transfers between devices, from_chip(): return lax.ppermute(value, 'wide', pairs)  6.63 us
    pallas_call x1, Pallas kernels, spread_back(): call(body, 'spread_back', [jax.ShapeDtypeStruct((cols, sources * BLK), F3...  4.27 us
    ppermute x3, starting transfers between devices, across(): return lax.ppermute(value, 'rows', [(i, i ^ 2) for i in range(n_rows)])  3.72 us
  transfers between devices with their start and end apart: 16, of which 7 were waited for; matrix products, arithmetic and copies ran while one was open for 1% of the time, Pallas kernels for 14%

profile of v5, /device:TPU:0, one launch (start us, length us, event | category | flops | bytes accessed | tf_op | source)
XLA Modules:
  0.0 86.8 jit_solution(17174988681657509152)
XLA Ops:
  0.6 0.5 collective-permute-start
  1.8 0.8 and_select_fusion.meta_ref
  2.6 0.1 collective-permute-done.refs_0_
  2.7 0.0 copy-start
  2.7 1.0 %copy-done = bf16[64,3072]{1,0:T(8,128)(2,1)S(1)} copy-done((bf16[64,3072]{1,0:T(8,128)(2,1)S(1)}, bf16[64,3072]{1,0:T(8,128)(2,1)}, u32[]{:S(2)}) %copy-start) | copy-done | bytes 393240
  3.7 3.5 %aggregate.5 = bf16[1536,128]{1,0:T(8,128)(2,1)S(1)} custom-call(s32[240]{0:T(256)S(1)} %and_select_fusion.meta_ref, bf16[240,128,128]{2,1,0:T(8,128)(2,1)} %tiles_ref.7, bf16[64,3072]{1,0:T(8,128)(2,1)S(1)} %copy-done, bf16[64,3072]{1,0:T(8,128)(2,1)S(1)} %collective-permute-done.refs_0_), custom_call_target="tpu_custom_call" | custom-call | flops 503316480 | bytes 3932160 | tf_op jit(solution)/shard_map/aggregate/pallas_call | solution.py:174
  7.2 0.0 copy-start.3
  7.3 0.0 copy-start.1
  7.3 0.0 copy-start.2
  7.3 3.0 %collective-permute-start.2 = (bf16[1536,128]{1,0:T(8,128)(2,1)S(1)}, bf16[1536,128]{1,0:T(8,128)(2,1)S(1)}, u32[]{:S(2)}, u32[]{:S(2)}) collective-permute-start(bf16[1536,128]{1,0:T(8,128)(2,1)S(1)} %aggregate.5), channel_id=1, source_target_pairs={{0,1},{1,0},{2,3},{3,2},{4,5},{5,4},{6,7},{7,6},{8,9},{9,8},{10,11... | collective-permute-start | bytes 1179656 | tf_op jit(solution)/shard_map/ppermute | solution.py:427
  10.2 3.9 %aggregate.4 = (bf16[768,128]{1,0:T(8,128)(2,1)S(1)}, bf16[768,128]{1,0:T(8,128)(2,1)S(1)}, bf16[768,128]{1,0:T(8,128)(2,1)S(1)}, bf16[768,128]{1,0:T(8,128)(2,1)S(1)}) custom-call(s32[240]{0:T(256)S(1)} %and_select_fusion.meta_ref, bf16[240,128,128]{2,1,0:T(8,128)(2,1)} %tiles_ref.7, bf16[64,3072]{1,0:T(8,128)(2,1)S(1)} %copy-done, ...), custom_call_target="tpu_custom_call" | custom-call | flops 503316480 | bytes 3932160 | tf_op jit(solution)/shard_map/aggregate/pallas_call | solution.py:174
  14.2 0.1 collective-permute-start.4
  14.3 5.9 %collective-permute-done.2 = bf16[1536,128]{1,0:T(8,128)(2,1)S(1)} collective-permute-done((bf16[1536,128]{1,0:T(8,128)(2,1)S(1)}, bf16[1536,128]{1,0:T(8,128)(2,1)S(1)}, u32[]{:S(2)}, u32[]{:S(2)}) %collective-permute-start.2) | collective-permute-done | bytes 393248 | tf_op jit(solution)/shard_map/ppermute | solution.py:427
  20.1 0.1 add_convert_fusion.1
  20.3 3.1 %collective-permute-start.5 = (bf16[768,128]{1,0:T(8,128)(2,1)S(1)}, bf16[768,128]{1,0:T(8,128)(2,1)S(1)}, u32[]{:S(2)}, u32[]{:S(2)}) collective-permute-start(bf16[768,128]{1,0:T(8,128)(2,1)S(1)} %get-tuple-element.40), channel_id=1, source_target_pairs={{0,2},{1,3},{2,0},{3,1},{4,6},{5,7},{6,4},{7,5},{8,10},{9,11},{10,... | collective-permute-start | bytes 589832 | tf_op jit(solution)/shard_map/ppermute | solution.py:430
  23.4 1.9 %collective-permute-start.1 = (bf16[768,128]{1,0:T(8,128)(2,1)S(1)}, bf16[768,128]{1,0:T(8,128)(2,1)S(1)}, u32[]{:S(2)}, u32[]{:S(2)}) collective-permute-start(bf16[768,128]{1,0:T(8,128)(2,1)S(1)} %get-tuple-element.23), channel_id=1, source_target_pairs={{0,1},{1,0},{2,3},{3,2},{4,5},{5,4},{6,7},{7,6},{8,9},{9,8},{10,11... | collective-permute-start | bytes 589832 | tf_op jit(solution)/shard_map/ppermute | solution.py:427
  25.3 3.6 %aggregate.3 = (f32[768,128]{1,0:T(8,128)S(1)}, f32[768,128]{1,0:T(8,128)S(1)}) custom-call(s32[240]{0:T(256)S(1)} %and_select_fusion.meta_ref, bf16[240,128,128]{2,1,0:T(8,128)(2,1)} %tiles_ref.7, bf16[64,3072]{1,0:T(8,128)(2,1)S(1)} %copy-done, bf16[64,3072]{1,0:T(8,128)(2,1)S(1)} %collective-permute-done.refs_0_), custom_call_target="tpu_custom_call" | custom-call | flops 503316480 | bytes 3932160 | tf_op jit(solution)/shard_map/aggregate/pallas_call | solution.py:174
  28.9 0.5 collective-permute-start.3
  29.4 0.0 collective-permute-done.4
  29.4 2.6 %collective-permute-done.5 = bf16[768,128]{1,0:T(8,128)(2,1)S(1)} collective-permute-done((bf16[768,128]{1,0:T(8,128)(2,1)S(1)}, bf16[768,128]{1,0:T(8,128)(2,1)S(1)}, u32[]{:S(2)}, u32[]{:S(2)}) %collective-permute-start.5) | collective-permute-done | bytes 196640 | tf_op jit(solution)/shard_map/ppermute | solution.py:430
  32.0 0.1 add_convert_fusion
  32.1 2.0 %collective-permute-start.6 = (bf16[768,128]{1,0:T(8,128)(2,1)S(1)}, bf16[768,128]{1,0:T(8,128)(2,1)S(1)}, u32[]{:S(2)}, u32[]{:S(2)}) collective-permute-start(bf16[768,128]{1,0:T(8,128)(2,1)S(1)} %add_convert_fusion), channel_id=1, source_target_pairs={{8,0},{12,4},{0,8},{4,12},{9,1},{13,5},{1,9},{5,13},{10,2},{14,6},... | collective-permute-start | bytes 589832 | tf_op jit(solution)/shard_map/ppermute | solution.py:421
  34.1 0.0 copy-done.3
  34.1 1.4 %collective-permute-done.1.refs_1_ = bf16[768,128]{1,0:T(8,128)(2,1)S(1)} collective-permute-done((bf16[768,128]{1,0:T(8,128)(2,1)S(1)}, bf16[768,128]{1,0:T(8,128)(2,1)S(1)}, u32[]{:S(2)}, u32[]{:S(2)}) %collective-permute-start.1) | collective-permute-done | bytes 196640 | tf_op jit(solution)/shard_map/ppermute | solution.py:427
  35.5 4.3 %collective-permute-done.3.refs_2_ = bf16[768,128]{1,0:T(8,128)(2,1)S(1)} collective-permute-done((bf16[768,128]{1,0:T(8,128)(2,1)S(1)}, bf16[768,128]{1,0:T(8,128)(2,1)S(1)}, u32[]{:S(2)}, u32[]{:S(2)}) %collective-permute-start.3) | collective-permute-done | bytes 196640 | tf_op jit(solution)/shard_map/ppermute | solution.py:430
  39.9 0.0 collective-permute-done.6.refs_3_
  39.9 0.0 copy-done.1
  39.9 0.0 copy-done.2
  39.9 2.1 %layer.1 = (bf16[768,256]{1,0:T(8,128)(2,1)}, bf16[128,768]{1,0:T(8,128)(2,1)S(1)}, bf16[128,768]{1,0:T(8,128)(2,1)S(1)}, bf16[768,128]{1,0:T(8,128)(2,1)S(1)}, ...) custom-call(f32[768,128]{1,0:T(8,128)S(1)} %get-tuple-element.22.refs_0_, ...), custom_call_target="tpu_custom_call" | custom-call | flops 201326592 | bytes 1966080 | tf_op jit(solution)/shard_map/layer/pallas_call | solution.py:298
  41.9 0.3 weight_parts.1
  42.3 0.1 collective-permute-start.11
  42.3 0.1 collective-permute-start.8
  42.4 1.8 %collective-permute-start.9 = (bf16[128,768]{1,0:T(8,128)(2,1)S(1)}, bf16[128,768]{1,0:T(8,128)(2,1)S(1)}, u32[]{:S(2)}, u32[]{:S(2)}) collective-permute-start(bf16[128,768]{1,0:T(8,128)(2,1)S(1)} %get-tuple-element.30), channel_id=1, source_target_pairs={{8,0},{12,4},{0,8},{4,12},{9,1},{13,5},{1,9},{5,13},{10,2},{14,6},... | collective-permute-start | bytes 589832 | tf_op jit(solution)/shard_map/ppermute | solution.py:421
  44.2 0.0 collective-permute-done.11
  44.3 1.3 %collective-permute-start.12 = (f32[72,256]{1,0:T(8,128)S(1)}, f32[72,256]{1,0:T(8,128)S(1)}, u32[]{:S(2)}, u32[]{:S(2)}) collective-permute-start(f32[72,256]{1,0:T(8,128)S(1)} %slice_bitcast_fusion.4), channel_id=1, source_target_pairs={{8,0},{12,4},{0,8},{4,12},{9,1},{13,5},{1,9},{5,13},{10,2},{14,6},... | collective-permute-start | bytes 221192 | tf_op jit(solution)/shard_map/ppermute | solution.py:421
  45.5 5.7 %collective-permute-start.7 = (bf16[128,768]{1,0:T(8,128)(2,1)S(1)}, bf16[128,768]{1,0:T(8,128)(2,1)S(1)}, u32[]{:S(2)}, u32[]{:S(2)}) collective-permute-start(bf16[128,768]{1,0:T(8,128)(2,1)S(1)} %get-tuple-element.29.refs_0_), channel_id=1, source_target_pairs={{0,1},{1,0},{2,3},{3,2},{4,5},{5,4},{6,7},{7,6},{8,9},{9,8},{10,11... | collective-permute-start | bytes 589832 | tf_op jit(solution)/shard_map/ppermute | solution.py:427
  51.3 3.6 %collective-permute-done.8.refs_2_ = bf16[128,768]{1,0:T(8,128)(2,1)S(1)} collective-permute-done((bf16[128,768]{1,0:T(8,128)(2,1)S(1)}, bf16[128,768]{1,0:T(8,128)(2,1)S(1)}, u32[]{:S(2)}, u32[]{:S(2)}) %collective-permute-start.8) | collective-permute-done | bytes 196640 | tf_op jit(solution)/shard_map/ppermute | solution.py:430
  54.9 0.0 collective-permute-done.9
  54.9 2.0 %collective-permute-start.10 = (bf16[128,768]{1,0:T(8,128)(2,1)S(1)}, bf16[128,768]{1,0:T(8,128)(2,1)S(1)}, u32[]{:S(2)}, u32[]{:S(2)}) collective-permute-start(bf16[128,768]{1,0:T(8,128)(2,1)S(1)} %collective-permute-done.8.refs_2_), channel_id=1, source_target_pairs={{0,1},{1,0},{2,3},{3,2},{4,5},{5,4},{6,7},{7,6},{8,9},{9,8},{10,11... | collective-permute-start | bytes 589832 | tf_op jit(solution)/shard_map/ppermute | solution.py:427
  56.9 0.0 collective-permute-done.12
  56.9 21.0 %all_gather.3.refs_4_.ref = bf16[608,768]{1,0:T(8,128)(2,1)S(1)} all-gather(bf16[152,768]{1,0:T(8,128)(2,1)S(1)} %maximum_maximum_fusion), channel_id=1, replica_groups=mesh['groups'=2,'wide'=4,'rows'=4] {'rows'}, dimensions={0}, use_global_device_ids=true | all-gather | bytes 1167360 | tf_op jit(solution)/shard_map/all_gather | solution.py:505
  78.0 1.6 %collective-permute-start.14 = (f32[72,256]{1,0:T(8,128)S(1)}, f32[72,256]{1,0:T(8,128)S(1)}, u32[]{:S(2)}, u32[]{:S(2)}) collective-permute-start(f32[72,256]{1,0:T(8,128)S(1)} %weight_sums.1.refs_0_), channel_id=1, source_target_pairs={{8,0},{12,4},{0,8},{4,12},{9,1},{13,5},{1,9},{5,13},{10,2},{14,6},... | collective-permute-start | bytes 221192 | tf_op jit(solution)/shard_map/ppermute | solution.py:421
  79.6 0.0 collective-permute-done.7.refs_1_
  79.6 0.0 collective-permute-done.10.refs_3_
  79.6 4.3 %spread_back.1 = (f32[64,3072]{1,0:T(8,128)S(1)}, bf16[64,3072]{1,0:T(8,128)(2,1)S(1)}) custom-call(s32[240]{0:T(256)S(1)} %and_select_fusion.meta_ref, bf16[240,128,128]{2,1,0:T(8,128)(2,1)} %tiles_ref.7, bf16[128,768]{1,0:T(8,128)(2,1)S(1)} %get-tuple-element.29.refs_0_, bf16[128,768]{1,0:T(8,128)(2,1)S(1)} %collective-permute-done.7.refs_1_, ...), custom_call_target="tpu_custom_call" | custom-call | flops 503316480 | bytes 3932160 | tf_op jit(solution)/shard_map/spread_back/pallas_call | solution.py:232
  83.8 0.1 collective-permute-start.13
  83.9 0.0 collective-permute-done.14.refs_1_
  84.0 0.5 collective-permute-start.15
  84.5 1.3 %collective-permute-done.15 = f32[2,72,256]{2,1,0:T(8,128)S(1)} collective-permute-done((f32[2,72,256]{2,1,0:T(8,128)S(1)}, f32[2,72,256]{2,1,0:T(8,128)S(1)}, u32[]{:S(2)}, u32[]{:S(2)}) %collective-permute-start.15) | collective-permute-done | bytes 147488 | tf_op jit(solution)/shard_map/ppermute | solution.py:417
  85.9 0.0 collective-permute-done.13.got_ref
  85.9 0.9 %assemble.1 = (bf16[64,3072]{1,0:T(8,128)(2,1)}, f32[256,256]{1,0:T(8,128)}, f32[1,256]{1,0:T(1,128)}) custom-call(f32[64,3072]{1,0:T(8,128)S(1)} %get-tuple-element.35.keep_ref, bf16[64,3072]{1,0:T(8,128)(2,1)S(1)} %collective-permute-done.13.got_ref, f32[72,256]{1,0:T(8,128)S(1)} %weight_sums.1.refs_0_, f32[72,256]{1,0:T(8,128)S(1)} %collective-permute-done.14.refs_1_, ...), custom_call_target="tpu_custom_call" | custom-call | bytes 262144 | tf_op jit(solution)/shard_map/assemble/pallas_call | solution.py:384
  (10 shorter events, 0.1 us)
Async XLA Ops:
  0.6 2.1 %collective-permute-start = (bf16[64,3072]{1,0:T(8,128)(2,1)}, bf16[64,3072]{1,0:T(8,128)(2,1)S(1)}, u32[]{:S(2)}, u32[]{:S(2)}) collective-permute-start(bf16[64,3072]{1,0:T(8,128)(2,1)} %own_ref.5), channel_id=1, source_target_pairs={{0,4},{4,0},{8,12},{12,8},{1,5},{5,1},{9,13},{13,9},{2,6},{6,2},{1... | collective-permute-start | bytes 1179656 | tf_op jit(solution)/shard_map/ppermute | solution.py:417
  2.7 1.0 %copy-start = (bf16[64,3072]{1,0:T(8,128)(2,1)S(1)}, bf16[64,3072]{1,0:T(8,128)(2,1)}, u32[]{:S(2)}) copy-start(bf16[64,3072]{1,0:T(8,128)(2,1)} %own_ref.5) | copy-start | bytes 1179652
  7.2 26.8 %copy-start.3 = (bf16[256]{0:T(256)(128)(2,1)S(1)}, bf16[256]{0:T(256)(128)(2,1)}, u32[]{:S(2)}) copy-start(bf16[256]{0:T(256)(128)(2,1)} %param.14) | copy-start | bytes 1540
  7.3 32.6 %copy-start.1 = (bf16[768,256]{1,0:T(8,128)(2,1)S(1)}, bf16[768,256]{1,0:T(8,128)(2,1)}, u32[]{:S(2)}) copy-start(bf16[768,256]{1,0:T(8,128)(2,1)} %refs_6_.1) | copy-start | bytes 1179652
  7.3 32.6 %copy-start.2 = (bf16[256,256]{1,0:T(8,128)(2,1)S(1)}, bf16[256,256]{1,0:T(8,128)(2,1)}, u32[]{:S(2)}) copy-start(bf16[256,256]{1,0:T(8,128)(2,1)} %refs_4_.1) | copy-start | bytes 393220
  7.3 12.9 %collective-permute-start.2 = (bf16[1536,128]{1,0:T(8,128)(2,1)S(1)}, bf16[1536,128]{1,0:T(8,128)(2,1)S(1)}, u32[]{:S(2)}, u32[]{:S(2)}) collective-permute-start(bf16[1536,128]{1,0:T(8,128)(2,1)S(1)} %aggregate.5), channel_id=1, source_target_pairs={{0,1},{1,0},{2,3},{3,2},{4,5},{5,4},{6,7},{7,6},{8,9},{9,8},{10,11... | collective-permute-start | bytes 1179656 | tf_op jit(solution)/shard_map/ppermute | solution.py:427
  14.2 15.2 %collective-permute-start.4 = (bf16[768,128]{1,0:T(8,128)(2,1)S(1)}, bf16[768,128]{1,0:T(8,128)(2,1)S(1)}, u32[]{:S(2)}, u32[]{:S(2)}) collective-permute-start(bf16[768,128]{1,0:T(8,128)(2,1)S(1)} %get-tuple-element.26), channel_id=1, source_target_pairs={{0,1},{1,0},{2,3},{3,2},{4,5},{5,4},{6,7},{7,6},{8,9},{9,8},{10,11... | collective-permute-start | bytes 589832 | tf_op jit(solution)/shard_map/ppermute | solution.py:427
  20.3 11.7 %collective-permute-start.5 = (bf16[768,128]{1,0:T(8,128)(2,1)S(1)}, bf16[768,128]{1,0:T(8,128)(2,1)S(1)}, u32[]{:S(2)}, u32[]{:S(2)}) collective-permute-start(bf16[768,128]{1,0:T(8,128)(2,1)S(1)} %get-tuple-element.40), channel_id=1, source_target_pairs={{0,2},{1,3},{2,0},{3,1},{4,6},{5,7},{6,4},{7,5},{8,10},{9,11},{10,... | collective-permute-start | bytes 589832 | tf_op jit(solution)/shard_map/ppermute | solution.py:430
  23.4 12.2 %collective-permute-start.1 = (bf16[768,128]{1,0:T(8,128)(2,1)S(1)}, bf16[768,128]{1,0:T(8,128)(2,1)S(1)}, u32[]{:S(2)}, u32[]{:S(2)}) collective-permute-start(bf16[768,128]{1,0:T(8,128)(2,1)S(1)} %get-tuple-element.23), channel_id=1, source_target_pairs={{0,1},{1,0},{2,3},{3,2},{4,5},{5,4},{6,7},{7,6},{8,9},{9,8},{10,11... | collective-permute-start | bytes 589832 | tf_op jit(solution)/shard_map/ppermute | solution.py:427
  28.9 11.0 %collective-permute-start.3 = (bf16[768,128]{1,0:T(8,128)(2,1)S(1)}, bf16[768,128]{1,0:T(8,128)(2,1)S(1)}, u32[]{:S(2)}, u32[]{:S(2)}) collective-permute-start(bf16[768,128]{1,0:T(8,128)(2,1)S(1)} %get-tuple-element.41), channel_id=1, source_target_pairs={{0,2},{1,3},{2,0},{3,1},{4,6},{5,7},{6,4},{7,5},{8,10},{9,11},{10,... | collective-permute-start | bytes 589832 | tf_op jit(solution)/shard_map/ppermute | solution.py:430
  32.1 7.8 %collective-permute-start.6 = (bf16[768,128]{1,0:T(8,128)(2,1)S(1)}, bf16[768,128]{1,0:T(8,128)(2,1)S(1)}, u32[]{:S(2)}, u32[]{:S(2)}) collective-permute-start(bf16[768,128]{1,0:T(8,128)(2,1)S(1)} %add_convert_fusion), channel_id=1, source_target_pairs={{8,0},{12,4},{0,8},{4,12},{9,1},{13,5},{1,9},{5,13},{10,2},{14,6},... | collective-permute-start | bytes 589832 | tf_op jit(solution)/shard_map/ppermute | solution.py:421
  42.3 1.9 %collective-permute-start.11 = (f32[2,72,256]{2,1,0:T(8,128)S(1)}, f32[2,72,256]{2,1,0:T(8,128)S(1)}, u32[]{:S(2)}, u32[]{:S(2)}) collective-permute-start(f32[2,72,256]{2,1,0:T(8,128)S(1)} %slice_bitcast_fusion), channel_id=1, source_target_pairs={{0,4},{4,0},{8,12},{12,8},{1,5},{5,1},{9,13},{13,9},{2,6},{6,2},{1... | collective-permute-start | bytes 442376 | tf_op jit(solution)/shard_map/ppermute | solution.py:417
  42.3 12.5 %collective-permute-start.8 = (bf16[128,768]{1,0:T(8,128)(2,1)S(1)}, bf16[128,768]{1,0:T(8,128)(2,1)S(1)}, u32[]{:S(2)}, u32[]{:S(2)}) collective-permute-start(bf16[128,768]{1,0:T(8,128)(2,1)S(1)} %get-tuple-element.29.refs_0_), channel_id=1, source_target_pairs={{0,2},{1,3},{2,0},{3,1},{4,6},{5,7},{6,4},{7,5},{8,10},{9,11},{10,... | collective-permute-start | bytes 589832 | tf_op jit(solution)/shard_map/ppermute | solution.py:430
  42.4 12.5 %collective-permute-start.9 = (bf16[128,768]{1,0:T(8,128)(2,1)S(1)}, bf16[128,768]{1,0:T(8,128)(2,1)S(1)}, u32[]{:S(2)}, u32[]{:S(2)}) collective-permute-start(bf16[128,768]{1,0:T(8,128)(2,1)S(1)} %get-tuple-element.30), channel_id=1, source_target_pairs={{8,0},{12,4},{0,8},{4,12},{9,1},{13,5},{1,9},{5,13},{10,2},{14,6},... | collective-permute-start | bytes 589832 | tf_op jit(solution)/shard_map/ppermute | solution.py:421
  44.3 12.6 %collective-permute-start.12 = (f32[72,256]{1,0:T(8,128)S(1)}, f32[72,256]{1,0:T(8,128)S(1)}, u32[]{:S(2)}, u32[]{:S(2)}) collective-permute-start(f32[72,256]{1,0:T(8,128)S(1)} %slice_bitcast_fusion.4), channel_id=1, source_target_pairs={{8,0},{12,4},{0,8},{4,12},{9,1},{13,5},{1,9},{5,13},{10,2},{14,6},... | collective-permute-start | bytes 221192 | tf_op jit(solution)/shard_map/ppermute | solution.py:421
  45.5 34.0 %collective-permute-start.7 = (bf16[128,768]{1,0:T(8,128)(2,1)S(1)}, bf16[128,768]{1,0:T(8,128)(2,1)S(1)}, u32[]{:S(2)}, u32[]{:S(2)}) collective-permute-start(bf16[128,768]{1,0:T(8,128)(2,1)S(1)} %get-tuple-element.29.refs_0_), channel_id=1, source_target_pairs={{0,1},{1,0},{2,3},{3,2},{4,5},{5,4},{6,7},{7,6},{8,9},{9,8},{10,11... | collective-permute-start | bytes 589832 | tf_op jit(solution)/shard_map/ppermute | solution.py:427
  54.9 24.7 %collective-permute-start.10 = (bf16[128,768]{1,0:T(8,128)(2,1)S(1)}, bf16[128,768]{1,0:T(8,128)(2,1)S(1)}, u32[]{:S(2)}, u32[]{:S(2)}) collective-permute-start(bf16[128,768]{1,0:T(8,128)(2,1)S(1)} %collective-permute-done.8.refs_2_), channel_id=1, source_target_pairs={{0,1},{1,0},{2,3},{3,2},{4,5},{5,4},{6,7},{7,6},{8,9},{9,8},{10,11... | collective-permute-start | bytes 589832 | tf_op jit(solution)/shard_map/ppermute | solution.py:427
  78.0 5.9 %collective-permute-start.14 = (f32[72,256]{1,0:T(8,128)S(1)}, f32[72,256]{1,0:T(8,128)S(1)}, u32[]{:S(2)}, u32[]{:S(2)}) collective-permute-start(f32[72,256]{1,0:T(8,128)S(1)} %weight_sums.1.refs_0_), channel_id=1, source_target_pairs={{8,0},{12,4},{0,8},{4,12},{9,1},{13,5},{1,9},{5,13},{10,2},{14,6},... | collective-permute-start | bytes 221192 | tf_op jit(solution)/shard_map/ppermute | solution.py:421
  83.8 2.0 %collective-permute-start.13 = (bf16[64,3072]{1,0:T(8,128)(2,1)S(1)}, bf16[64,3072]{1,0:T(8,128)(2,1)S(1)}, u32[]{:S(2)}, u32[]{:S(2)}) collective-permute-start(bf16[64,3072]{1,0:T(8,128)(2,1)S(1)} %get-tuple-element.36), channel_id=1, source_target_pairs={{0,4},{4,0},{8,12},{12,8},{1,5},{5,1},{9,13},{13,9},{2,6},{6,2},{1... | collective-permute-start | bytes 1179656 | tf_op jit(solution)/shard_map/ppermute | solution.py:417
  84.0 1.9 %collective-permute-start.15 = (f32[2,72,256]{2,1,0:T(8,128)S(1)}, f32[2,72,256]{2,1,0:T(8,128)S(1)}, u32[]{:S(2)}, u32[]{:S(2)}) collective-permute-start(f32[2,72,256]{2,1,0:T(8,128)S(1)} %pad_maximum_fusion), channel_id=1, source_target_pairs={{0,4},{4,0},{8,12},{12,8},{1,5},{5,1},{9,13},{13,9},{2,6},{6,2},{1... | collective-permute-start | bytes 442376 | tf_op jit(solution)/shard_map/ppermute | solution.py:417

commit v6 on v5

--- a/solution.py
+++ b/solution.py
@@ -117,8 +117,9 @@
     n_rows, per_row = lax.axis_size("rows"), cuts[-1]
     dead = n_rows * per_row
     pieces = list(zip(cuts[:-1], cuts[1:]))
+    kept = (0, 2) if way == "pair" else (0,)
     shapes = [
-        jax.ShapeDtypeStruct(((high - low) * BLK, columns), F32 if i == 0 else BF16)
+        jax.ShapeDtypeStruct(((high - low) * BLK, columns), F32 if i in kept else BF16)
         for i in owners
         for low, high in pieces
     ]

time: 87.3 us -> 87 us (level); the launches traced: 86.8 us -> 85.6 us
  Pallas kernels: 18.7 us -> 17.2 us
    ppermute x5, starting transfers between devices: 12.7 us -> 10.8 us  [beside(): return lax.ppermute(value, 'rows', [(i, i ^ 1) for i in range(n_rows)])]
    ppermute x5, waiting for transfers between devices: 7.34 us -> 5.83 us  [beside(): return lax.ppermute(value, 'rows', [(i, i ^ 1) for i in range(n_rows)])]
    ppermute x3, waiting for transfers between devices: 10.5 us -> 11.8 us  [across(): return lax.ppermute(value, 'rows', [(i, i ^ 2) for i in range(n_rows)])]
    ppermute x3, starting transfers between devices: 3.72 us -> 4.96 us  [across(): return lax.ppermute(value, 'rows', [(i, i ^ 2) for i in range(n_rows)])]
  transfers between devices with their start and end apart: 16 -> 16, of which waited for: 7 -> 6; matrix products, arithmetic and copies ran while one was open for 1% -> 1% of each run, Pallas kernels for 14% -> 12%
where the time goes in v6:
time: 87 us; the launch traced here: 85.6 us
  starting transfers between devices  24.5 us (28%)
  blocking collectives  21.2 us (24%)
  waiting for transfers between devices  19.2 us (22%)
  Pallas kernels  17.2 us (20%)
  between operations  1.47 us (2%)
  local copies, waits for them, and re-layouts  1.05 us (1%)
  other arithmetic  0.99 us (1%)
    all_gather x1, blocking collectives, per_device(): lax.all_gather(jnp.concatenate([coming, extra], axis=0), 'rows', axis=0,...  21.2 us
    ppermute x3, waiting for transfers between devices, across(): return lax.ppermute(value, 'rows', [(i, i ^ 2) for i in range(n_rows)])  11.8 us
    ppermute x5, starting transfers between devices, beside(): return lax.ppermute(value, 'rows', [(i, i ^ 1) for i in range(n_rows)])  10.8 us
    pallas_call x3, Pallas kernels, aggregate(): call(body, 'aggregate', shapes, [SMEM_SPEC, HBM_SPEC, HBM_SPEC] + [VMEM_S...  10.4 us
    ppermute x4, starting transfers between devices, from_chip(): return lax.ppermute(value, 'wide', pairs)  7.48 us
    ppermute x5, waiting for transfers between devices, beside(): return lax.ppermute(value, 'rows', [(i, i ^ 1) for i in range(n_rows)])  5.83 us
    ppermute x3, starting transfers between devices, across(): return lax.ppermute(value, 'rows', [(i, i ^ 2) for i in range(n_rows)])  4.96 us
    pallas_call x1, Pallas kernels, spread_back(): call(body, 'spread_back', [jax.ShapeDtypeStruct((cols, sources * BLK), F3...  3.51 us
  transfers between devices with their start and end apart: 16, of which 6 were waited for; matrix products, arithmetic and copies ran while one was open for 1% of the time, Pallas kernels for 12%

profile of v6, /device:TPU:0, one launch (start us, length us, event | category | flops | bytes accessed | tf_op | source)
XLA Modules:
  0.0 85.6 jit_solution(16836953516219702649)
XLA Ops:
  0.6 0.5 collective-permute-start
  1.8 0.8 and_select_fusion.meta_ref
  2.6 0.1 collective-permute-done.refs_0_
  2.7 0.0 copy-start
  2.7 1.0 %copy-done = bf16[64,3072]{1,0:T(8,128)(2,1)S(1)} copy-done((bf16[64,3072]{1,0:T(8,128)(2,1)S(1)}, bf16[64,3072]{1,0:T(8,128)(2,1)}, u32[]{:S(2)}) %copy-start) | copy-done | bytes 393240
  3.7 3.6 %aggregate.5 = bf16[1536,128]{1,0:T(8,128)(2,1)S(1)} custom-call(s32[240]{0:T(256)S(1)} %and_select_fusion.meta_ref, bf16[240,128,128]{2,1,0:T(8,128)(2,1)} %tiles_ref.7, bf16[64,3072]{1,0:T(8,128)(2,1)S(1)} %copy-done, bf16[64,3072]{1,0:T(8,128)(2,1)S(1)} %collective-permute-done.refs_0_), custom_call_target="tpu_custom_call" | custom-call | flops 503316480 | bytes 3932160 | tf_op jit(solution)/shard_map/aggregate/pallas_call | solution.py:175
  7.3 0.0 copy-start.3
  7.3 0.0 copy-start.1
  7.4 0.0 copy-start.2
  7.4 1.8 %collective-permute-start.2 = (bf16[1536,128]{1,0:T(8,128)(2,1)S(1)}, bf16[1536,128]{1,0:T(8,128)(2,1)S(1)}, u32[]{:S(2)}, u32[]{:S(2)}) collective-permute-start(bf16[1536,128]{1,0:T(8,128)(2,1)S(1)} %aggregate.5), channel_id=1, source_target_pairs={{0,1},{1,0},{2,3},{3,2},{4,5},{5,4},{6,7},{7,6},{8,9},{9,8},{10,11... | collective-permute-start | bytes 1179656 | tf_op jit(solution)/shard_map/ppermute | solution.py:428
  9.2 3.1 %aggregate.4 = (bf16[768,128]{1,0:T(8,128)(2,1)S(1)}, bf16[768,128]{1,0:T(8,128)(2,1)S(1)}, f32[768,128]{1,0:T(8,128)S(1)}, f32[768,128]{1,0:T(8,128)S(1)}) custom-call(s32[240]{0:T(256)S(1)} %and_select_fusion.meta_ref, bf16[240,128,128]{2,1,0:T(8,128)(2,1)} %tiles_ref.7, bf16[64,3072]{1,0:T(8,128)(2,1)S(1)} %copy-done, ...), custom_call_target="tpu_custom_call" | custom-call | flops 503316480 | bytes 3932160 | tf_op jit(solution)/shard_map/aggregate/pallas_call | solution.py:175
  12.3 1.2 %collective-permute-start.4 = (bf16[768,128]{1,0:T(8,128)(2,1)S(1)}, bf16[768,128]{1,0:T(8,128)(2,1)S(1)}, u32[]{:S(2)}, u32[]{:S(2)}) collective-permute-start(bf16[768,128]{1,0:T(8,128)(2,1)S(1)} %get-tuple-element.26), channel_id=1, source_target_pairs={{0,1},{1,0},{2,3},{3,2},{4,5},{5,4},{6,7},{7,6},{8,9},{9,8},{10,11... | collective-permute-start | bytes 589832 | tf_op jit(solution)/shard_map/ppermute | solution.py:428
  13.5 5.8 %collective-permute-done.2 = bf16[1536,128]{1,0:T(8,128)(2,1)S(1)} collective-permute-done((bf16[1536,128]{1,0:T(8,128)(2,1)S(1)}, bf16[1536,128]{1,0:T(8,128)(2,1)S(1)}, u32[]{:S(2)}, u32[]{:S(2)}) %collective-permute-start.2) | collective-permute-done | bytes 393248 | tf_op jit(solution)/shard_map/ppermute | solution.py:428
  19.4 0.1 add_convert_fusion.1
  19.4 3.8 %collective-permute-start.5 = (bf16[768,128]{1,0:T(8,128)(2,1)S(1)}, bf16[768,128]{1,0:T(8,128)(2,1)S(1)}, u32[]{:S(2)}, u32[]{:S(2)}) collective-permute-start(bf16[768,128]{1,0:T(8,128)(2,1)S(1)} %get-tuple-element.40), channel_id=1, source_target_pairs={{0,2},{1,3},{2,0},{3,1},{4,6},{5,7},{6,4},{7,5},{8,10},{9,11},{10,... | collective-permute-start | bytes 589832 | tf_op jit(solution)/shard_map/ppermute | solution.py:431
  23.3 1.7 %collective-permute-start.1 = (bf16[768,128]{1,0:T(8,128)(2,1)S(1)}, bf16[768,128]{1,0:T(8,128)(2,1)S(1)}, u32[]{:S(2)}, u32[]{:S(2)}) collective-permute-start(bf16[768,128]{1,0:T(8,128)(2,1)S(1)} %get-tuple-element.23), channel_id=1, source_target_pairs={{0,1},{1,0},{2,3},{3,2},{4,5},{5,4},{6,7},{7,6},{8,9},{9,8},{10,11... | collective-permute-start | bytes 589832 | tf_op jit(solution)/shard_map/ppermute | solution.py:428
  24.9 3.7 %aggregate.3 = (f32[768,128]{1,0:T(8,128)S(1)}, f32[768,128]{1,0:T(8,128)S(1)}) custom-call(s32[240]{0:T(256)S(1)} %and_select_fusion.meta_ref, bf16[240,128,128]{2,1,0:T(8,128)(2,1)} %tiles_ref.7, bf16[64,3072]{1,0:T(8,128)(2,1)S(1)} %copy-done, bf16[64,3072]{1,0:T(8,128)(2,1)S(1)} %collective-permute-done.refs_0_), custom_call_target="tpu_custom_call" | custom-call | flops 503316480 | bytes 3932160 | tf_op jit(solution)/shard_map/aggregate/pallas_call | solution.py:175
  28.7 1.0 %collective-permute-start.3 = (bf16[768,128]{1,0:T(8,128)(2,1)S(1)}, bf16[768,128]{1,0:T(8,128)(2,1)S(1)}, u32[]{:S(2)}, u32[]{:S(2)}) collective-permute-start(bf16[768,128]{1,0:T(8,128)(2,1)S(1)} %get-tuple-element.41), channel_id=1, source_target_pairs={{0,2},{1,3},{2,0},{3,1},{4,6},{5,7},{6,4},{7,5},{8,10},{9,11},{10,... | collective-permute-start | bytes 589832 | tf_op jit(solution)/shard_map/ppermute | solution.py:431
  29.7 0.0 collective-permute-done.4
  29.7 2.3 %collective-permute-done.5 = bf16[768,128]{1,0:T(8,128)(2,1)S(1)} collective-permute-done((bf16[768,128]{1,0:T(8,128)(2,1)S(1)}, bf16[768,128]{1,0:T(8,128)(2,1)S(1)}, u32[]{:S(2)}, u32[]{:S(2)}) %collective-permute-start.5) | collective-permute-done | bytes 196640 | tf_op jit(solution)/shard_map/ppermute | solution.py:431
  32.0 0.1 add_convert_fusion
  32.1 2.4 %collective-permute-start.6 = (bf16[768,128]{1,0:T(8,128)(2,1)S(1)}, bf16[768,128]{1,0:T(8,128)(2,1)S(1)}, u32[]{:S(2)}, u32[]{:S(2)}) collective-permute-start(bf16[768,128]{1,0:T(8,128)(2,1)S(1)} %add_convert_fusion), channel_id=1, source_target_pairs={{8,0},{12,4},{0,8},{4,12},{9,1},{13,5},{1,9},{5,13},{10,2},{14,6},... | collective-permute-start | bytes 589832 | tf_op jit(solution)/shard_map/ppermute | solution.py:422
  34.5 0.0 copy-done.3
  34.5 0.0 collective-permute-done.1.refs_1_
  34.5 5.3 %collective-permute-done.3.refs_2_ = bf16[768,128]{1,0:T(8,128)(2,1)S(1)} collective-permute-done((bf16[768,128]{1,0:T(8,128)(2,1)S(1)}, bf16[768,128]{1,0:T(8,128)(2,1)S(1)}, u32[]{:S(2)}, u32[]{:S(2)}) %collective-permute-start.3) | collective-permute-done | bytes 196640 | tf_op jit(solution)/shard_map/ppermute | solution.py:431
  39.7 0.0 collective-permute-done.6.refs_3_
  39.7 0.0 copy-done.1
  39.7 0.0 copy-done.2
  39.7 2.1 %layer.1 = (bf16[768,256]{1,0:T(8,128)(2,1)}, bf16[128,768]{1,0:T(8,128)(2,1)S(1)}, bf16[128,768]{1,0:T(8,128)(2,1)S(1)}, bf16[768,128]{1,0:T(8,128)(2,1)S(1)}, ...) custom-call(f32[768,128]{1,0:T(8,128)S(1)} %get-tuple-element.22.refs_0_, ...), custom_call_target="tpu_custom_call" | custom-call | flops 201326592 | bytes 1966080 | tf_op jit(solution)/shard_map/layer/pallas_call | solution.py:299
  41.8 0.3 weight_parts.1
  42.1 0.1 collective-permute-start.11
  42.2 0.1 collective-permute-start.8
  42.3 2.0 %collective-permute-start.9 = (bf16[128,768]{1,0:T(8,128)(2,1)S(1)}, bf16[128,768]{1,0:T(8,128)(2,1)S(1)}, u32[]{:S(2)}, u32[]{:S(2)}) collective-permute-start(bf16[128,768]{1,0:T(8,128)(2,1)S(1)} %get-tuple-element.30), channel_id=1, source_target_pairs={{8,0},{12,4},{0,8},{4,12},{9,1},{13,5},{1,9},{5,13},{10,2},{14,6},... | collective-permute-start | bytes 589832 | tf_op jit(solution)/shard_map/ppermute | solution.py:422
  44.3 0.0 collective-permute-done.11
  44.3 1.3 %collective-permute-start.12 = (f32[72,256]{1,0:T(8,128)S(1)}, f32[72,256]{1,0:T(8,128)S(1)}, u32[]{:S(2)}, u32[]{:S(2)}) collective-permute-start(f32[72,256]{1,0:T(8,128)S(1)} %slice_bitcast_fusion.4), channel_id=1, source_target_pairs={{8,0},{12,4},{0,8},{4,12},{9,1},{13,5},{1,9},{5,13},{10,2},{14,6},... | collective-permute-start | bytes 221192 | tf_op jit(solution)/shard_map/ppermute | solution.py:422
  45.6 4.8 %collective-permute-start.7 = (bf16[128,768]{1,0:T(8,128)(2,1)S(1)}, bf16[128,768]{1,0:T(8,128)(2,1)S(1)}, u32[]{:S(2)}, u32[]{:S(2)}) collective-permute-start(bf16[128,768]{1,0:T(8,128)(2,1)S(1)} %get-tuple-element.29.refs_0_), channel_id=1, source_target_pairs={{0,1},{1,0},{2,3},{3,2},{4,5},{5,4},{6,7},{7,6},{8,9},{9,8},{10,11... | collective-permute-start | bytes 589832 | tf_op jit(solution)/shard_map/ppermute | solution.py:428
  50.4 4.3 %collective-permute-done.8.refs_2_ = bf16[128,768]{1,0:T(8,128)(2,1)S(1)} collective-permute-done((bf16[128,768]{1,0:T(8,128)(2,1)S(1)}, bf16[128,768]{1,0:T(8,128)(2,1)S(1)}, u32[]{:S(2)}, u32[]{:S(2)}) %collective-permute-start.8) | collective-permute-done | bytes 196640 | tf_op jit(solution)/shard_map/ppermute | solution.py:431
  54.7 0.0 collective-permute-done.9
  54.7 1.3 %collective-permute-start.10 = (bf16[128,768]{1,0:T(8,128)(2,1)S(1)}, bf16[128,768]{1,0:T(8,128)(2,1)S(1)}, u32[]{:S(2)}, u32[]{:S(2)}) collective-permute-start(bf16[128,768]{1,0:T(8,128)(2,1)S(1)} %collective-permute-done.8.refs_2_), channel_id=1, source_target_pairs={{0,1},{1,0},{2,3},{3,2},{4,5},{5,4},{6,7},{7,6},{8,9},{9,8},{10,11... | collective-permute-start | bytes 589832 | tf_op jit(solution)/shard_map/ppermute | solution.py:428
  56.0 0.0 collective-permute-done.12
  56.1 21.2 %all_gather.3.refs_4_.ref = bf16[608,768]{1,0:T(8,128)(2,1)S(1)} all-gather(bf16[152,768]{1,0:T(8,128)(2,1)S(1)} %maximum_maximum_fusion), channel_id=1, replica_groups=mesh['groups'=2,'wide'=4,'rows'=4] {'rows'}, dimensions={0}, use_global_device_ids=true | all-gather | bytes 1167360 | tf_op jit(solution)/shard_map/all_gather | solution.py:506
  77.3 1.8 %collective-permute-start.14 = (f32[72,256]{1,0:T(8,128)S(1)}, f32[72,256]{1,0:T(8,128)S(1)}, u32[]{:S(2)}, u32[]{:S(2)}) collective-permute-start(f32[72,256]{1,0:T(8,128)S(1)} %weight_sums.1.refs_0_), channel_id=1, source_target_pairs={{8,0},{12,4},{0,8},{4,12},{9,1},{13,5},{1,9},{5,13},{10,2},{14,6},... | collective-permute-start | bytes 221192 | tf_op jit(solution)/shard_map/ppermute | solution.py:422
  79.1 0.0 collective-permute-done.7.refs_1_
  79.1 0.0 collective-permute-done.10.refs_3_
  79.1 3.5 %spread_back.1 = (f32[64,3072]{1,0:T(8,128)S(1)}, bf16[64,3072]{1,0:T(8,128)(2,1)S(1)}) custom-call(s32[240]{0:T(256)S(1)} %and_select_fusion.meta_ref, bf16[240,128,128]{2,1,0:T(8,128)(2,1)} %tiles_ref.7, bf16[128,768]{1,0:T(8,128)(2,1)S(1)} %get-tuple-element.29.refs_0_, bf16[128,768]{1,0:T(8,128)(2,1)S(1)} %collective-permute-done.7.refs_1_, ...), custom_call_target="tpu_custom_call" | custom-call | flops 503316480 | bytes 3932160 | tf_op jit(solution)/shard_map/spread_back/pallas_call | solution.py:233
  82.6 0.1 collective-permute-start.13
  82.7 0.0 collective-permute-done.14.refs_1_
  82.7 0.5 collective-permute-start.15
  83.3 1.3 %collective-permute-done.15 = f32[2,72,256]{2,1,0:T(8,128)S(1)} collective-permute-done((f32[2,72,256]{2,1,0:T(8,128)S(1)}, f32[2,72,256]{2,1,0:T(8,128)S(1)}, u32[]{:S(2)}, u32[]{:S(2)}) %collective-permute-start.15) | collective-permute-done | bytes 147488 | tf_op jit(solution)/shard_map/ppermute | solution.py:418
  84.6 0.0 collective-permute-done.13.got_ref
  84.7 0.9 %assemble.1 = (bf16[64,3072]{1,0:T(8,128)(2,1)}, f32[256,256]{1,0:T(8,128)}, f32[1,256]{1,0:T(1,128)}) custom-call(f32[64,3072]{1,0:T(8,128)S(1)} %get-tuple-element.35.keep_ref, bf16[64,3072]{1,0:T(8,128)(2,1)S(1)} %collective-permute-done.13.got_ref, f32[72,256]{1,0:T(8,128)S(1)} %weight_sums.1.refs_0_, f32[72,256]{1,0:T(8,128)S(1)} %collective-permute-done.14.refs_1_, ...), custom_call_target="tpu_custom_call" | custom-call | bytes 262144 | tf_op jit(solution)/shard_map/assemble/pallas_call | solution.py:385
  (10 shorter events, 0.1 us)
Async XLA Ops:
  0.6 2.1 %collective-permute-start = (bf16[64,3072]{1,0:T(8,128)(2,1)}, bf16[64,3072]{1,0:T(8,128)(2,1)S(1)}, u32[]{:S(2)}, u32[]{:S(2)}) collective-permute-start(bf16[64,3072]{1,0:T(8,128)(2,1)} %own_ref.5), channel_id=1, source_target_pairs={{0,4},{4,0},{8,12},{12,8},{1,5},{5,1},{9,13},{13,9},{2,6},{6,2},{1... | collective-permute-start | bytes 1179656 | tf_op jit(solution)/shard_map/ppermute | solution.py:418
  2.7 1.0 %copy-start = (bf16[64,3072]{1,0:T(8,128)(2,1)S(1)}, bf16[64,3072]{1,0:T(8,128)(2,1)}, u32[]{:S(2)}) copy-start(bf16[64,3072]{1,0:T(8,128)(2,1)} %own_ref.5) | copy-start | bytes 1179652
  7.3 27.1 %copy-start.3 = (bf16[256]{0:T(256)(128)(2,1)S(1)}, bf16[256]{0:T(256)(128)(2,1)}, u32[]{:S(2)}) copy-start(bf16[256]{0:T(256)(128)(2,1)} %param.14) | copy-start | bytes 1540
  7.3 32.4 %copy-start.1 = (bf16[768,256]{1,0:T(8,128)(2,1)S(1)}, bf16[768,256]{1,0:T(8,128)(2,1)}, u32[]{:S(2)}) copy-start(bf16[768,256]{1,0:T(8,128)(2,1)} %refs_6_.1) | copy-start | bytes 1179652
  7.4 32.4 %copy-start.2 = (bf16[256,256]{1,0:T(8,128)(2,1)S(1)}, bf16[256,256]{1,0:T(8,128)(2,1)}, u32[]{:S(2)}) copy-start(bf16[256,256]{1,0:T(8,128)(2,1)} %refs_4_.1) | copy-start | bytes 393220
  7.4 12.0 %collective-permute-start.2 = (bf16[1536,128]{1,0:T(8,128)(2,1)S(1)}, bf16[1536,128]{1,0:T(8,128)(2,1)S(1)}, u32[]{:S(2)}, u32[]{:S(2)}) collective-permute-start(bf16[1536,128]{1,0:T(8,128)(2,1)S(1)} %aggregate.5), channel_id=1, source_target_pairs={{0,1},{1,0},{2,3},{3,2},{4,5},{5,4},{6,7},{7,6},{8,9},{9,8},{10,11... | collective-permute-start | bytes 1179656 | tf_op jit(solution)/shard_map/ppermute | solution.py:428
  12.3 17.4 %collective-permute-start.4 = (bf16[768,128]{1,0:T(8,128)(2,1)S(1)}, bf16[768,128]{1,0:T(8,128)(2,1)S(1)}, u32[]{:S(2)}, u32[]{:S(2)}) collective-permute-start(bf16[768,128]{1,0:T(8,128)(2,1)S(1)} %get-tuple-element.26), channel_id=1, source_target_pairs={{0,1},{1,0},{2,3},{3,2},{4,5},{5,4},{6,7},{7,6},{8,9},{9,8},{10,11... | collective-permute-start | bytes 589832 | tf_op jit(solution)/shard_map/ppermute | solution.py:428
  19.4 12.5 %collective-permute-start.5 = (bf16[768,128]{1,0:T(8,128)(2,1)S(1)}, bf16[768,128]{1,0:T(8,128)(2,1)S(1)}, u32[]{:S(2)}, u32[]{:S(2)}) collective-permute-start(bf16[768,128]{1,0:T(8,128)(2,1)S(1)} %get-tuple-element.40), channel_id=1, source_target_pairs={{0,2},{1,3},{2,0},{3,1},{4,6},{5,7},{6,4},{7,5},{8,10},{9,11},{10,... | collective-permute-start | bytes 589832 | tf_op jit(solution)/shard_map/ppermute | solution.py:431
  23.3 11.2 %collective-permute-start.1 = (bf16[768,128]{1,0:T(8,128)(2,1)S(1)}, bf16[768,128]{1,0:T(8,128)(2,1)S(1)}, u32[]{:S(2)}, u32[]{:S(2)}) collective-permute-start(bf16[768,128]{1,0:T(8,128)(2,1)S(1)} %get-tuple-element.23), channel_id=1, source_target_pairs={{0,1},{1,0},{2,3},{3,2},{4,5},{5,4},{6,7},{7,6},{8,9},{9,8},{10,11... | collective-permute-start | bytes 589832 | tf_op jit(solution)/shard_map/ppermute | solution.py:428
  28.7 11.0 %collective-permute-start.3 = (bf16[768,128]{1,0:T(8,128)(2,1)S(1)}, bf16[768,128]{1,0:T(8,128)(2,1)S(1)}, u32[]{:S(2)}, u32[]{:S(2)}) collective-permute-start(bf16[768,128]{1,0:T(8,128)(2,1)S(1)} %get-tuple-element.41), channel_id=1, source_target_pairs={{0,2},{1,3},{2,0},{3,1},{4,6},{5,7},{6,4},{7,5},{8,10},{9,11},{10,... | collective-permute-start | bytes 589832 | tf_op jit(solution)/shard_map/ppermute | solution.py:431
  32.1 7.7 %collective-permute-start.6 = (bf16[768,128]{1,0:T(8,128)(2,1)S(1)}, bf16[768,128]{1,0:T(8,128)(2,1)S(1)}, u32[]{:S(2)}, u32[]{:S(2)}) collective-permute-start(bf16[768,128]{1,0:T(8,128)(2,1)S(1)} %add_convert_fusion), channel_id=1, source_target_pairs={{8,0},{12,4},{0,8},{4,12},{9,1},{13,5},{1,9},{5,13},{10,2},{14,6},... | collective-permute-start | bytes 589832 | tf_op jit(solution)/shard_map/ppermute | solution.py:422
  42.1 2.1 %collective-permute-start.11 = (f32[2,72,256]{2,1,0:T(8,128)S(1)}, f32[2,72,256]{2,1,0:T(8,128)S(1)}, u32[]{:S(2)}, u32[]{:S(2)}) collective-permute-start(f32[2,72,256]{2,1,0:T(8,128)S(1)} %slice_bitcast_fusion), channel_id=1, source_target_pairs={{0,4},{4,0},{8,12},{12,8},{1,5},{5,1},{9,13},{13,9},{2,6},{6,2},{1... | collective-permute-start | bytes 442376 | tf_op jit(solution)/shard_map/ppermute | solution.py:418
  42.2 12.5 %collective-permute-start.8 = (bf16[128,768]{1,0:T(8,128)(2,1)S(1)}, bf16[128,768]{1,0:T(8,128)(2,1)S(1)}, u32[]{:S(2)}, u32[]{:S(2)}) collective-permute-start(bf16[128,768]{1,0:T(8,128)(2,1)S(1)} %get-tuple-element.29.refs_0_), channel_id=1, source_target_pairs={{0,2},{1,3},{2,0},{3,1},{4,6},{5,7},{6,4},{7,5},{8,10},{9,11},{10,... | collective-permute-start | bytes 589832 | tf_op jit(solution)/shard_map/ppermute | solution.py:431
  42.3 12.5 %collective-permute-start.9 = (bf16[128,768]{1,0:T(8,128)(2,1)S(1)}, bf16[128,768]{1,0:T(8,128)(2,1)S(1)}, u32[]{:S(2)}, u32[]{:S(2)}) collective-permute-start(bf16[128,768]{1,0:T(8,128)(2,1)S(1)} %get-tuple-element.30), channel_id=1, source_target_pairs={{8,0},{12,4},{0,8},{4,12},{9,1},{13,5},{1,9},{5,13},{10,2},{14,6},... | collective-permute-start | bytes 589832 | tf_op jit(solution)/shard_map/ppermute | solution.py:422
  44.3 11.7 %collective-permute-start.12 = (f32[72,256]{1,0:T(8,128)S(1)}, f32[72,256]{1,0:T(8,128)S(1)}, u32[]{:S(2)}, u32[]{:S(2)}) collective-permute-start(f32[72,256]{1,0:T(8,128)S(1)} %slice_bitcast_fusion.4), channel_id=1, source_target_pairs={{8,0},{12,4},{0,8},{4,12},{9,1},{13,5},{1,9},{5,13},{10,2},{14,6},... | collective-permute-start | bytes 221192 | tf_op jit(solution)/shard_map/ppermute | solution.py:422
  45.6 33.5 %collective-permute-start.7 = (bf16[128,768]{1,0:T(8,128)(2,1)S(1)}, bf16[128,768]{1,0:T(8,128)(2,1)S(1)}, u32[]{:S(2)}, u32[]{:S(2)}) collective-permute-start(bf16[128,768]{1,0:T(8,128)(2,1)S(1)} %get-tuple-element.29.refs_0_), channel_id=1, source_target_pairs={{0,1},{1,0},{2,3},{3,2},{4,5},{5,4},{6,7},{7,6},{8,9},{9,8},{10,11... | collective-permute-start | bytes 589832 | tf_op jit(solution)/shard_map/ppermute | solution.py:428
  54.7 24.4 %collective-permute-start.10 = (bf16[128,768]{1,0:T(8,128)(2,1)S(1)}, bf16[128,768]{1,0:T(8,128)(2,1)S(1)}, u32[]{:S(2)}, u32[]{:S(2)}) collective-permute-start(bf16[128,768]{1,0:T(8,128)(2,1)S(1)} %collective-permute-done.8.refs_2_), channel_id=1, source_target_pairs={{0,1},{1,0},{2,3},{3,2},{4,5},{5,4},{6,7},{7,6},{8,9},{9,8},{10,11... | collective-permute-start | bytes 589832 | tf_op jit(solution)/shard_map/ppermute | solution.py:428
  77.3 5.4 %collective-permute-start.14 = (f32[72,256]{1,0:T(8,128)S(1)}, f32[72,256]{1,0:T(8,128)S(1)}, u32[]{:S(2)}, u32[]{:S(2)}) collective-permute-start(f32[72,256]{1,0:T(8,128)S(1)} %weight_sums.1.refs_0_), channel_id=1, source_target_pairs={{8,0},{12,4},{0,8},{4,12},{9,1},{13,5},{1,9},{5,13},{10,2},{14,6},... | collective-permute-start | bytes 221192 | tf_op jit(solution)/shard_map/ppermute | solution.py:422
  82.6 2.0 %collective-permute-start.13 = (bf16[64,3072]{1,0:T(8,128)(2,1)S(1)}, bf16[64,3072]{1,0:T(8,128)(2,1)S(1)}, u32[]{:S(2)}, u32[]{:S(2)}) collective-permute-start(bf16[64,3072]{1,0:T(8,128)(2,1)S(1)} %get-tuple-element.36), channel_id=1, source_target_pairs={{0,4},{4,0},{8,12},{12,8},{1,5},{5,1},{9,13},{13,9},{2,6},{6,2},{1... | collective-permute-start | bytes 1179656 | tf_op jit(solution)/shard_map/ppermute | solution.py:418
  82.7 1.9 %collective-permute-start.15 = (f32[2,72,256]{2,1,0:T(8,128)S(1)}, f32[2,72,256]{2,1,0:T(8,128)S(1)}, u32[]{:S(2)}, u32[]{:S(2)}) collective-permute-start(f32[2,72,256]{2,1,0:T(8,128)S(1)} %pad_maximum_fusion), channel_id=1, source_target_pairs={{0,4},{4,0},{8,12},{12,8},{1,5},{5,1},{9,13},{13,9},{2,6},{6,2},{1... | collective-permute-start | bytes 442376 | tf_op jit(solution)/shard_map/ppermute | solution.py:418

commit v7 on v6

--- a/solution.py
+++ b/solution.py
@@ -125,16 +125,13 @@
     ]
     many = len(owners) == n_rows
 
-    def body(meta_ref, tiles_ref, own_ref, *refs):
-        part_refs = refs[: len(parts) - 1]
-        outs = refs[len(parts) - 1 : len(parts) - 1 + len(shapes)]
-        own, own_sem, turned, total, picked, ring, sems = refs[len(parts) - 1 + len(shapes) :]
-        fetch = pltpu.make_async_copy(own_ref, own, own_sem)
-        fetch.start()
+    def body(meta_ref, tiles_ref, *refs):
+        part_refs = refs[: len(parts)]
+        outs = refs[len(parts) : len(parts) + len(shapes)]
+        turned, total, picked, ring, sems = refs[len(parts) + len(shapes) :]
         rows = [row_at(way, i) for i in owners]
 
         def prepare():
-            fetch.wait()
             if many:
                 total[...] = jnp.zeros_like(total)
             else:
@@ -143,7 +140,7 @@
                     total[pl.ds(row * per_row, per_row)] = jnp.zeros((per_row, BLK, columns), F32)
             for s in range(sources):
                 now = slice(s * BLK, (s + 1) * BLK)
-                block = jnp.concatenate([own[:, now]] + [ref[:, now] for ref in part_refs], axis=0)
+                block = jnp.concatenate([ref[:, now] for ref in part_refs], axis=0)
                 turned[s] = jnp.transpose(block)
 
         def multiply(entry, tile):
@@ -176,10 +173,8 @@
         body,
         "aggregate",
         shapes,
-        [SMEM_SPEC, HBM_SPEC, HBM_SPEC] + [VMEM_SPEC] * (len(parts) - 1),
+        [SMEM_SPEC, HBM_SPEC] + [VMEM_SPEC] * len(parts),
         [
-            pltpu.VMEM(parts[0].shape, BF16),
-            pltpu.SemaphoreType.DMA,
             pltpu.VMEM((sources, BLK, columns), BF16),
             pltpu.VMEM((dead + 1, BLK, columns), F32),
         ]

time: 87 us -> 88.6 us (1.018)
  starting transfers between devices: 24.5 us -> 21.4 us
  Pallas kernels: 17.2 us -> 20 us
  waiting for transfers between devices: 19.2 us -> 21.3 us
    ppermute x5, starting transfers between devices: 10.8 us -> 8.71 us  [beside(): return lax.ppermute(value, 'rows', [(i, i ^ 1) for i in range(n_rows)])]
    pallas_call x1, Pallas kernels: 3.51 us -> 5.64 us  [spread_back(): call(body, 'spread_back', [jax.ShapeDtypeStruct((cols, sources * BLK), F3...]
    ppermute x3, waiting for transfers between devices: 11.8 us -> 13.7 us  [across(): return lax.ppermute(value, 'rows', [(i, i ^ 2) for i in range(n_rows)])]
  transfers between devices with their start and end apart: 16 -> 16, of which waited for: 6 -> 6; matrix products, arithmetic and copies ran while one was open for 1% -> 1% of each run, Pallas kernels for 12% -> 15%
where the time goes in v7:
time: 88.6 us; the launch traced here: 87.4 us
  starting transfers between devices  21.4 us (24%)
  waiting for transfers between devices  21.3 us (24%)
  blocking collectives  21.2 us (24%)
  Pallas kernels  20 us (23%)
  between operations  1.48 us (2%)
  local copies, waits for them, and re-layouts  1.05 us (1%)
  other arithmetic  0.99 us (1%)
    all_gather x1, blocking collectives, per_device(): lax.all_gather(jnp.concatenate([coming, extra], axis=0), 'rows', axis=0,...  21.2 us
    ppermute x3, waiting for transfers between devices, across(): return lax.ppermute(value, 'rows', [(i, i ^ 2) for i in range(n_rows)])  13.7 us
    pallas_call x3, Pallas kernels, aggregate(): call(body, 'aggregate', shapes, [SMEM_SPEC, HBM_SPEC] + [VMEM_SPEC] * len...  11 us
    ppermute x5, starting transfers between devices, beside(): return lax.ppermute(value, 'rows', [(i, i ^ 1) for i in range(n_rows)])  8.71 us
    ppermute x4, starting transfers between devices, from_chip(): return lax.ppermute(value, 'wide', pairs)  7.29 us
    ppermute x5, waiting for transfers between devices, beside(): return lax.ppermute(value, 'rows', [(i, i ^ 1) for i in range(n_rows)])  6.07 us
    pallas_call x1, Pallas kernels, spread_back(): call(body, 'spread_back', [jax.ShapeDtypeStruct((cols, sources * BLK), F3...  5.64 us
    ppermute x3, starting transfers between devices, across(): return lax.ppermute(value, 'rows', [(i, i ^ 2) for i in range(n_rows)])  4.21 us
  transfers between devices with their start and end apart: 16, of which 6 were waited for; matrix products, arithmetic and copies ran while one was open for 1% of the time, Pallas kernels for 15%

profile of v7, /device:TPU:0, one launch (start us, length us, event | category | flops | bytes accessed | tf_op | source)
XLA Modules:
  0.0 87.4 jit_solution(16223969130013227307)
XLA Ops:
  0.6 0.5 collective-permute-start
  1.8 0.8 and_select_fusion.meta_ref
  2.6 0.1 collective-permute-done.refs_1_
  2.7 0.0 copy-start
  2.7 1.0 %copy-done = bf16[64,3072]{1,0:T(8,128)(2,1)S(1)} copy-done((bf16[64,3072]{1,0:T(8,128)(2,1)S(1)}, bf16[64,3072]{1,0:T(8,128)(2,1)}, u32[]{:S(2)}) %copy-start) | copy-done | bytes 393240
  3.7 3.3 %aggregate.5 = bf16[1536,128]{1,0:T(8,128)(2,1)S(1)} custom-call(s32[240]{0:T(256)S(1)} %and_select_fusion.meta_ref, bf16[240,128,128]{2,1,0:T(8,128)(2,1)} %tiles_ref.7, bf16[64,3072]{1,0:T(8,128)(2,1)S(1)} %copy-done, bf16[64,3072]{1,0:T(8,128)(2,1)S(1)} %collective-permute-done.refs_1_), custom_call_target="tpu_custom_call" | custom-call | flops 503316480 | bytes 3932160 | tf_op jit(solution)/shard_map/aggregate/pallas_call | solution.py:172
  7.0 0.0 copy-start.3
  7.0 0.0 copy-start.1
  7.0 0.0 copy-start.2
  7.0 2.0 %collective-permute-start.2 = (bf16[1536,128]{1,0:T(8,128)(2,1)S(1)}, bf16[1536,128]{1,0:T(8,128)(2,1)S(1)}, u32[]{:S(2)}, u32[]{:S(2)}) collective-permute-start(bf16[1536,128]{1,0:T(8,128)(2,1)S(1)} %aggregate.5), channel_id=1, source_target_pairs={{0,1},{1,0},{2,3},{3,2},{4,5},{5,4},{6,7},{7,6},{8,9},{9,8},{10,11... | collective-permute-start | bytes 1179656 | tf_op jit(solution)/shard_map/ppermute | solution.py:423
  9.0 3.5 %aggregate.4 = (bf16[768,128]{1,0:T(8,128)(2,1)S(1)}, bf16[768,128]{1,0:T(8,128)(2,1)S(1)}, f32[768,128]{1,0:T(8,128)S(1)}, f32[768,128]{1,0:T(8,128)S(1)}) custom-call(s32[240]{0:T(256)S(1)} %and_select_fusion.meta_ref, bf16[240,128,128]{2,1,0:T(8,128)(2,1)} %tiles_ref.7, bf16[64,3072]{1,0:T(8,128)(2,1)S(1)} %copy-done, ...), custom_call_target="tpu_custom_call" | custom-call | flops 503316480 | bytes 3932160 | tf_op jit(solution)/shard_map/aggregate/pallas_call | solution.py:172
  12.6 0.4 collective-permute-start.4
  13.0 6.1 %collective-permute-done.2 = bf16[1536,128]{1,0:T(8,128)(2,1)S(1)} collective-permute-done((bf16[1536,128]{1,0:T(8,128)(2,1)S(1)}, bf16[1536,128]{1,0:T(8,128)(2,1)S(1)}, u32[]{:S(2)}, u32[]{:S(2)}) %collective-permute-start.2) | collective-permute-done | bytes 393248 | tf_op jit(solution)/shard_map/ppermute | solution.py:423
  19.0 0.1 add_convert_fusion.1
  19.1 4.1 %collective-permute-start.5 = (bf16[768,128]{1,0:T(8,128)(2,1)S(1)}, bf16[768,128]{1,0:T(8,128)(2,1)S(1)}, u32[]{:S(2)}, u32[]{:S(2)}) collective-permute-start(bf16[768,128]{1,0:T(8,128)(2,1)S(1)} %get-tuple-element.40), channel_id=1, source_target_pairs={{0,2},{1,3},{2,0},{3,1},{4,6},{5,7},{6,4},{7,5},{8,10},{9,11},{10,... | collective-permute-start | bytes 589832 | tf_op jit(solution)/shard_map/ppermute | solution.py:426
  23.2 0.5 collective-permute-start.1
  23.7 4.2 %aggregate.3 = (f32[768,128]{1,0:T(8,128)S(1)}, f32[768,128]{1,0:T(8,128)S(1)}) custom-call(s32[240]{0:T(256)S(1)} %and_select_fusion.meta_ref, bf16[240,128,128]{2,1,0:T(8,128)(2,1)} %tiles_ref.7, bf16[64,3072]{1,0:T(8,128)(2,1)S(1)} %copy-done, bf16[64,3072]{1,0:T(8,128)(2,1)S(1)} %collective-permute-done.refs_1_), custom_call_target="tpu_custom_call" | custom-call | flops 503316480 | bytes 3932160 | tf_op jit(solution)/shard_map/aggregate/pallas_call | solution.py:172
  28.0 0.1 collective-permute-start.3
  28.0 0.0 collective-permute-done.4
  28.0 3.9 %collective-permute-done.5 = bf16[768,128]{1,0:T(8,128)(2,1)S(1)} collective-permute-done((bf16[768,128]{1,0:T(8,128)(2,1)S(1)}, bf16[768,128]{1,0:T(8,128)(2,1)S(1)}, u32[]{:S(2)}, u32[]{:S(2)}) %collective-permute-start.5) | collective-permute-done | bytes 196640 | tf_op jit(solution)/shard_map/ppermute | solution.py:426
  31.9 0.1 add_convert_fusion
  32.0 2.2 %collective-permute-start.6 = (bf16[768,128]{1,0:T(8,128)(2,1)S(1)}, bf16[768,128]{1,0:T(8,128)(2,1)S(1)}, u32[]{:S(2)}, u32[]{:S(2)}) collective-permute-start(bf16[768,128]{1,0:T(8,128)(2,1)S(1)} %add_convert_fusion), channel_id=1, source_target_pairs={{8,0},{12,4},{0,8},{4,12},{9,1},{13,5},{1,9},{5,13},{10,2},{14,6},... | collective-permute-start | bytes 589832 | tf_op jit(solution)/shard_map/ppermute | solution.py:417
  34.2 0.0 copy-done.3
  34.2 0.0 collective-permute-done.1.refs_1_
  34.2 5.3 %collective-permute-done.3.refs_2_ = bf16[768,128]{1,0:T(8,128)(2,1)S(1)} collective-permute-done((bf16[768,128]{1,0:T(8,128)(2,1)S(1)}, bf16[768,128]{1,0:T(8,128)(2,1)S(1)}, u32[]{:S(2)}, u32[]{:S(2)}) %collective-permute-start.3) | collective-permute-done | bytes 196640 | tf_op jit(solution)/shard_map/ppermute | solution.py:426
  39.5 0.0 collective-permute-done.6.refs_3_
  39.5 0.0 copy-done.1
  39.5 0.0 copy-done.2
  39.5 2.1 %layer.1 = (bf16[768,256]{1,0:T(8,128)(2,1)}, bf16[128,768]{1,0:T(8,128)(2,1)S(1)}, bf16[128,768]{1,0:T(8,128)(2,1)S(1)}, bf16[768,128]{1,0:T(8,128)(2,1)S(1)}, ...) custom-call(f32[768,128]{1,0:T(8,128)S(1)} %get-tuple-element.22.refs_0_, ...), custom_call_target="tpu_custom_call" | custom-call | flops 201326592 | bytes 1966080 | tf_op jit(solution)/shard_map/layer/pallas_call | solution.py:294
  41.6 0.3 weight_parts.1
  41.9 0.1 collective-permute-start.11
  42.0 0.1 collective-permute-start.8
  42.1 1.9 %collective-permute-start.9 = (bf16[128,768]{1,0:T(8,128)(2,1)S(1)}, bf16[128,768]{1,0:T(8,128)(2,1)S(1)}, u32[]{:S(2)}, u32[]{:S(2)}) collective-permute-start(bf16[128,768]{1,0:T(8,128)(2,1)S(1)} %get-tuple-element.30), channel_id=1, source_target_pairs={{8,0},{12,4},{0,8},{4,12},{9,1},{13,5},{1,9},{5,13},{10,2},{14,6},... | collective-permute-start | bytes 589832 | tf_op jit(solution)/shard_map/ppermute | solution.py:417
  43.9 0.0 collective-permute-done.11
  44.0 1.3 %collective-permute-start.12 = (f32[72,256]{1,0:T(8,128)S(1)}, f32[72,256]{1,0:T(8,128)S(1)}, u32[]{:S(2)}, u32[]{:S(2)}) collective-permute-start(f32[72,256]{1,0:T(8,128)S(1)} %slice_bitcast_fusion.4), channel_id=1, source_target_pairs={{8,0},{12,4},{0,8},{4,12},{9,1},{13,5},{1,9},{5,13},{10,2},{14,6},... | collective-permute-start | bytes 221192 | tf_op jit(solution)/shard_map/ppermute | solution.py:417
  45.2 4.7 %collective-permute-start.7 = (bf16[128,768]{1,0:T(8,128)(2,1)S(1)}, bf16[128,768]{1,0:T(8,128)(2,1)S(1)}, u32[]{:S(2)}, u32[]{:S(2)}) collective-permute-start(bf16[128,768]{1,0:T(8,128)(2,1)S(1)} %get-tuple-element.29.refs_0_), channel_id=1, source_target_pairs={{0,1},{1,0},{2,3},{3,2},{4,5},{5,4},{6,7},{7,6},{8,9},{9,8},{10,11... | collective-permute-start | bytes 589832 | tf_op jit(solution)/shard_map/ppermute | solution.py:423
  50.0 4.5 %collective-permute-done.8.refs_2_ = bf16[128,768]{1,0:T(8,128)(2,1)S(1)} collective-permute-done((bf16[128,768]{1,0:T(8,128)(2,1)S(1)}, bf16[128,768]{1,0:T(8,128)(2,1)S(1)}, u32[]{:S(2)}, u32[]{:S(2)}) %collective-permute-start.8) | collective-permute-done | bytes 196640 | tf_op jit(solution)/shard_map/ppermute | solution.py:426
  54.5 0.0 collective-permute-done.9
  54.5 1.1 %collective-permute-start.10 = (bf16[128,768]{1,0:T(8,128)(2,1)S(1)}, bf16[128,768]{1,0:T(8,128)(2,1)S(1)}, u32[]{:S(2)}, u32[]{:S(2)}) collective-permute-start(bf16[128,768]{1,0:T(8,128)(2,1)S(1)} %collective-permute-done.8.refs_2_), channel_id=1, source_target_pairs={{0,1},{1,0},{2,3},{3,2},{4,5},{5,4},{6,7},{7,6},{8,9},{9,8},{10,11... | collective-permute-start | bytes 589832 | tf_op jit(solution)/shard_map/ppermute | solution.py:423
  55.6 0.0 collective-permute-done.12
  55.6 21.2 %all_gather.3.refs_4_.ref = bf16[608,768]{1,0:T(8,128)(2,1)S(1)} all-gather(bf16[152,768]{1,0:T(8,128)(2,1)S(1)} %maximum_maximum_fusion), channel_id=1, replica_groups=mesh['groups'=2,'wide'=4,'rows'=4] {'rows'}, dimensions={0}, use_global_device_ids=true | all-gather | bytes 1167360 | tf_op jit(solution)/shard_map/all_gather | solution.py:501
  76.9 2.0 %collective-permute-start.14 = (f32[72,256]{1,0:T(8,128)S(1)}, f32[72,256]{1,0:T(8,128)S(1)}, u32[]{:S(2)}, u32[]{:S(2)}) collective-permute-start(f32[72,256]{1,0:T(8,128)S(1)} %weight_sums.1.refs_0_), channel_id=1, source_target_pairs={{8,0},{12,4},{0,8},{4,12},{9,1},{13,5},{1,9},{5,13},{10,2},{14,6},... | collective-permute-start | bytes 221192 | tf_op jit(solution)/shard_map/ppermute | solution.py:417
  78.8 0.0 collective-permute-done.7.refs_1_
  78.8 0.0 collective-permute-done.10.refs_3_
  78.8 5.6 %spread_back.1 = (f32[64,3072]{1,0:T(8,128)S(1)}, bf16[64,3072]{1,0:T(8,128)(2,1)S(1)}) custom-call(s32[240]{0:T(256)S(1)} %and_select_fusion.meta_ref, bf16[240,128,128]{2,1,0:T(8,128)(2,1)} %tiles_ref.7, bf16[128,768]{1,0:T(8,128)(2,1)S(1)} %get-tuple-element.29.refs_0_, bf16[128,768]{1,0:T(8,128)(2,1)S(1)} %collective-permute-done.7.refs_1_, ...), custom_call_target="tpu_custom_call" | custom-call | flops 503316480 | bytes 3932160 | tf_op jit(solution)/shard_map/spread_back/pallas_call | solution.py:228
  84.5 0.1 collective-permute-start.13
  84.6 0.0 collective-permute-done.14.refs_1_
  84.6 0.5 collective-permute-start.15
  85.1 1.3 %collective-permute-done.15 = f32[2,72,256]{2,1,0:T(8,128)S(1)} collective-permute-done((f32[2,72,256]{2,1,0:T(8,128)S(1)}, f32[2,72,256]{2,1,0:T(8,128)S(1)}, u32[]{:S(2)}, u32[]{:S(2)}) %collective-permute-start.15) | collective-permute-done | bytes 147488 | tf_op jit(solution)/shard_map/ppermute | solution.py:413
  86.5 0.0 collective-permute-done.13.got_ref
  86.5 0.9 %assemble.1 = (bf16[64,3072]{1,0:T(8,128)(2,1)}, f32[256,256]{1,0:T(8,128)}, f32[1,256]{1,0:T(1,128)}) custom-call(f32[64,3072]{1,0:T(8,128)S(1)} %get-tuple-element.35.keep_ref, bf16[64,3072]{1,0:T(8,128)(2,1)S(1)} %collective-permute-done.13.got_ref, f32[72,256]{1,0:T(8,128)S(1)} %weight_sums.1.refs_0_, f32[72,256]{1,0:T(8,128)S(1)} %collective-permute-done.14.refs_1_, ...), custom_call_target="tpu_custom_call" | custom-call | bytes 262144 | tf_op jit(solution)/shard_map/assemble/pallas_call | solution.py:380
  (10 shorter events, 0.1 us)
Async XLA Ops:
  0.6 2.1 %collective-permute-start = (bf16[64,3072]{1,0:T(8,128)(2,1)}, bf16[64,3072]{1,0:T(8,128)(2,1)S(1)}, u32[]{:S(2)}, u32[]{:S(2)}) collective-permute-start(bf16[64,3072]{1,0:T(8,128)(2,1)} %refs_0_.5), channel_id=1, source_target_pairs={{0,4},{4,0},{8,12},{12,8},{1,5},{5,1},{9,13},{13,9},{2,6},{6,2},{1... | collective-permute-start | bytes 1179656 | tf_op jit(solution)/shard_map/ppermute | solution.py:413
  2.7 1.0 %copy-start = (bf16[64,3072]{1,0:T(8,128)(2,1)S(1)}, bf16[64,3072]{1,0:T(8,128)(2,1)}, u32[]{:S(2)}) copy-start(bf16[64,3072]{1,0:T(8,128)(2,1)} %refs_0_.5) | copy-start | bytes 1179652
  7.0 27.2 %copy-start.3 = (bf16[256]{0:T(256)(128)(2,1)S(1)}, bf16[256]{0:T(256)(128)(2,1)}, u32[]{:S(2)}) copy-start(bf16[256]{0:T(256)(128)(2,1)} %param.14) | copy-start | bytes 1540
  7.0 32.5 %copy-start.1 = (bf16[768,256]{1,0:T(8,128)(2,1)S(1)}, bf16[768,256]{1,0:T(8,128)(2,1)}, u32[]{:S(2)}) copy-start(bf16[768,256]{1,0:T(8,128)(2,1)} %refs_6_.1) | copy-start | bytes 1179652
  7.0 32.5 %copy-start.2 = (bf16[256,256]{1,0:T(8,128)(2,1)S(1)}, bf16[256,256]{1,0:T(8,128)(2,1)}, u32[]{:S(2)}) copy-start(bf16[256,256]{1,0:T(8,128)(2,1)} %refs_4_.1) | copy-start | bytes 393220
  7.0 12.0 %collective-permute-start.2 = (bf16[1536,128]{1,0:T(8,128)(2,1)S(1)}, bf16[1536,128]{1,0:T(8,128)(2,1)S(1)}, u32[]{:S(2)}, u32[]{:S(2)}) collective-permute-start(bf16[1536,128]{1,0:T(8,128)(2,1)S(1)} %aggregate.5), channel_id=1, source_target_pairs={{0,1},{1,0},{2,3},{3,2},{4,5},{5,4},{6,7},{7,6},{8,9},{9,8},{10,11... | collective-permute-start | bytes 1179656 | tf_op jit(solution)/shard_map/ppermute | solution.py:423
  12.6 15.5 %collective-permute-start.4 = (bf16[768,128]{1,0:T(8,128)(2,1)S(1)}, bf16[768,128]{1,0:T(8,128)(2,1)S(1)}, u32[]{:S(2)}, u32[]{:S(2)}) collective-permute-start(bf16[768,128]{1,0:T(8,128)(2,1)S(1)} %get-tuple-element.26), channel_id=1, source_target_pairs={{0,1},{1,0},{2,3},{3,2},{4,5},{5,4},{6,7},{7,6},{8,9},{9,8},{10,11... | collective-permute-start | bytes 589832 | tf_op jit(solution)/shard_map/ppermute | solution.py:423
  19.1 12.8 %collective-permute-start.5 = (bf16[768,128]{1,0:T(8,128)(2,1)S(1)}, bf16[768,128]{1,0:T(8,128)(2,1)S(1)}, u32[]{:S(2)}, u32[]{:S(2)}) collective-permute-start(bf16[768,128]{1,0:T(8,128)(2,1)S(1)} %get-tuple-element.40), channel_id=1, source_target_pairs={{0,2},{1,3},{2,0},{3,1},{4,6},{5,7},{6,4},{7,5},{8,10},{9,11},{10,... | collective-permute-start | bytes 589832 | tf_op jit(solution)/shard_map/ppermute | solution.py:426
  23.2 11.0 %collective-permute-start.1 = (bf16[768,128]{1,0:T(8,128)(2,1)S(1)}, bf16[768,128]{1,0:T(8,128)(2,1)S(1)}, u32[]{:S(2)}, u32[]{:S(2)}) collective-permute-start(bf16[768,128]{1,0:T(8,128)(2,1)S(1)} %get-tuple-element.23), channel_id=1, source_target_pairs={{0,1},{1,0},{2,3},{3,2},{4,5},{5,4},{6,7},{7,6},{8,9},{9,8},{10,11... | collective-permute-start | bytes 589832 | tf_op jit(solution)/shard_map/ppermute | solution.py:423
  28.0 11.5 %collective-permute-start.3 = (bf16[768,128]{1,0:T(8,128)(2,1)S(1)}, bf16[768,128]{1,0:T(8,128)(2,1)S(1)}, u32[]{:S(2)}, u32[]{:S(2)}) collective-permute-start(bf16[768,128]{1,0:T(8,128)(2,1)S(1)} %get-tuple-element.41), channel_id=1, source_target_pairs={{0,2},{1,3},{2,0},{3,1},{4,6},{5,7},{6,4},{7,5},{8,10},{9,11},{10,... | collective-permute-start | bytes 589832 | tf_op jit(solution)/shard_map/ppermute | solution.py:426
  32.0 7.5 %collective-permute-start.6 = (bf16[768,128]{1,0:T(8,128)(2,1)S(1)}, bf16[768,128]{1,0:T(8,128)(2,1)S(1)}, u32[]{:S(2)}, u32[]{:S(2)}) collective-permute-start(bf16[768,128]{1,0:T(8,128)(2,1)S(1)} %add_convert_fusion), channel_id=1, source_target_pairs={{8,0},{12,4},{0,8},{4,12},{9,1},{13,5},{1,9},{5,13},{10,2},{14,6},... | collective-permute-start | bytes 589832 | tf_op jit(solution)/shard_map/ppermute | solution.py:417
  41.9 2.0 %collective-permute-start.11 = (f32[2,72,256]{2,1,0:T(8,128)S(1)}, f32[2,72,256]{2,1,0:T(8,128)S(1)}, u32[]{:S(2)}, u32[]{:S(2)}) collective-permute-start(f32[2,72,256]{2,1,0:T(8,128)S(1)} %slice_bitcast_fusion), channel_id=1, source_target_pairs={{0,4},{4,0},{8,12},{12,8},{1,5},{5,1},{9,13},{13,9},{2,6},{6,2},{1... | collective-permute-start | bytes 442376 | tf_op jit(solution)/shard_map/ppermute | solution.py:413
  42.0 12.5 %collective-permute-start.8 = (bf16[128,768]{1,0:T(8,128)(2,1)S(1)}, bf16[128,768]{1,0:T(8,128)(2,1)S(1)}, u32[]{:S(2)}, u32[]{:S(2)}) collective-permute-start(bf16[128,768]{1,0:T(8,128)(2,1)S(1)} %get-tuple-element.29.refs_0_), channel_id=1, source_target_pairs={{0,2},{1,3},{2,0},{3,1},{4,6},{5,7},{6,4},{7,5},{8,10},{9,11},{10,... | collective-permute-start | bytes 589832 | tf_op jit(solution)/shard_map/ppermute | solution.py:426
  42.1 12.5 %collective-permute-start.9 = (bf16[128,768]{1,0:T(8,128)(2,1)S(1)}, bf16[128,768]{1,0:T(8,128)(2,1)S(1)}, u32[]{:S(2)}, u32[]{:S(2)}) collective-permute-start(bf16[128,768]{1,0:T(8,128)(2,1)S(1)} %get-tuple-element.30), channel_id=1, source_target_pairs={{8,0},{12,4},{0,8},{4,12},{9,1},{13,5},{1,9},{5,13},{10,2},{14,6},... | collective-permute-start | bytes 589832 | tf_op jit(solution)/shard_map/ppermute | solution.py:417
  44.0 11.6 %collective-permute-start.12 = (f32[72,256]{1,0:T(8,128)S(1)}, f32[72,256]{1,0:T(8,128)S(1)}, u32[]{:S(2)}, u32[]{:S(2)}) collective-permute-start(f32[72,256]{1,0:T(8,128)S(1)} %slice_bitcast_fusion.4), channel_id=1, source_target_pairs={{8,0},{12,4},{0,8},{4,12},{9,1},{13,5},{1,9},{5,13},{10,2},{14,6},... | collective-permute-start | bytes 221192 | tf_op jit(solution)/shard_map/ppermute | solution.py:417
  45.2 33.6 %collective-permute-start.7 = (bf16[128,768]{1,0:T(8,128)(2,1)S(1)}, bf16[128,768]{1,0:T(8,128)(2,1)S(1)}, u32[]{:S(2)}, u32[]{:S(2)}) collective-permute-start(bf16[128,768]{1,0:T(8,128)(2,1)S(1)} %get-tuple-element.29.refs_0_), channel_id=1, source_target_pairs={{0,1},{1,0},{2,3},{3,2},{4,5},{5,4},{6,7},{7,6},{8,9},{9,8},{10,11... | collective-permute-start | bytes 589832 | tf_op jit(solution)/shard_map/ppermute | solution.py:423
  54.5 24.3 %collective-permute-start.10 = (bf16[128,768]{1,0:T(8,128)(2,1)S(1)}, bf16[128,768]{1,0:T(8,128)(2,1)S(1)}, u32[]{:S(2)}, u32[]{:S(2)}) collective-permute-start(bf16[128,768]{1,0:T(8,128)(2,1)S(1)} %collective-permute-done.8.refs_2_), channel_id=1, source_target_pairs={{0,1},{1,0},{2,3},{3,2},{4,5},{5,4},{6,7},{7,6},{8,9},{9,8},{10,11... | collective-permute-start | bytes 589832 | tf_op jit(solution)/shard_map/ppermute | solution.py:423
  76.9 7.7 %collective-permute-start.14 = (f32[72,256]{1,0:T(8,128)S(1)}, f32[72,256]{1,0:T(8,128)S(1)}, u32[]{:S(2)}, u32[]{:S(2)}) collective-permute-start(f32[72,256]{1,0:T(8,128)S(1)} %weight_sums.1.refs_0_), channel_id=1, source_target_pairs={{8,0},{12,4},{0,8},{4,12},{9,1},{13,5},{1,9},{5,13},{10,2},{14,6},... | collective-permute-start | bytes 221192 | tf_op jit(solution)/shard_map/ppermute | solution.py:417
  84.5 2.0 %collective-permute-start.13 = (bf16[64,3072]{1,0:T(8,128)(2,1)S(1)}, bf16[64,3072]{1,0:T(8,128)(2,1)S(1)}, u32[]{:S(2)}, u32[]{:S(2)}) collective-permute-start(bf16[64,3072]{1,0:T(8,128)(2,1)S(1)} %get-tuple-element.36), channel_id=1, source_target_pairs={{0,4},{4,0},{8,12},{12,8},{1,5},{5,1},{9,13},{13,9},{2,6},{6,2},{1... | collective-permute-start | bytes 1179656 | tf_op jit(solution)/shard_map/ppermute | solution.py:413
  84.6 1.9 %collective-permute-start.15 = (f32[2,72,256]{2,1,0:T(8,128)S(1)}, f32[2,72,256]{2,1,0:T(8,128)S(1)}, u32[]{:S(2)}, u32[]{:S(2)}) collective-permute-start(f32[2,72,256]{2,1,0:T(8,128)S(1)} %pad_maximum_fusion), channel_id=1, source_target_pairs={{0,4},{4,0},{8,12},{12,8},{1,5},{5,1},{9,13},{13,9},{2,6},{6,2},{1... | collective-permute-start | bytes 442376 | tf_op jit(solution)/shard_map/ppermute | solution.py:413
